TPU v7x, 32 devices: a whole 2x2x4 slice. The times are simulated.
32 devices in a mesh: groups: 2 (over x), tile: 16 (over z, y, core).
Axes of the slice: x: 2, y: 2, z: 4, core: 2. Of those that a mesh axis runs over, the one named last changes fastest.
Arguments:
- observations: bfloat16 [2048, 64, 256], P(('groups', 'tile')), parts along dimension 0, may hold values from -6 to 6
- pixel_geometry: float32 [2048, 8, 256], P(('groups', 'tile')), parts along dimension 0, as said below
- block_counts: int32 [2048], P(('groups', 'tile')), parts along dimension 0, may hold values from 1 to 256, as said below
- block_tiles: int32 [2048], P(('groups', 'tile')), parts along dimension 0, may hold values from 0 to 511, as said below
- cutoff_lists: int32 [512, 3], replicated, may hold values from 0 to 127, as said below
- patch_geometry: float32 [4, 32768], replicated, as said below
- stress: bfloat16 [64, 65536], P(None, ('groups', 'tile')), parts along dimension 1, may hold values from -3 to 3
- screens: bfloat16 [1024, 64, 256], P(('groups', 'tile')), parts along dimension 0, may hold values from -3 to 3
Outputs:
- stress_gradient: float32 [64, 65536], P(None, ('groups', 'tile')), parts along dimension 1
- screen_gradient: float32 [1024, 64, 256], P(('groups', 'tile')), parts along dimension 0
There are 2 independent parts, one for each index of `groups`. A program takes and returns all parts, laid end to end along the dimension named above; an argument that names none is the same for every part. Nothing has to cross between parts.
Inputs may be any that keep to these rules, and one draw needn't show every extreme that they name: `block_tiles`: the owner of tile t is index t // 32 of tile. Among the 64 blocks of one device at most 8 belong to the tiles of one owner, and some owner gets exactly 8 from every device. The live pixels of a block are its first block_counts pixels. `cutoff_lists`: the 3 entries of a row are different patch blocks. `patch_geometry`: depths are 1 or more; compliances are positive. `pixel_geometry`: u and v lie within 0 to 15; weights are positive.
All inputs are finite; a program needn't handle non-finite values.
Results may differ from a plain program's by a relative error of at most 0.0037.
Values may be sent and summed in bfloat16 or wider, within the bound.
No kernel may reach another device: no remote copies, remote signals or barrier semaphores. Data moves between devices by JAX's collectives and lax.ppermute only.
A program may use at most 128 MiB of HBM per device.

v0:
```python
import functools

import jax
import jax.numpy as jnp
from jax import lax
from jax.experimental import pallas as pl
from jax.experimental.pallas import tpu as pltpu
from jax.sharding import PartitionSpec as P

PBLK = 256
NEAR = 3
SG = 16
CHUNK = 128
LAYER = 4
PAIR = 2
NARROW = 3
ROUNDS = (6, 6, 4)
MIB = 1 << 20
TERMS = 32
CROSS = ((0, 0), (0, 1), (1, 0), (0, 2), (1, 1), (2, 0))


def round_sizes(slots):
    return [slots * r // sum(ROUNDS) for r in ROUNDS]


def pack_kernel(local_tiles, layers, slots, here, tiles, counts, obs_in, pix_in, *rest):
    sizes = round_sizes(slots)
    total = len(sizes)
    obs_out, pix_out = rest[: total * layers], rest[total * layers : (total + 1) * layers]
    obs, pix, obs_all, pix_all, fill, sems = rest[(total + 1) * layers :]
    loads = [
        pltpu.make_async_copy(obs_in, obs, sems.at[0]),
        pltpu.make_async_copy(pix_in, pix, sems.at[1]),
    ]
    for copy in loads:
        copy.start()
    my_layer, my_seat = lax.div(here[0], LAYER), lax.rem(here[0], LAYER)
    chunks = pix.shape[2] // CHUNK
    stride = slots + 1
    for x in range(layers):
        fill[x] = 0
    lane = lax.broadcasted_iota(jnp.int32, (8, CHUNK), 1)
    row = lax.broadcasted_iota(jnp.int32, (8, CHUNK), 0)
    for copy in loads:
        copy.wait()

    def put(b, infos):
        tile = tiles[b]
        count = counts[b]
        owner = lax.div(tile, local_tiles)
        x = lax.div(owner, LAYER) ^ my_layer
        seat = lax.rem(owner, LAYER) ^ my_seat
        spot = lax.rem(seat, PAIR) * PAIR + lax.div(seat, PAIR)
        screen = spot * local_tiles + lax.rem(tile, local_tiles)
        slot = fill[x]
        fill[x] = slot + lax.div(count + CHUNK - 1, CHUNK)
        for c in range(chunks):
            at = slot + c
            live = jnp.clip(count - c * CHUNK, 0, CHUNK)
            obs_all[x * stride + at] = obs[b, :, c * CHUNK : (c + 1) * CHUNK]
            pix_all[x * stride + at] = pix[b, :, c * CHUNK : (c + 1) * CHUNK]
            entry = jnp.where(row == 0, live, jnp.where(row == 1, tile, screen))
            here_only = (lane == at) & (row < 3)
            infos = tuple(
                jnp.where(here_only & (x == i), entry, info) for i, info in enumerate(infos)
            )
        return infos

    infos = lax.fori_loop(
        0, obs.shape[0], put, tuple(jnp.zeros((8, CHUNK), jnp.int32) for _ in range(layers))
    )
    copies = []
    for x in range(layers):
        at = x * stride
        pix_all[at + slots] = infos[x].astype(jnp.float32)
        copies.append((pix_all.at[pl.ds(at, stride)], pix_out[x]))
        for i, size in enumerate(sizes):
            copies.append((obs_all.at[pl.ds(at, size)], obs_out[i * layers + x]))
            at += size
    copies = [pltpu.make_async_copy(a, b, sems.at[i]) for i, (a, b) in enumerate(copies)]
    for copy in copies:
        copy.start()
    for copy in copies:
        copy.wait()


def pack(observations, pixel_geometry, block_counts, block_tiles, here, devices, local_tiles):
    blocks, epochs, width = observations.shape
    layers = devices // LAYER
    slots = LAYER * (2 * blocks // devices) * (width // CHUNK)
    sizes = round_sizes(slots)
    smem = pl.BlockSpec(memory_space=pltpu.SMEM)
    hbm = pl.BlockSpec(memory_space=pl.ANY)
    pix_part = jax.ShapeDtypeStruct((slots + 1, 8, CHUNK), jnp.float32)
    out = pl.pallas_call(
        functools.partial(pack_kernel, local_tiles, layers, slots),
        in_specs=[smem, smem, smem, hbm, hbm],
        out_specs=[hbm] * ((len(sizes) + 1) * layers),
        out_shape=[
            jax.ShapeDtypeStruct((size, epochs, CHUNK), observations.dtype)
            for size in sizes
            for _ in range(layers)
        ]
        + [pix_part] * layers,
        scratch_shapes=[
            pltpu.VMEM(observations.shape, observations.dtype),
            pltpu.VMEM(pixel_geometry.shape, jnp.float32),
            pltpu.VMEM((layers * (slots + 1), epochs, CHUNK), observations.dtype),
            pltpu.VMEM((layers * (slots + 1), 8, CHUNK), jnp.float32),
            pltpu.SMEM((layers,), jnp.int32),
            pltpu.SemaphoreType.DMA(((len(sizes) + 1) * layers,)),
        ],
        compiler_params=pltpu.CompilerParams(vmem_limit_bytes=10 * MIB),
        name="pack",
    )(here, block_tiles, block_counts, observations, pixel_geometry)
    rounds = len(sizes)
    return [out[i * layers : (i + 1) * layers] for i in range(rounds)], out[rounds * layers :]


def split(values):
    parts = []
    for _ in range(3):
        part = lax.reduce_precision(values, 8, 7)
        parts.append(part)
        values = values - part
    return parts


def kernel_split(values):
    parts = []
    for _ in range(3):
        part = values.astype(jnp.bfloat16).astype(jnp.float32)
        parts.append(part)
        values = values - part
    return parts


def fit_kernel(first, final, layers, slots, groups, *refs):
    info, cutoffs, places, spots, origin = refs[:5]
    rest = refs[5:]
    obs_in, pix_in = [], []
    for _ in groups:
        obs_in.append(rest[:layers])
        pix_in.append(rest[layers : 2 * layers])
        rest = rest[2 * layers :]
    patches, forms = rest[:2]
    rest = rest[1:]
    if first:
        screen_parts, stress_parts = rest[1 : 1 + LAYER], rest[1 + LAYER : 1 + 2 * LAYER]
        rest = rest[1 + 2 * LAYER :]
        grad, screen_grad, screens, stress = rest[:4]
        rest = rest[4:]
    else:
        screens, stress = rest[1:3]
        grad, screen_grad = rest[5:7]
        rest = rest[7:]
    outs = rest[:3] if final else ()
    rest = rest[len(outs) :]
    obs, pix, green_a, hats_a, green_b, hats_b, wide, sights, items, sems = rest
    epochs = obs.shape[1]
    base = groups[0][0]
    span = sum(size for _, _, size in groups)
    local_tiles = screens.shape[0] // LAYER

    loads = []
    for x in range(layers):
        at = x * span
        for g, (_, low, size) in enumerate(groups):
            loads.append((obs_in[g][x], obs.at[pl.ds(at, size)]))
            loads.append((pix_in[g][x].at[pl.ds(low, size)], pix.at[pl.ds(at, size)]))
            at += size
    if first:
        for parts, whole in ((screen_parts, screens), (stress_parts, stress)):
            size = whole.shape[0] // LAYER
            for i, part in enumerate(parts):
                loads.append((part, whole.at[pl.ds(i * size, size)]))
    loads = [pltpu.make_async_copy(a, b, sems.at[i]) for i, (a, b) in enumerate(loads)]
    for copy in loads:
        copy.start()
    if first:
        grad[...] = jnp.zeros_like(grad)
        screen_grad[...] = jnp.zeros_like(screen_grad)

    def info_of(slot, kind):
        x = lax.div(slot, span)
        return info[(x * 3 + kind) * slots + base + lax.rem(slot, span)]

    def list_slot(slot, total):
        items[total] = slot
        return total + jnp.where(info_of(slot, 0) > 0, 1, 0)

    total = lax.fori_loop(0, layers * span, list_slot, 0)
    for copy in loads:
        copy.wait()

    def item_of(i):
        slot = items[jnp.minimum(i, total - 1)]
        tile = info_of(slot, 1)
        return slot, [cutoffs[tile * NEAR + k] for k in range(NEAR)]

    def spread(rows, sights):
        columns = rows.T
        for i in range(2):
            wide[i] = jnp.broadcast_to(columns[:, i : i + 1], (CHUNK, CHUNK))
        le, ln = rows[4:5], rows[5:6]
        along = le * (rows[0:1] - origin[0]) + ln * (rows[1:2] - origin[1])
        row = lax.broadcasted_iota(jnp.int32, (8, CHUNK), 0)
        factors = jnp.where(
            row == 0, along, jnp.where(row == 1, le, jnp.where(row == 2, ln, rows[6:7]))
        )
        parts = kernel_split(factors)
        low = row < 4
        tiles = []
        for first_part, second_part in zip(CROSS[::2], CROSS[1::2]):
            upper = jnp.concatenate([parts[second_part[0]][:4]] * 2, axis=0)
            tiles.append(jnp.where(low, parts[first_part[0]], upper))
        tiles.append(jnp.zeros((8, CHUNK), jnp.float32))
        sights[...] = jnp.concatenate(tiles, axis=0).T.astype(jnp.bfloat16)

    def make_strips(near, k, lows, sights, green):
        patch = [
            jnp.broadcast_to(patches[near[k], r : r + 1], (8, PBLK)) for r in range(3)
        ]
        begin, end = lows[0], lows[-1] + 16
        alongs = jnp.dot(sights[begin:end], forms[near[k]], preferred_element_type=jnp.float32)
        for low in lows:
            along = alongs[low - begin : low - begin + 16]
            inverses = []
            for at in (low, low + 8):
                east, north = (
                    jnp.concatenate([wide[i, at : at + 8]] * (PBLK // CHUNK), axis=1)
                    for i in range(2)
                )
                dx = east - patch[0]
                dy = north - patch[1]
                inverses.append(lax.rsqrt(dx * dx + dy * dy + patch[2]))
            inverse = jnp.concatenate(inverses, axis=0)
            green[low : low + 16, k * PBLK : (k + 1) * PBLK] = (
                along * inverse * inverse * inverse
            ).astype(jnp.bfloat16)

    def make_hats(rows, hats):
        node = lax.broadcasted_iota(jnp.int32, (SG, CHUNK), 0).astype(jnp.float32)
        across = jnp.maximum(0.0, 1.0 - jnp.abs(rows[2:3] - node))
        upward = jnp.maximum(0.0, 1.0 - jnp.abs(rows[3:4] - node))
        for a in range(SG):
            hats[a * SG : (a + 1) * SG] = (across[a : a + 1] * upward).astype(jnp.bfloat16)

    def make_all(i, green, hats):
        slot, near = item_of(i)
        rows = pix[slot]
        make_hats(rows, hats)
        spread(rows, sights)
        for k in range(NEAR):
            for low in (0, CHUNK // 2):
                make_strips(near, k, range(low, low + CHUNK // 2, 16), sights, green)

    def turn(i, green, hats, green_next, hats_next):
        slot, near = item_of(i)
        slot_next, near_next = item_of(i + 1)
        rows = pix[slot_next]
        screen = info_of(slot, 2)

        def fill(k, low, high):
            make_strips(near_next, k, range(low, high, 16), sights, green_next)

        model = jnp.dot(screens[screen], hats[...], preferred_element_type=jnp.float32)
        for k in range(NEAR):
            model += lax.dot_general(
                stress[pl.ds(pl.multiple_of(spots[near[k]], 16), epochs), :],
                green[:, k * PBLK : (k + 1) * PBLK],
                (((1,), (1,)), ((), ())),
                preferred_element_type=jnp.float32,
            )
        make_hats(rows, hats_next)
        spread(rows, sights)
        fill(0, 0, CHUNK // 2)
        fill(0, CHUNK // 2, CHUNK)
        live = jnp.where(i < total, info_of(slot, 0), 0)
        lane = lax.broadcasted_iota(jnp.int32, (1, CHUNK), 1)
        scale = jnp.where(lane < live, pix[slot, 7:8, :], 0.0)
        weighted = ((model - obs[slot].astype(jnp.float32)) * scale).astype(jnp.bfloat16)

        def add(k):
            grad[places[near[k]]] += jnp.dot(
                weighted,
                green[:, k * PBLK : (k + 1) * PBLK],
                preferred_element_type=jnp.float32,
            )

        add(0)
        fill(1, 0, CHUNK // 2)
        add(1)
        fill(1, CHUNK // 2, CHUNK)
        add(2)
        fill(2, 0, CHUNK // 2)
        screen_grad[screen] += lax.dot_general(
            weighted, hats[...], (((1,), (1,)), ((), ())), preferred_element_type=jnp.float32
        )
        fill(2, CHUNK // 2, CHUNK)

    @pl.when(total > 0)
    def _():
        make_all(0, green_a, hats_a)

        def step(j, _):
            turn(2 * j, green_a, hats_a, green_b, hats_b)
            turn(2 * j + 1, green_b, hats_b, green_a, hats_a)
            return 0

        lax.fori_loop(0, lax.div(total + 1, 2), step, 0)

    if final:
        half = grad.shape[0] // 2
        outs[0][...] = grad[half:].astype(outs[0].dtype)
        for i, out in enumerate(outs[1:]):
            low = (PAIR + i) * local_tiles
            out[...] = screen_grad[low : low + local_tiles].astype(out.dtype)


def fit(tables, groups, patches, forms, screens, stress, state, first, final):
    layers = len(groups[0][1])
    slots = tables[0].shape[0] // (3 * layers)
    smem = pl.BlockSpec(memory_space=pltpu.SMEM)
    vmem = pl.BlockSpec(memory_space=pltpu.VMEM)
    hbm = pl.BlockSpec(memory_space=pl.ANY)
    spans = tuple((base, low, obs[0].shape[0]) for base, obs, _, low in groups)
    arrays = [a for _, obs, pix, _ in groups for a in (*obs, *pix)]
    span = sum(size for _, _, size in spans)
    blocks, epochs = state[0].shape[0], state[0].shape[1]
    out_shape = [jax.ShapeDtypeStruct(a.shape, a.dtype) for a in state]
    if first:
        state = ()
        for parts in (screens, stress):
            shape = (LAYER * parts[0].shape[0],) + parts[0].shape[1:]
            out_shape.append(jax.ShapeDtypeStruct(shape, parts[0].dtype))
    else:
        screens, stress = [screens], [stress]
    if final:
        out_shape.append(jax.ShapeDtypeStruct((blocks // 2, epochs, PBLK), jnp.bfloat16))
        shape = (state[1].shape[0] // LAYER,) + state[1].shape[1:]
        out_shape += [jax.ShapeDtypeStruct(shape, jnp.bfloat16)] * 2
    before = len(tables) + len(arrays) + 2 + len(screens) + len(stress)
    return pl.pallas_call(
        functools.partial(fit_kernel, first, final, layers, slots, spans),
        in_specs=[smem] * len(tables)
        + [hbm] * len(arrays)
        + [vmem] * 2
        + [hbm if first else vmem] * (len(screens) + len(stress))
        + [vmem] * len(state),
        out_specs=[vmem] * len(out_shape),
        out_shape=out_shape,
        scratch_shapes=[
            pltpu.VMEM((layers * span, epochs, CHUNK), arrays[0].dtype),
            pltpu.VMEM((layers * span, 8, CHUNK), jnp.float32),
        ]
        + [
            pltpu.VMEM((CHUNK, NEAR * PBLK), jnp.bfloat16),
            pltpu.VMEM((SG * SG, CHUNK), jnp.bfloat16),
        ]
        * 2
        + [
            pltpu.VMEM((2, CHUNK, CHUNK), jnp.float32),
            pltpu.VMEM((CHUNK, TERMS), jnp.bfloat16),
            pltpu.SMEM((layers * span + 1,), jnp.int32),
            pltpu.SemaphoreType.DMA((2 * layers * len(groups) + 2 * LAYER,)),
        ],
        input_output_aliases={} if first else {before: 0, before + 1: 1},
        compiler_params=pltpu.CompilerParams(vmem_limit_bytes=8 * MIB),
        cost_estimate=pl.CostEstimate(
            flops=layers * span * 4 * epochs * CHUNK * (NEAR + 1) * PBLK,
            bytes_accessed=20 * MIB,
            transcendentals=layers * span * CHUNK * NEAR * PBLK,
        ),
        name="fit",
    )(*tables, *arrays, patches, forms, *screens, *stress, *state)


def partner(values, devices, distance):
    return lax.ppermute(values, "tile", [(i, i ^ distance) for i in range(devices)])


def orders(devices):
    stages = devices.bit_length() - 1
    high = list(range(stages - 1, 1, -1))
    return [1] + high, high + [1]


def block_places(devices, here, blocks, local, epochs):
    block = jnp.arange(blocks)
    other = (block // local) ^ here
    seat = block % local
    half = local // 2
    turned = []
    for order in orders(devices):
        spot = 0
        for bit in order:
            spot = spot * 2 + ((other >> bit) & 1)
        turned.append(spot)
    chips = devices // 2
    upper = seat // half
    spot = jnp.where(upper == 0, turned[0], turned[1])
    place = (((other & 1) * 2 + upper) * chips + spot) * half + seat % half
    stages = devices.bit_length() - 1
    held = sum(((other >> (stages - 1 - s)) & 1) << s for s in range(stages))
    return place.astype(jnp.int32), ((held * local + seat) * epochs).astype(jnp.int32)


def halve(kept, given, there, devices):
    total = kept + partner(given, devices, 1).astype(jnp.float32)
    middle = total.shape[0] // 2
    parts = [total[:middle], total[middle:]]
    both = orders(devices)
    stages = len(both[0])
    back = None
    for stage in range(stages):
        got = []
        for side in range(2):
            given = parts[side][parts[side].shape[0] // 2 :]
            if stages - stage <= NARROW:
                given = given.astype(jnp.bfloat16)
            got.append(partner(given, devices, 1 << both[side][stage]))
        for side in range(2):
            if side:
                parts[0], got[1] = lax.optimization_barrier((parts[0], got[1]))
            size = parts[side].shape[0] // 2
            parts[side] = parts[side][:size] + got[side].astype(jnp.float32)
            if back is None:
                parts[0], there = lax.optimization_barrier((parts[0], there))
                back = partner(there, devices, PAIR)
    return jnp.concatenate(parts, axis=0), back


def on_device(
    observations,
    pixel_geometry,
    block_counts,
    block_tiles,
    cutoff_lists,
    patch_geometry,
    stress,
    screens,
):
    devices = lax.axis_size("tile")
    here = lax.axis_index("tile")
    blocks, epochs, width = observations.shape
    local_tiles = screens.shape[0]
    layers = devices // LAYER
    local = stress.shape[1] // PBLK

    slots = LAYER * (2 * blocks // devices) * (width // CHUNK)
    sizes = round_sizes(slots)

    held = jnp.swapaxes(stress.reshape(epochs, local, PBLK), 0, 1).reshape(-1, PBLK)
    other = partner(held, devices, devices // 2)
    across_screens = partner(screens, devices, PAIR)
    obs, pix = pack(
        observations,
        pixel_geometry,
        block_counts,
        block_tiles,
        jnp.reshape(here, (1,)).astype(jnp.int32),
        devices,
        local_tiles,
    )

    def exchange(parts):
        return [parts[0]] + [partner(parts[x], devices, x * LAYER) for x in range(1, layers)]

    other, pix = lax.optimization_barrier((other, pix))
    pix = exchange(pix)
    distance = devices // 2
    while distance >= LAYER:
        if distance < devices // 2:
            other = partner(held, devices, distance)
        held = jnp.concatenate([held, other], axis=0)
        distance //= 2
    held, pix, across_screens = lax.optimization_barrier((held, pix, across_screens))
    got = [exchange(o) for o in obs]
    across = partner(held, devices, PAIR)
    across, got[0][1] = lax.optimization_barrier((across, got[0][1]))
    all_stress = [held, across, partner(held, devices, 1), partner(across, devices, 1)]
    all_screens = [
        screens,
        across_screens,
        partner(screens, devices, 1),
        partner(across_screens, devices, 1),
    ]

    patch_blocks = devices * local
    east, north, depth, compliance = patch_geometry
    origin = patch_geometry[:2, 0]
    strength = compliance * depth * depth
    faces = split(
        jnp.stack(
            [
                strength,
                -strength * (east - origin[0]),
                -strength * (north - origin[1]),
                strength * depth,
            ]
        )
    )
    forms = jnp.concatenate(
        [faces[second] for _, second in CROSS] + [jnp.zeros((8,) + east.shape, jnp.float32)]
    ).astype(jnp.bfloat16)
    forms = jnp.swapaxes(forms.reshape(TERMS, patch_blocks, PBLK), 0, 1)
    patches = jnp.stack([east, north, depth * depth])
    patches = jnp.swapaxes(patches.reshape(3, patch_blocks, PBLK), 0, 1)
    places, spots = block_places(devices, here, patch_blocks, local, epochs)
    info = jnp.stack([p[slots, :3, :slots] for p in pix]).astype(jnp.int32).reshape(-1)
    tables = (info, cutoff_lists.reshape(-1), places, spots, origin)

    state = (
        jax.ShapeDtypeStruct((patch_blocks, epochs, PBLK), jnp.float32),
        jax.ShapeDtypeStruct((LAYER * local_tiles,) + screens.shape[1:], jnp.float32),
    )
    base = 0
    for i, size in enumerate(sizes):
        first, final = i == 0, i == len(sizes) - 1
        groups = [(base, got[i], pix, base)]
        state = fit(
            tables,
            groups,
            patches,
            forms,
            all_screens,
            all_stress,
            state[:2],
            first,
            final,
        )
        if first:
            all_screens, all_stress = state[2:]
        base += size
    grad, screen_grad, given, next_door, diagonal = state
    own, far = screen_grad[:local_tiles], screen_grad[local_tiles : PAIR * local_tiles]
    there = (far + partner(diagonal, devices, 1).astype(jnp.float32)).astype(jnp.bfloat16)
    grad, back = halve(grad[: grad.shape[0] // 2], given, there, devices)
    screen_gradient = (
        own + partner(next_door, devices, 1).astype(jnp.float32) + back.astype(jnp.float32)
    )
    return (jnp.swapaxes(grad, 0, 1).reshape(epochs, local * PBLK), screen_gradient)


def solution(mesh):
    return jax.shard_map(
        on_device,
        mesh=mesh,
        in_specs=(
            P(("groups", "tile"), None, None),
            P(("groups", "tile"), None, None),
            P(("groups", "tile")),
            P(("groups", "tile")),
            P(),
            P(),
            P(None, ("groups", "tile")),
            P(("groups", "tile"), None, None),
        ),
        out_specs=(P(None, ("groups", "tile")), P(("groups", "tile"), None, None)),
        check_vma=False,
    )
```

profile of v0, /device:TPU:26, one launch (start us, length us, event | category | flops | bytes accessed | tf_op | source)
XLA Modules:
  0.0 244.8 jit_solution(10460326554944417280)
XLA Ops:
  7.5 5.0 %pack.1 = (bf16[24,64,128]{2,1,0:T(8,128)(2,1)S(1)}, bf16[24,64,128]{2,1,0:T(8,128)(2,1)S(1)}, bf16[24,64,128]{2,1,0:T(8,128)(2,1)S(1)}, bf16[24,64,128]{2,1,0:T...) custom-call(s32[1]{0:T(128)} %bitcast.3.here, ...), custom_call_target="tpu_custom_call" | custom-call | tf_op jit(solution)/shard_map/pack/pallas_call | solution.py:96
  21.3 15.5 %collective-permute-done.1 = bf16[1024,256]{1,0:T(8,128)(2,1)S(1)} collective-permute-done((bf16[1024,256]{1,0:T(8,128)(2,1)S(1)}, bf16[1024,256]{1,0:T(8,128)(2,1)S(1)}, u32[]{:S(2)}, u32[]{:S(2)}) %collective-permute-start.1) | collective-permute-done | bytes 524320 | tf_op jit(solution)/shard_map/ppermute | solution.py:381
  37.8 4.7 %collective-permute-done.2.refs_10_ = f32[65,8,128]{2,1,0:T(8,128)S(1)} collective-permute-done((f32[65,8,128]{2,1,0:T(8,128)S(1)}, f32[65,8,128]{2,1,0:T(8,128)S(1)}, u32[]{:S(2)}, u32[]{:S(2)}) %collective-permute-start.2) | collective-permute-done | bytes 266272 | tf_op jit(solution)/shard_map/ppermute | solution.py:381
  43.3 6.6 %collective-permute-done.4.refs_12_ = f32[65,8,128]{2,1,0:T(8,128)} collective-permute-done((f32[65,8,128]{2,1,0:T(8,128)S(1)}, f32[65,8,128]{2,1,0:T(8,128)}, u32[]{:S(2)}, u32[]{:S(2)}) %collective-permute-start.4) | collective-permute-done | bytes 266272 | tf_op jit(solution)/shard_map/ppermute | solution.py:381
  50.0 3.3 %collective-permute-start.9 = (bf16[2048,256]{1,0:T(8,128)(2,1)}, bf16[2048,256]{1,0:T(8,128)(2,1)}, u32[]{:S(2)}, u32[]{:S(2)}) collective-permute-start(bf16[2048,256]{1,0:T(8,128)(2,1)} %pad_maximum_fusion.refs_19_), channel_id=1, source_target_pairs={{0,2},{1,3},{2,0},{3,1},{4,6},{5,7},{6,4},{7,5},{8,10},{9,11},{10,... | collective-permute-start | bytes 3145736 | tf_op jit(solution)/shard_map/ppermute | solution.py:381
  54.2 10.3 %collective-permute-done.10.refs_6_ = bf16[24,64,128]{2,1,0:T(8,128)(2,1)S(1)} collective-permute-done((bf16[24,64,128]{2,1,0:T(8,128)(2,1)S(1)}, bf16[24,64,128]{2,1,0:T(8,128)(2,1)S(1)}, u32[]{:S(2)}, u32[]{:S(2)}) %collective-permute-start.10) | collective-permute-done | bytes 393248 | tf_op jit(solution)/shard_map/ppermute | solution.py:381
  65.3 6.6 %collective-permute-done.9.refs_20_ = bf16[2048,256]{1,0:T(8,128)(2,1)} collective-permute-done((bf16[2048,256]{1,0:T(8,128)(2,1)}, bf16[2048,256]{1,0:T(8,128)(2,1)}, u32[]{:S(2)}, u32[]{:S(2)}) %collective-permute-start.9) | collective-permute-done | bytes 1048608 | tf_op jit(solution)/shard_map/ppermute | solution.py:381
  74.3 2.5 %collective-permute-start.12 = (bf16[24,64,128]{2,1,0:T(8,128)(2,1)}, bf16[24,64,128]{2,1,0:T(8,128)(2,1)}, u32[]{:S(2)}, u32[]{:S(2)}) collective-permute-start(bf16[24,64,128]{2,1,0:T(8,128)(2,1)} %get-tuple-element.72), channel_id=1, source_target_pairs={{0,12},{1,13},{2,14},{3,15},{4,8},{5,9},{6,10},{7,11},{8,4},{9,5},... | collective-permute-start | bytes 1179656 | tf_op jit(solution)/shard_map/ppermute | solution.py:381
  80.2 4.7 %concatenate.21 = bf16[32,128,256]{2,0,1:T(8,128)(2,1)S(1)} concatenate(bf16[4,128,256]{2,0,1:T(4,128)(2,1)S(1)} %get-tuple-element.108, bf16[4,128,256]{2,0,1:T(4,128)(2,1)S(1)} %get-tuple-element.107, bf16[4,128,256]{2,0,1:T(4,128)(2,1)S(1)} %get-tuple-element.108, bf16[4,128,256]{2,0,1:T(4,128)(2,1)} %get-tuple-element.106, bf16[4,128,256]{2,0,1:T(4,128)(2,1)S(1)} %get-tuple-element.107, ...), dimensions={0} | concatenate | bytes 4194304 | tf_op jit(solution)/shard_map/concatenate | solution.py:505
  88.1 3.4 %collective-permute-start.17 = (bf16[24,64,128]{2,1,0:T(8,128)(2,1)}, bf16[24,64,128]{2,1,0:T(8,128)(2,1)}, u32[]{:S(2)}, u32[]{:S(2)}) collective-permute-start(bf16[24,64,128]{2,1,0:T(8,128)(2,1)} %copy-done.15), channel_id=1, source_target_pairs={{0,4},{1,5},{2,6},{3,7},{4,0},{5,1},{6,2},{7,3},{8,12},{9,13},{10,... | collective-permute-start | bytes 1179656 | tf_op jit(solution)/shard_map/ppermute | solution.py:381
  100.8 32.1 %fit.3 = (f32[128,64,256]{2,1,0:T(8,128)S(1)}, f32[128,64,256]{2,1,0:T(8,128)S(1)}, bf16[128,64,256]{2,1,0:T(8,128)(2,1)S(1)}, bf16[8192,256]{1,0:T(8,128)(2,1)S(1)}) custom-call(s32[768]{0:T(1024)S(1)} %convert_element_type.49.refs_0_, s32[1536]{0:T(1024)S(1)} %reshape.52.refs_1_, s32[128]{0:T(128)S(1)} %get-tuple-element.112.refs_2_, ...), custom_call_target="tpu_custom_call" | custom-call | flops 3221225472 | bytes 20971520 | tf_op jit(solution)/shard_map/fit/pallas_call | solution.py:345
  132.9 18.7 %collective-permute-start.8 = (bf16[16,64,128]{2,1,0:T(8,128)(2,1)S(1)}, bf16[16,64,128]{2,1,0:T(8,128)(2,1)S(1)}, u32[]{:S(2)}, u32[]{:S(2)}) collective-permute-start(bf16[16,64,128]{2,1,0:T(8,128)(2,1)S(1)} %copy-done.23), channel_id=1, source_target_pairs={{0,12},{1,13},{2,14},{3,15},{4,8},{5,9},{6,10},{7,11},{8,4},{9,5},... | collective-permute-start | bytes 786440 | tf_op jit(solution)/shard_map/ppermute | solution.py:381
  151.7 2.9 %fit.4 = (f32[128,64,256]{2,1,0:T(8,128)S(1)}, f32[128,64,256]{2,1,0:T(8,128)S(1)}) custom-call(s32[768]{0:T(1024)S(1)} %convert_element_type.49.refs_0_, s32[1536]{0:T(1024)S(1)} %reshape.52.refs_1_, s32[128]{0:T(128)S(1)} %get-tuple-element.112.refs_2_, s32[128]{0:T(128)S(1)} %get-tuple-element.113.refs_3_, ...), custom_call_target="tpu_custom_call", output_to_operand_aliasing={{0}: (17, {}), {1}: (18, {})} | custom-call | flops 3221225472 | bytes 20971520 | tf_op jit(solution)/shard_map/fit/pallas_call | solution.py:345
  154.6 2.2 collective-permute-done.8.refs_8_
  156.8 3.5 %fit.5 = (f32[128,64,256]{2,1,0:T(8,128)S(1)}, f32[128,64,256]{2,1,0:T(8,128)S(1)}, bf16[64,64,256]{2,1,0:T(8,128)(2,1)S(1)}, bf16[32,64,256]{2,1,0:T(8,128)(2,1)S(1)}, bf16[32,64,256]{2,1,0:T(8,128)(2,1)}) custom-call(s32[768]{0:T(1024)S(1)} %convert_element_type.49.refs_0_, ...), custom_call_target="tpu_custom_call", output_to_operand_aliasing={{0}: (17, {}), {1}: (18, {})} | custom-call | flops 2147483648 | bytes 20971520 | tf_op jit(solution)/shard_map/fit/pallas_call | solution.py:345
  161.9 5.1 %collective-permute-done.20 = bf16[64,64,256]{2,1,0:T(8,128)(2,1)S(1)} collective-permute-done((bf16[64,64,256]{2,1,0:T(8,128)(2,1)S(1)}, bf16[64,64,256]{2,1,0:T(8,128)(2,1)S(1)}, u32[]{:S(2)}, u32[]{:S(2)}) %collective-permute-start.20) | collective-permute-done | bytes 2097184 | tf_op jit(solution)/shard_map/ppermute | solution.py:381
  170.0 7.8 %collective-permute-start.23 = (bf16[16,64,256]{2,1,0:T(8,128)(2,1)S(1)}, bf16[16,64,256]{2,1,0:T(8,128)(2,1)S(1)}, u32[]{:S(2)}, u32[]{:S(2)}) collective-permute-start(bf16[16,64,256]{2,1,0:T(8,128)(2,1)S(1)} %get-tuple-element.102), channel_id=1, source_target_pairs={{0,8},{1,9},{2,10},{3,11},{4,12},{5,13},{6,14},{7,15},{8,0},{9,1},... | collective-permute-start | bytes 1572872 | tf_op jit(solution)/shard_map/ppermute | solution.py:381
  178.2 4.0 %collective-permute-done.21 = bf16[16,64,256]{2,1,0:T(8,128)(2,1)S(1)} collective-permute-done((bf16[16,64,256]{2,1,0:T(8,128)(2,1)S(1)}, bf16[16,64,256]{2,1,0:T(8,128)(2,1)S(1)}, u32[]{:S(2)}, u32[]{:S(2)}) %collective-permute-start.21) | collective-permute-done | bytes 524320 | tf_op jit(solution)/shard_map/ppermute | solution.py:381
  182.4 7.4 %collective-permute-done.23 = bf16[16,64,256]{2,1,0:T(8,128)(2,1)S(1)} collective-permute-done((bf16[16,64,256]{2,1,0:T(8,128)(2,1)S(1)}, bf16[16,64,256]{2,1,0:T(8,128)(2,1)S(1)}, u32[]{:S(2)}, u32[]{:S(2)}) %collective-permute-start.23) | collective-permute-done | bytes 524320 | tf_op jit(solution)/shard_map/ppermute | solution.py:381
  189.8 2.7 %collective-permute-start.24 = (bf16[8,64,256]{2,1,0:T(8,128)(2,1)S(1)}, bf16[8,64,256]{2,1,0:T(8,128)(2,1)S(1)}, u32[]{:S(2)}, u32[]{:S(2)}) collective-permute-start(bf16[8,64,256]{2,1,0:T(8,128)(2,1)S(1)} %slice.130), channel_id=1, source_target_pairs={{0,8},{1,9},{2,10},{3,11},{4,12},{5,13},{6,14},{7,15},{8,0},{9,1},... | collective-permute-start | bytes 786440 | tf_op jit(solution)/shard_map/ppermute | solution.py:381
  192.7 21.0 %collective-permute-start.25 = (bf16[8,64,256]{2,1,0:T(8,128)(2,1)S(1)}, bf16[8,64,256]{2,1,0:T(8,128)(2,1)S(1)}, u32[]{:S(2)}, u32[]{:S(2)}) collective-permute-start(bf16[8,64,256]{2,1,0:T(8,128)(2,1)S(1)} %slice.129), channel_id=1, source_target_pairs={{0,4},{1,5},{2,6},{3,7},{4,0},{5,1},{6,2},{7,3},{8,12},{9,13},{10,... | collective-permute-start | bytes 786440 | tf_op jit(solution)/shard_map/ppermute | solution.py:381
  214.4 5.5 %collective-permute-done.25 = bf16[8,64,256]{2,1,0:T(8,128)(2,1)S(1)} collective-permute-done((bf16[8,64,256]{2,1,0:T(8,128)(2,1)S(1)}, bf16[8,64,256]{2,1,0:T(8,128)(2,1)S(1)}, u32[]{:S(2)}, u32[]{:S(2)}) %collective-permute-start.25) | collective-permute-done | bytes 262176 | tf_op jit(solution)/shard_map/ppermute | solution.py:381
  222.5 2.4 collective-permute-done.26
  224.9 17.1 %collective-permute-done.27 = bf16[4,64,256]{2,1,0:T(8,128)(2,1)S(1)} collective-permute-done((bf16[4,64,256]{2,1,0:T(8,128)(2,1)S(1)}, bf16[4,64,256]{2,1,0:T(8,128)(2,1)S(1)}, u32[]{:S(2)}, u32[]{:S(2)}) %collective-permute-start.27) | collective-permute-done | bytes 131104 | tf_op jit(solution)/shard_map/ppermute | solution.py:381
  (133 shorter events, 48.7 us)
Async XLA Ops:
  2.1 47.9 %collective-permute-start.5 = (bf16[32,64,256]{2,1,0:T(8,128)(2,1)}, bf16[32,64,256]{2,1,0:T(8,128)(2,1)}, u32[]{:S(2)}, u32[]{:S(2)}) collective-permute-start(bf16[32,64,256]{2,1,0:T(8,128)(2,1)} %refs_15_.1), channel_id=1, source_target_pairs={{0,2},{1,3},{2,0},{3,1},{4,6},{5,7},{6,4},{7,5},{8,10},{9,11},{10,... | collective-permute-start | bytes 3145736 | tf_op jit(solution)/shard_map/ppermute | solution.py:381
  16.2 20.6 %collective-permute-start.1 = (bf16[1024,256]{1,0:T(8,128)(2,1)S(1)}, bf16[1024,256]{1,0:T(8,128)(2,1)S(1)}, u32[]{:S(2)}, u32[]{:S(2)}) collective-permute-start(bf16[1024,256]{1,0:T(8,128)(2,1)S(1)} %pad_maximum_fusion.1), channel_id=1, source_target_pairs={{0,4},{1,5},{2,6},{3,7},{4,0},{5,1},{6,2},{7,3},{8,12},{9,13},{10,... | collective-permute-start | bytes 1572872 | tf_op jit(solution)/shard_map/ppermute | solution.py:381
  16.4 26.2 %collective-permute-start.2 = (f32[65,8,128]{2,1,0:T(8,128)S(1)}, f32[65,8,128]{2,1,0:T(8,128)S(1)}, u32[]{:S(2)}, u32[]{:S(2)}) collective-permute-start(f32[65,8,128]{2,1,0:T(8,128)S(1)} %get-tuple-element.56), channel_id=1, source_target_pairs={{0,4},{1,5},{2,6},{3,7},{4,0},{5,1},{6,2},{7,3},{8,12},{9,13},{10,... | collective-permute-start | bytes 798728 | tf_op jit(solution)/shard_map/ppermute | solution.py:381
  18.3 24.3 %collective-permute-start.3 = (f32[65,8,128]{2,1,0:T(8,128)S(1)}, f32[65,8,128]{2,1,0:T(8,128)S(1)}, u32[]{:S(2)}, u32[]{:S(2)}) collective-permute-start(f32[65,8,128]{2,1,0:T(8,128)S(1)} %get-tuple-element.57), channel_id=1, source_target_pairs={{0,8},{1,9},{2,10},{3,11},{4,12},{5,13},{6,14},{7,15},{8,0},{9,1},... | collective-permute-start | bytes 798728 | tf_op jit(solution)/shard_map/ppermute | solution.py:381
  20.4 29.6 %collective-permute-start.4 = (f32[65,8,128]{2,1,0:T(8,128)S(1)}, f32[65,8,128]{2,1,0:T(8,128)}, u32[]{:S(2)}, u32[]{:S(2)}) collective-permute-start(f32[65,8,128]{2,1,0:T(8,128)S(1)} %get-tuple-element.58), channel_id=1, source_target_pairs={{0,12},{1,13},{2,14},{3,15},{4,8},{5,9},{6,10},{7,11},{8,4},{9,5},... | collective-permute-start | bytes 798728 | tf_op jit(solution)/shard_map/ppermute | solution.py:381
  36.8 54.7 %collective-permute-start.13 = (bf16[32,64,256]{2,1,0:T(8,128)(2,1)}, bf16[32,64,256]{2,1,0:T(8,128)(2,1)}, u32[]{:S(2)}, u32[]{:S(2)}) collective-permute-start(bf16[32,64,256]{2,1,0:T(8,128)(2,1)} %refs_15_.1), channel_id=1, source_target_pairs={{0,1},{1,0},{2,3},{3,2},{4,5},{5,4},{6,7},{7,6},{8,9},{9,8},{10,11... | collective-permute-start | bytes 3145736 | tf_op jit(solution)/shard_map/ppermute | solution.py:381
  42.6 21.9 %collective-permute-start.10 = (bf16[24,64,128]{2,1,0:T(8,128)(2,1)S(1)}, bf16[24,64,128]{2,1,0:T(8,128)(2,1)S(1)}, u32[]{:S(2)}, u32[]{:S(2)}) collective-permute-start(bf16[24,64,128]{2,1,0:T(8,128)(2,1)S(1)} %get-tuple-element.69), channel_id=1, source_target_pairs={{0,4},{1,5},{2,6},{3,7},{4,0},{5,1},{6,2},{7,3},{8,12},{9,13},{10,... | collective-permute-start | bytes 1179656 | tf_op jit(solution)/shard_map/ppermute | solution.py:381
  42.6 31.0 %collective-permute-start.11 = (bf16[24,64,128]{2,1,0:T(8,128)(2,1)S(1)}, bf16[24,64,128]{2,1,0:T(8,128)(2,1)S(1)}, u32[]{:S(2)}, u32[]{:S(2)}) collective-permute-start(bf16[24,64,128]{2,1,0:T(8,128)(2,1)S(1)} %get-tuple-element.71), channel_id=1, source_target_pairs={{0,8},{1,9},{2,10},{3,11},{4,12},{5,13},{6,14},{7,15},{8,0},{9,1},... | collective-permute-start | bytes 1179656 | tf_op jit(solution)/shard_map/ppermute | solution.py:381
  50.0 21.9 %collective-permute-start.9 = (bf16[2048,256]{1,0:T(8,128)(2,1)}, bf16[2048,256]{1,0:T(8,128)(2,1)}, u32[]{:S(2)}, u32[]{:S(2)}) collective-permute-start(bf16[2048,256]{1,0:T(8,128)(2,1)} %pad_maximum_fusion.refs_19_), channel_id=1, source_target_pairs={{0,2},{1,3},{2,0},{3,1},{4,6},{5,7},{6,4},{7,5},{8,10},{9,11},{10,... | collective-permute-start | bytes 3145736 | tf_op jit(solution)/shard_map/ppermute | solution.py:381
  54.1 39.9 %collective-permute-start.15 = (bf16[2048,256]{1,0:T(8,128)(2,1)}, bf16[2048,256]{1,0:T(8,128)(2,1)}, u32[]{:S(2)}, u32[]{:S(2)}) collective-permute-start(bf16[2048,256]{1,0:T(8,128)(2,1)} %pad_maximum_fusion.refs_19_), channel_id=1, source_target_pairs={{0,1},{1,0},{2,3},{3,2},{4,5},{5,4},{6,7},{7,6},{8,9},{9,8},{10,11... | collective-permute-start | bytes 3145736 | tf_op jit(solution)/shard_map/ppermute | solution.py:381
  65.3 27.1 %collective-permute-start.14 = (bf16[32,64,256]{2,1,0:T(8,128)(2,1)}, bf16[32,64,256]{2,1,0:T(8,128)(2,1)}, u32[]{:S(2)}, u32[]{:S(2)}) collective-permute-start(bf16[32,64,256]{2,1,0:T(8,128)(2,1)} %collective-permute-done.5.refs_16_), channel_id=1, source_target_pairs={{0,1},{1,0},{2,3},{3,2},{4,5},{5,4},{6,7},{7,6},{8,9},{9,8},{10,11... | collective-permute-start | bytes 3145736 | tf_op jit(solution)/shard_map/ppermute | solution.py:381
  71.9 23.2 %collective-permute-start.16 = (bf16[2048,256]{1,0:T(8,128)(2,1)}, bf16[2048,256]{1,0:T(8,128)(2,1)}, u32[]{:S(2)}, u32[]{:S(2)}) collective-permute-start(bf16[2048,256]{1,0:T(8,128)(2,1)} %collective-permute-done.9.refs_20_), channel_id=1, source_target_pairs={{0,1},{1,0},{2,3},{3,2},{4,5},{5,4},{6,7},{7,6},{8,9},{9,8},{10,11... | collective-permute-start | bytes 3145736 | tf_op jit(solution)/shard_map/ppermute | solution.py:381
  88.1 44.8 %collective-permute-start.17 = (bf16[24,64,128]{2,1,0:T(8,128)(2,1)}, bf16[24,64,128]{2,1,0:T(8,128)(2,1)}, u32[]{:S(2)}, u32[]{:S(2)}) collective-permute-start(bf16[24,64,128]{2,1,0:T(8,128)(2,1)} %copy-done.15), channel_id=1, source_target_pairs={{0,4},{1,5},{2,6},{3,7},{4,0},{5,1},{6,2},{7,3},{8,12},{9,13},{10,... | collective-permute-start | bytes 1179656 | tf_op jit(solution)/shard_map/ppermute | solution.py:381
  91.5 60.2 %collective-permute-start.18 = (bf16[24,64,128]{2,1,0:T(8,128)(2,1)}, bf16[24,64,128]{2,1,0:T(8,128)(2,1)}, u32[]{:S(2)}, u32[]{:S(2)}) collective-permute-start(bf16[24,64,128]{2,1,0:T(8,128)(2,1)} %copy-done.14), channel_id=1, source_target_pairs={{0,8},{1,9},{2,10},{3,11},{4,12},{5,13},{6,14},{7,15},{8,0},{9,1},... | collective-permute-start | bytes 1179656 | tf_op jit(solution)/shard_map/ppermute | solution.py:381
  92.4 59.3 %collective-permute-start.19 = (bf16[24,64,128]{2,1,0:T(8,128)(2,1)}, bf16[24,64,128]{2,1,0:T(8,128)(2,1)}, u32[]{:S(2)}, u32[]{:S(2)}) collective-permute-start(bf16[24,64,128]{2,1,0:T(8,128)(2,1)} %copy-done.13), channel_id=1, source_target_pairs={{0,12},{1,13},{2,14},{3,15},{4,8},{5,9},{6,10},{7,11},{8,4},{9,5},... | collective-permute-start | bytes 1179656 | tf_op jit(solution)/shard_map/ppermute | solution.py:381
  94.0 60.6 %collective-permute-start.6 = (bf16[16,64,128]{2,1,0:T(8,128)(2,1)}, bf16[16,64,128]{2,1,0:T(8,128)(2,1)S(1)}, u32[]{:S(2)}, u32[]{:S(2)}) collective-permute-start(bf16[16,64,128]{2,1,0:T(8,128)(2,1)} %copy-done.25), channel_id=1, source_target_pairs={{0,4},{1,5},{2,6},{3,7},{4,0},{5,1},{6,2},{7,3},{8,12},{9,13},{10,... | collective-permute-start | bytes 786440 | tf_op jit(solution)/shard_map/ppermute | solution.py:381
  95.1 59.5 %collective-permute-start.7 = (bf16[16,64,128]{2,1,0:T(8,128)(2,1)}, bf16[16,64,128]{2,1,0:T(8,128)(2,1)S(1)}, u32[]{:S(2)}, u32[]{:S(2)}) collective-permute-start(bf16[16,64,128]{2,1,0:T(8,128)(2,1)} %copy-done.24), channel_id=1, source_target_pairs={{0,8},{1,9},{2,10},{3,11},{4,12},{5,13},{6,14},{7,15},{8,0},{9,1},... | collective-permute-start | bytes 786440 | tf_op jit(solution)/shard_map/ppermute | solution.py:381
  132.9 23.9 %collective-permute-start.8 = (bf16[16,64,128]{2,1,0:T(8,128)(2,1)S(1)}, bf16[16,64,128]{2,1,0:T(8,128)(2,1)S(1)}, u32[]{:S(2)}, u32[]{:S(2)}) collective-permute-start(bf16[16,64,128]{2,1,0:T(8,128)(2,1)S(1)} %copy-done.23), channel_id=1, source_target_pairs={{0,12},{1,13},{2,14},{3,15},{4,8},{5,9},{6,10},{7,11},{8,4},{9,5},... | collective-permute-start | bytes 786440 | tf_op jit(solution)/shard_map/ppermute | solution.py:381
  170.0 19.8 %collective-permute-start.23 = (bf16[16,64,256]{2,1,0:T(8,128)(2,1)S(1)}, bf16[16,64,256]{2,1,0:T(8,128)(2,1)S(1)}, u32[]{:S(2)}, u32[]{:S(2)}) collective-permute-start(bf16[16,64,256]{2,1,0:T(8,128)(2,1)S(1)} %get-tuple-element.102), channel_id=1, source_target_pairs={{0,8},{1,9},{2,10},{3,11},{4,12},{5,13},{6,14},{7,15},{8,0},{9,1},... | collective-permute-start | bytes 1572872 | tf_op jit(solution)/shard_map/ppermute | solution.py:381
  189.8 24.5 %collective-permute-start.24 = (bf16[8,64,256]{2,1,0:T(8,128)(2,1)S(1)}, bf16[8,64,256]{2,1,0:T(8,128)(2,1)S(1)}, u32[]{:S(2)}, u32[]{:S(2)}) collective-permute-start(bf16[8,64,256]{2,1,0:T(8,128)(2,1)S(1)} %slice.130), channel_id=1, source_target_pairs={{0,8},{1,9},{2,10},{3,11},{4,12},{5,13},{6,14},{7,15},{8,0},{9,1},... | collective-permute-start | bytes 786440 | tf_op jit(solution)/shard_map/ppermute | solution.py:381
  192.7 27.2 %collective-permute-start.25 = (bf16[8,64,256]{2,1,0:T(8,128)(2,1)S(1)}, bf16[8,64,256]{2,1,0:T(8,128)(2,1)S(1)}, u32[]{:S(2)}, u32[]{:S(2)}) collective-permute-start(bf16[8,64,256]{2,1,0:T(8,128)(2,1)S(1)} %slice.129), channel_id=1, source_target_pairs={{0,4},{1,5},{2,6},{3,7},{4,0},{5,1},{6,2},{7,3},{8,12},{9,13},{10,... | collective-permute-start | bytes 786440 | tf_op jit(solution)/shard_map/ppermute | solution.py:381
  213.6 29.3 %collective-permute-start.28 = (bf16[32,64,256]{2,1,0:T(8,128)(2,1)S(1)}, bf16[32,64,256]{2,1,0:T(8,128)(2,1)S(1)}, u32[]{:S(2)}, u32[]{:S(2)}) collective-permute-start(bf16[32,64,256]{2,1,0:T(8,128)(2,1)S(1)} %copy-done.12), channel_id=1, source_target_pairs={{0,1},{1,0},{2,3},{3,2},{4,5},{5,4},{6,7},{7,6},{8,9},{9,8},{10,11... | collective-permute-start | bytes 3145736 | tf_op jit(solution)/shard_map/ppermute | solution.py:381
  213.7 29.3 %collective-permute-start.29 = (bf16[32,64,256]{2,1,0:T(8,128)(2,1)S(1)}, bf16[32,64,256]{2,1,0:T(8,128)(2,1)S(1)}, u32[]{:S(2)}, u32[]{:S(2)}) collective-permute-start(bf16[32,64,256]{2,1,0:T(8,128)(2,1)S(1)} %add_convert_fusion), channel_id=1, source_target_pairs={{0,2},{1,3},{2,0},{3,1},{4,6},{5,7},{6,4},{7,5},{8,10},{9,11},{10,... | collective-permute-start | bytes 3145736 | tf_op jit(solution)/shard_map/ppermute | solution.py:381
  221.8 20.3 %collective-permute-start.27 = (bf16[4,64,256]{2,1,0:T(8,128)(2,1)S(1)}, bf16[4,64,256]{2,1,0:T(8,128)(2,1)S(1)}, u32[]{:S(2)}, u32[]{:S(2)}) collective-permute-start(bf16[4,64,256]{2,1,0:T(8,128)(2,1)S(1)} %slice.131), channel_id=1, source_target_pairs={{0,2},{1,3},{2,0},{3,1},{4,6},{5,7},{6,4},{7,5},{8,10},{9,11},{10,... | collective-permute-start | bytes 393224 | tf_op jit(solution)/shard_map/ppermute | solution.py:381
  (34 other events, 437.4 us)
where the time goes:
time: 246 us; the launch traced here: 245 us
  waiting for transfers between devices  88.5 us (36%)
  starting transfers between devices  77.5 us (32%)
  Pallas kernels  43.5 us (18%)
  local copies, waits for them, and re-layouts  24.3 us (10%)
  other arithmetic  10 us (4%)
    ppermute x30, waiting for transfers between devices, partner(): lax.ppermute(values, 'tile', [(i, i ^ distance) for i in range(devices)])  88.5 us
    ppermute x30, starting transfers between devices, partner(): lax.ppermute(values, 'tile', [(i, i ^ distance) for i in range(devices)])  77.5 us
    pallas_call x3, Pallas kernels, fit(): pl.pallas_call(functools.partial(fit_kernel, first, final, layers, slots,...  38.5 us
    unnamed x57, local copies, waits for them, and re-layouts  13.6 us
    pallas_call x1, Pallas kernels, pack(): pl.pallas_call(functools.partial(pack_kernel, local_tiles, layers, slots)...  5.03 us
  transfers between devices with their start and end apart: 30, of which 14 were waited for; matrix products, arithmetic and copies ran while one was open for 7% of the time, Pallas kernels for 16%

commit v1 on v0

--- a/solution.py
+++ b/solution.py
@@ -266,16 +266,21 @@
             make_strips(near_next, k, range(low, high, 16), sights, green_next)
 
         model = jnp.dot(screens[screen], hats[...], preferred_element_type=jnp.float32)
+        side = lax.broadcasted_iota(jnp.int32, (1, 2 * epochs), 1) >= epochs
+        turned = jnp.zeros((CHUNK, 2 * epochs), jnp.float32)
         for k in range(NEAR):
-            model += lax.dot_general(
-                stress[pl.ds(pl.multiple_of(spots[near[k]], 16), epochs), :],
+            both = jnp.dot(
                 green[:, k * PBLK : (k + 1) * PBLK],
-                (((1,), (1,)), ((), ())),
+                stress[pl.ds(pl.multiple_of(spots[near[k]], PBLK), PBLK), :],
                 preferred_element_type=jnp.float32,
             )
+            odd = lax.rem(near[k], 2) == 1
+            turned += jnp.where(side == odd, both, 0.0)
         make_hats(rows, hats_next)
         spread(rows, sights)
         fill(0, 0, CHUNK // 2)
+        turned = turned.T
+        model += turned[:epochs] + turned[epochs:]
         fill(0, CHUNK // 2, CHUNK)
         live = jnp.where(i < total, info_of(slot, 0), 0)
         lane = lax.broadcasted_iota(jnp.int32, (1, CHUNK), 1)
@@ -404,7 +409,7 @@
     place = (((other & 1) * 2 + upper) * chips + spot) * half + seat % half
     stages = devices.bit_length() - 1
     held = sum(((other >> (stages - 1 - s)) & 1) << s for s in range(stages))
-    return place.astype(jnp.int32), ((held * local + seat) * epochs).astype(jnp.int32)
+    return place.astype(jnp.int32), ((held * local + seat) // 2 * PBLK).astype(jnp.int32)
 
 
 def halve(kept, given, there, devices):
@@ -413,7 +418,7 @@
     parts = [total[:middle], total[middle:]]
     both = orders(devices)
     stages = len(both[0])
-    back = None
+    back = partner(there, devices, PAIR)
     for stage in range(stages):
         got = []
         for side in range(2):
@@ -426,9 +431,6 @@
                 parts[0], got[1] = lax.optimization_barrier((parts[0], got[1]))
             size = parts[side].shape[0] // 2
             parts[side] = parts[side][:size] + got[side].astype(jnp.float32)
-            if back is None:
-                parts[0], there = lax.optimization_barrier((parts[0], there))
-                back = partner(there, devices, PAIR)
     return jnp.concatenate(parts, axis=0), back
 
 
@@ -452,7 +454,8 @@
     slots = LAYER * (2 * blocks // devices) * (width // CHUNK)
     sizes = round_sizes(slots)
 
-    held = jnp.swapaxes(stress.reshape(epochs, local, PBLK), 0, 1).reshape(-1, PBLK)
+    held = jnp.transpose(stress.reshape(epochs, local // 2, 2, PBLK), (1, 3, 2, 0))
+    held = held.reshape(local // 2 * PBLK, 2 * epochs)
     other = partner(held, devices, devices // 2)
     across_screens = partner(screens, devices, PAIR)
     obs, pix = pack(

time: 246 us -> 244 us (level)
  the two profiles are of different devices: /device:TPU:26 before, /device:TPU:0 now
where the time goes in v1:
time: 244 us; the launch traced here: 243 us
  starting transfers between devices  88.9 us (36%)
  waiting for transfers between devices  71.9 us (29%)
  Pallas kernels  46.9 us (19%)
  local copies, waits for them, and re-layouts  23.9 us (10%)
  other arithmetic  10 us (4%)
    ppermute x30, starting transfers between devices, partner(): lax.ppermute(values, 'tile', [(i, i ^ distance) for i in range(devices)])  88.9 us
    ppermute x30, waiting for transfers between devices, partner(): lax.ppermute(values, 'tile', [(i, i ^ distance) for i in range(devices)])  71.9 us
    pallas_call x3, Pallas kernels, fit(): pl.pallas_call(functools.partial(fit_kernel, first, final, layers, slots,...  41.8 us
    unnamed x54, local copies, waits for them, and re-layouts  12.6 us
    pallas_call x1, Pallas kernels, pack(): pl.pallas_call(functools.partial(pack_kernel, local_tiles, layers, slots)...  5.08 us
  transfers between devices with their start and end apart: 30, of which 14 were waited for; matrix products, arithmetic and copies ran while one was open for 8% of the time, Pallas kernels for 18%

profile of v1, /device:TPU:0, one launch (start us, length us, event | category | flops | bytes accessed | tf_op | source)
XLA Modules:
  0.0 242.6 jit_solution(5948342373252886517)
XLA Ops:
  2.3 4.1 %collective-permute-start = (bf16[1024,128]{1,0:T(8,128)(2,1)S(1)}, bf16[1024,128]{1,0:T(8,128)(2,1)S(1)}, u32[]{:S(2)}, u32[]{:S(2)}) collective-permute-start(bf16[1024,128]{1,0:T(8,128)(2,1)S(1)} %copy.24), channel_id=1, source_target_pairs={{0,8},{1,9},{2,10},{3,11},{4,12},{5,13},{6,14},{7,15},{8,0},{9,1},... | collective-permute-start | bytes 786440 | tf_op jit(solution)/shard_map/ppermute | solution.py:386
  9.0 5.1 %pack.1 = (bf16[24,64,128]{2,1,0:T(8,128)(2,1)S(1)}, bf16[24,64,128]{2,1,0:T(8,128)(2,1)S(1)}, bf16[24,64,128]{2,1,0:T(8,128)(2,1)S(1)}, bf16[24,64,128]{2,1,0:T...) custom-call(s32[1]{0:T(128)} %bitcast.1.here, ...), custom_call_target="tpu_custom_call" | custom-call | tf_op jit(solution)/shard_map/pack/pallas_call | solution.py:96
  23.2 17.5 %collective-permute-done.1 = bf16[2048,128]{1,0:T(8,128)(2,1)S(1)} collective-permute-done((bf16[2048,128]{1,0:T(8,128)(2,1)S(1)}, bf16[2048,128]{1,0:T(8,128)(2,1)S(1)}, u32[]{:S(2)}, u32[]{:S(2)}) %collective-permute-start.1) | collective-permute-done | bytes 524320 | tf_op jit(solution)/shard_map/ppermute | solution.py:386
  45.5 3.4 %collective-permute-start.11 = (bf16[24,64,128]{2,1,0:T(8,128)(2,1)S(1)}, bf16[24,64,128]{2,1,0:T(8,128)(2,1)S(1)}, u32[]{:S(2)}, u32[]{:S(2)}) collective-permute-start(bf16[24,64,128]{2,1,0:T(8,128)(2,1)S(1)} %get-tuple-element.69), channel_id=1, source_target_pairs={{0,8},{1,9},{2,10},{3,11},{4,12},{5,13},{6,14},{7,15},{8,0},{9,1},... | collective-permute-start | bytes 1179656 | tf_op jit(solution)/shard_map/ppermute | solution.py:386
  49.0 3.0 %collective-permute-done.4.refs_12_ = f32[65,8,128]{2,1,0:T(8,128)} collective-permute-done((f32[65,8,128]{2,1,0:T(8,128)S(1)}, f32[65,8,128]{2,1,0:T(8,128)}, u32[]{:S(2)}, u32[]{:S(2)}) %collective-permute-start.4) | collective-permute-done | bytes 266272 | tf_op jit(solution)/shard_map/ppermute | solution.py:386
  54.5 8.1 %collective-permute-done.10.refs_6_ = bf16[24,64,128]{2,1,0:T(8,128)(2,1)S(1)} collective-permute-done((bf16[24,64,128]{2,1,0:T(8,128)(2,1)S(1)}, bf16[24,64,128]{2,1,0:T(8,128)(2,1)S(1)}, u32[]{:S(2)}, u32[]{:S(2)}) %collective-permute-start.10) | collective-permute-done | bytes 393248 | tf_op jit(solution)/shard_map/ppermute | solution.py:386
  63.4 12.8 %collective-permute-done.9.refs_20_ = bf16[4096,128]{1,0:T(8,128)(2,1)} collective-permute-done((bf16[4096,128]{1,0:T(8,128)(2,1)}, bf16[4096,128]{1,0:T(8,128)(2,1)}, u32[]{:S(2)}, u32[]{:S(2)}) %collective-permute-start.9) | collective-permute-done | bytes 1048608 | tf_op jit(solution)/shard_map/ppermute | solution.py:386
  83.4 4.7 %concatenate.21 = bf16[32,128,256]{2,0,1:T(8,128)(2,1)S(1)} concatenate(bf16[4,128,256]{2,0,1:T(4,128)(2,1)S(1)} %get-tuple-element.104, bf16[4,128,256]{2,0,1:T(4,128)(2,1)S(1)} %get-tuple-element.103, bf16[4,128,256]{2,0,1:T(4,128)(2,1)S(1)} %get-tuple-element.104, bf16[4,128,256]{2,0,1:T(4,128)(2,1)} %get-tuple-element.102, bf16[4,128,256]{2,0,1:T(4,128)(2,1)S(1)} %get-tuple-element.103, ...), dimensions={0} | concatenate | bytes 4194304 | tf_op jit(solution)/shard_map/concatenate | solution.py:508
  92.4 8.9 %collective-permute-start.17 = (bf16[24,64,128]{2,1,0:T(8,128)(2,1)}, bf16[24,64,128]{2,1,0:T(8,128)(2,1)}, u32[]{:S(2)}, u32[]{:S(2)}) collective-permute-start(bf16[24,64,128]{2,1,0:T(8,128)(2,1)} %copy-done.13), channel_id=1, source_target_pairs={{0,4},{1,5},{2,6},{3,7},{4,0},{5,1},{6,2},{7,3},{8,12},{9,13},{10,... | collective-permute-start | bytes 1179656 | tf_op jit(solution)/shard_map/ppermute | solution.py:386
  101.3 2.4 collective-permute-start.19
  109.8 35.0 %fit.3 = (f32[128,64,256]{2,1,0:T(8,128)S(1)}, f32[128,64,256]{2,1,0:T(8,128)S(1)}, bf16[128,64,256]{2,1,0:T(8,128)(2,1)S(1)}, bf16[16384,128]{1,0:T(8,128)(2,1)S(1)}) custom-call(s32[768]{0:T(1024)S(1)} %convert_element_type.49.refs_0_, s32[1536]{0:T(1024)S(1)} %reshape.52.refs_1_, s32[128]{0:T(128)S(1)} %get-tuple-element.108.refs_2_, ...), custom_call_target="tpu_custom_call" | custom-call | flops 3221225472 | bytes 20971520 | tf_op jit(solution)/shard_map/fit/pallas_call | solution.py:350
  144.8 18.4 %collective-permute-start.8 = (bf16[16,64,128]{2,1,0:T(8,128)(2,1)S(1)}, bf16[16,64,128]{2,1,0:T(8,128)(2,1)S(1)}, u32[]{:S(2)}, u32[]{:S(2)}) collective-permute-start(bf16[16,64,128]{2,1,0:T(8,128)(2,1)S(1)} %copy-done.21), channel_id=1, source_target_pairs={{0,12},{1,13},{2,14},{3,15},{4,8},{5,9},{6,10},{7,11},{8,4},{9,5},... | collective-permute-start | bytes 786440 | tf_op jit(solution)/shard_map/ppermute | solution.py:386
  163.2 2.9 %fit.4 = (f32[128,64,256]{2,1,0:T(8,128)S(1)}, f32[128,64,256]{2,1,0:T(8,128)S(1)}) custom-call(s32[768]{0:T(1024)S(1)} %convert_element_type.49.refs_0_, s32[1536]{0:T(1024)S(1)} %reshape.52.refs_1_, s32[128]{0:T(128)S(1)} %get-tuple-element.108.refs_2_, s32[128]{0:T(128)S(1)} %get-tuple-element.109.refs_3_, ...), custom_call_target="tpu_custom_call", output_to_operand_aliasing={{0}: (17, {}), {1}: (18, {})} | custom-call | flops 3221225472 | bytes 20971520 | tf_op jit(solution)/shard_map/fit/pallas_call | solution.py:350
  166.2 2.5 %collective-permute-done.8.refs_8_ = bf16[16,64,128]{2,1,0:T(8,128)(2,1)S(1)} collective-permute-done((bf16[16,64,128]{2,1,0:T(8,128)(2,1)S(1)}, bf16[16,64,128]{2,1,0:T(8,128)(2,1)S(1)}, u32[]{:S(2)}, u32[]{:S(2)}) %collective-permute-start.8) | collective-permute-done | bytes 262176 | tf_op jit(solution)/shard_map/ppermute | solution.py:386
  168.7 3.9 %fit.5 = (f32[128,64,256]{2,1,0:T(8,128)S(1)}, f32[128,64,256]{2,1,0:T(8,128)S(1)}, bf16[64,64,256]{2,1,0:T(8,128)(2,1)S(1)}, bf16[32,64,256]{2,1,0:T(8,128)(2,1)}, bf16[32,64,256]{2,1,0:T(8,128)(2,1)}) custom-call(s32[768]{0:T(1024)S(1)} %convert_element_type.49.refs_0_, s32[1536]{0:T(1024)S(1)} %reshape.52.refs_1_, ...), custom_call_target="tpu_custom_call", output_to_operand_aliasing={{0}: (17, {}), {1}: (18, {})} | custom-call | flops 2147483648 | bytes 20971520 | tf_op jit(solution)/shard_map/fit/pallas_call | solution.py:350
  173.3 5.8 %collective-permute-done.20 = bf16[64,64,256]{2,1,0:T(8,128)(2,1)S(1)} collective-permute-done((bf16[64,64,256]{2,1,0:T(8,128)(2,1)S(1)}, bf16[64,64,256]{2,1,0:T(8,128)(2,1)S(1)}, u32[]{:S(2)}, u32[]{:S(2)}) %collective-permute-start.20) | collective-permute-done | bytes 2097184 | tf_op jit(solution)/shard_map/ppermute | solution.py:386
  182.8 5.4 %collective-permute-start.22 = (bf16[16,64,256]{2,1,0:T(8,128)(2,1)S(1)}, bf16[16,64,256]{2,1,0:T(8,128)(2,1)S(1)}, u32[]{:S(2)}, u32[]{:S(2)}) collective-permute-start(bf16[16,64,256]{2,1,0:T(8,128)(2,1)S(1)} %get-tuple-element.98), channel_id=1, source_target_pairs={{0,8},{1,9},{2,10},{3,11},{4,12},{5,13},{6,14},{7,15},{8,0},{9,1},... | collective-permute-start | bytes 1572872 | tf_op jit(solution)/shard_map/ppermute | solution.py:386
  188.1 6.9 %collective-permute-done.21 = bf16[16,64,256]{2,1,0:T(8,128)(2,1)S(1)} collective-permute-done((bf16[16,64,256]{2,1,0:T(8,128)(2,1)S(1)}, bf16[16,64,256]{2,1,0:T(8,128)(2,1)S(1)}, u32[]{:S(2)}, u32[]{:S(2)}) %collective-permute-start.21) | collective-permute-done | bytes 524320 | tf_op jit(solution)/shard_map/ppermute | solution.py:386
  195.2 4.6 %collective-permute-done.22 = bf16[16,64,256]{2,1,0:T(8,128)(2,1)S(1)} collective-permute-done((bf16[16,64,256]{2,1,0:T(8,128)(2,1)S(1)}, bf16[16,64,256]{2,1,0:T(8,128)(2,1)S(1)}, u32[]{:S(2)}, u32[]{:S(2)}) %collective-permute-start.22) | collective-permute-done | bytes 524320 | tf_op jit(solution)/shard_map/ppermute | solution.py:386
  200.0 2.7 %collective-permute-start.23 = (bf16[8,64,256]{2,1,0:T(8,128)(2,1)S(1)}, bf16[8,64,256]{2,1,0:T(8,128)(2,1)S(1)}, u32[]{:S(2)}, u32[]{:S(2)}) collective-permute-start(bf16[8,64,256]{2,1,0:T(8,128)(2,1)S(1)} %slice.130), channel_id=1, source_target_pairs={{0,8},{1,9},{2,10},{3,11},{4,12},{5,13},{6,14},{7,15},{8,0},{9,1},... | collective-permute-start | bytes 786440 | tf_op jit(solution)/shard_map/ppermute | solution.py:386
  202.7 18.4 %collective-permute-start.24 = (bf16[8,64,256]{2,1,0:T(8,128)(2,1)S(1)}, bf16[8,64,256]{2,1,0:T(8,128)(2,1)S(1)}, u32[]{:S(2)}, u32[]{:S(2)}) collective-permute-start(bf16[8,64,256]{2,1,0:T(8,128)(2,1)S(1)} %slice.129), channel_id=1, source_target_pairs={{0,4},{1,5},{2,6},{3,7},{4,0},{5,1},{6,2},{7,3},{8,12},{9,13},{10,... | collective-permute-start | bytes 786440 | tf_op jit(solution)/shard_map/ppermute | solution.py:386
  221.1 1.8 convert_add_fusion.1
  223.0 3.8 %collective-permute-done.24 = bf16[8,64,256]{2,1,0:T(8,128)(2,1)S(1)} collective-permute-done((bf16[8,64,256]{2,1,0:T(8,128)(2,1)S(1)}, bf16[8,64,256]{2,1,0:T(8,128)(2,1)S(1)}, u32[]{:S(2)}, u32[]{:S(2)}) %collective-permute-start.24) | collective-permute-done | bytes 262176 | tf_op jit(solution)/shard_map/ppermute | solution.py:386
  226.9 9.7 %collective-permute-start.25 = (bf16[4,64,256]{2,1,0:T(8,128)(2,1)S(1)}, bf16[4,64,256]{2,1,0:T(8,128)(2,1)S(1)}, u32[]{:S(2)}, u32[]{:S(2)}) collective-permute-start(bf16[4,64,256]{2,1,0:T(8,128)(2,1)S(1)} %slice.132), channel_id=1, source_target_pairs={{0,4},{1,5},{2,6},{3,7},{4,0},{5,1},{6,2},{7,3},{8,12},{9,13},{10,... | collective-permute-start | bytes 393224 | tf_op jit(solution)/shard_map/ppermute | solution.py:386
  (132 shorter events, 49.6 us)
Async XLA Ops:
  2.3 17.7 %collective-permute-start = (bf16[1024,128]{1,0:T(8,128)(2,1)S(1)}, bf16[1024,128]{1,0:T(8,128)(2,1)S(1)}, u32[]{:S(2)}, u32[]{:S(2)}) collective-permute-start(bf16[1024,128]{1,0:T(8,128)(2,1)S(1)} %copy.24), channel_id=1, source_target_pairs={{0,8},{1,9},{2,10},{3,11},{4,12},{5,13},{6,14},{7,15},{8,0},{9,1},... | collective-permute-start | bytes 786440 | tf_op jit(solution)/shard_map/ppermute | solution.py:386
  6.4 45.6 %collective-permute-start.5 = (bf16[32,64,256]{2,1,0:T(8,128)(2,1)}, bf16[32,64,256]{2,1,0:T(8,128)(2,1)}, u32[]{:S(2)}, u32[]{:S(2)}) collective-permute-start(bf16[32,64,256]{2,1,0:T(8,128)(2,1)} %refs_15_.1), channel_id=1, source_target_pairs={{0,2},{1,3},{2,0},{3,1},{4,6},{5,7},{6,4},{7,5},{8,10},{9,11},{10,... | collective-permute-start | bytes 3145736 | tf_op jit(solution)/shard_map/ppermute | solution.py:386
  20.0 20.6 %collective-permute-start.1 = (bf16[2048,128]{1,0:T(8,128)(2,1)S(1)}, bf16[2048,128]{1,0:T(8,128)(2,1)S(1)}, u32[]{:S(2)}, u32[]{:S(2)}) collective-permute-start(bf16[2048,128]{1,0:T(8,128)(2,1)S(1)} %pad_maximum_fusion.1), channel_id=1, source_target_pairs={{0,4},{1,5},{2,6},{3,7},{4,0},{5,1},{6,2},{7,3},{8,12},{9,13},{10,... | collective-permute-start | bytes 1572872 | tf_op jit(solution)/shard_map/ppermute | solution.py:386
  21.7 79.6 %collective-permute-start.13 = (bf16[32,64,256]{2,1,0:T(8,128)(2,1)}, bf16[32,64,256]{2,1,0:T(8,128)(2,1)}, u32[]{:S(2)}, u32[]{:S(2)}) collective-permute-start(bf16[32,64,256]{2,1,0:T(8,128)(2,1)} %refs_15_.1), channel_id=1, source_target_pairs={{0,1},{1,0},{2,3},{3,2},{4,5},{5,4},{6,7},{7,6},{8,9},{9,8},{10,11... | collective-permute-start | bytes 3145736 | tf_op jit(solution)/shard_map/ppermute | solution.py:386
  22.2 22.4 %collective-permute-start.2 = (f32[65,8,128]{2,1,0:T(8,128)S(1)}, f32[65,8,128]{2,1,0:T(8,128)S(1)}, u32[]{:S(2)}, u32[]{:S(2)}) collective-permute-start(f32[65,8,128]{2,1,0:T(8,128)S(1)} %get-tuple-element.54), channel_id=1, source_target_pairs={{0,4},{1,5},{2,6},{3,7},{4,0},{5,1},{6,2},{7,3},{8,12},{9,13},{10,... | collective-permute-start | bytes 798728 | tf_op jit(solution)/shard_map/ppermute | solution.py:386
  22.7 22.8 %collective-permute-start.3 = (f32[65,8,128]{2,1,0:T(8,128)S(1)}, f32[65,8,128]{2,1,0:T(8,128)S(1)}, u32[]{:S(2)}, u32[]{:S(2)}) collective-permute-start(f32[65,8,128]{2,1,0:T(8,128)S(1)} %get-tuple-element.55), channel_id=1, source_target_pairs={{0,8},{1,9},{2,10},{3,11},{4,12},{5,13},{6,14},{7,15},{8,0},{9,1},... | collective-permute-start | bytes 798728 | tf_op jit(solution)/shard_map/ppermute | solution.py:386
  44.6 18.0 %collective-permute-start.10 = (bf16[24,64,128]{2,1,0:T(8,128)(2,1)S(1)}, bf16[24,64,128]{2,1,0:T(8,128)(2,1)S(1)}, u32[]{:S(2)}, u32[]{:S(2)}) collective-permute-start(bf16[24,64,128]{2,1,0:T(8,128)(2,1)S(1)} %get-tuple-element.67), channel_id=1, source_target_pairs={{0,4},{1,5},{2,6},{3,7},{4,0},{5,1},{6,2},{7,3},{8,12},{9,13},{10,... | collective-permute-start | bytes 1179656 | tf_op jit(solution)/shard_map/ppermute | solution.py:386
  45.5 32.4 %collective-permute-start.11 = (bf16[24,64,128]{2,1,0:T(8,128)(2,1)S(1)}, bf16[24,64,128]{2,1,0:T(8,128)(2,1)S(1)}, u32[]{:S(2)}, u32[]{:S(2)}) collective-permute-start(bf16[24,64,128]{2,1,0:T(8,128)(2,1)S(1)} %get-tuple-element.69), channel_id=1, source_target_pairs={{0,8},{1,9},{2,10},{3,11},{4,12},{5,13},{6,14},{7,15},{8,0},{9,1},... | collective-permute-start | bytes 1179656 | tf_op jit(solution)/shard_map/ppermute | solution.py:386
  52.0 24.2 %collective-permute-start.9 = (bf16[4096,128]{1,0:T(8,128)(2,1)}, bf16[4096,128]{1,0:T(8,128)(2,1)}, u32[]{:S(2)}, u32[]{:S(2)}) collective-permute-start(bf16[4096,128]{1,0:T(8,128)(2,1)} %pad_maximum_fusion.refs_19_), channel_id=1, source_target_pairs={{0,2},{1,3},{2,0},{3,1},{4,6},{5,7},{6,4},{7,5},{8,10},{9,11},{10,... | collective-permute-start | bytes 3145736 | tf_op jit(solution)/shard_map/ppermute | solution.py:386
  54.5 49.3 %collective-permute-start.15 = (bf16[4096,128]{1,0:T(8,128)(2,1)}, bf16[4096,128]{1,0:T(8,128)(2,1)}, u32[]{:S(2)}, u32[]{:S(2)}) collective-permute-start(bf16[4096,128]{1,0:T(8,128)(2,1)} %pad_maximum_fusion.refs_19_), channel_id=1, source_target_pairs={{0,1},{1,0},{2,3},{3,2},{4,5},{5,4},{6,7},{7,6},{8,9},{9,8},{10,11... | collective-permute-start | bytes 3145736 | tf_op jit(solution)/shard_map/ppermute | solution.py:386
  63.4 37.9 %collective-permute-start.14 = (bf16[32,64,256]{2,1,0:T(8,128)(2,1)}, bf16[32,64,256]{2,1,0:T(8,128)(2,1)}, u32[]{:S(2)}, u32[]{:S(2)}) collective-permute-start(bf16[32,64,256]{2,1,0:T(8,128)(2,1)} %collective-permute-done.5.refs_16_), channel_id=1, source_target_pairs={{0,1},{1,0},{2,3},{3,2},{4,5},{5,4},{6,7},{7,6},{8,9},{9,8},{10,11... | collective-permute-start | bytes 3145736 | tf_op jit(solution)/shard_map/ppermute | solution.py:386
  76.2 28.6 %collective-permute-start.16 = (bf16[4096,128]{1,0:T(8,128)(2,1)}, bf16[4096,128]{1,0:T(8,128)(2,1)}, u32[]{:S(2)}, u32[]{:S(2)}) collective-permute-start(bf16[4096,128]{1,0:T(8,128)(2,1)} %collective-permute-done.9.refs_20_), channel_id=1, source_target_pairs={{0,1},{1,0},{2,3},{3,2},{4,5},{5,4},{6,7},{7,6},{8,9},{9,8},{10,11... | collective-permute-start | bytes 3145736 | tf_op jit(solution)/shard_map/ppermute | solution.py:386
  92.4 52.4 %collective-permute-start.17 = (bf16[24,64,128]{2,1,0:T(8,128)(2,1)}, bf16[24,64,128]{2,1,0:T(8,128)(2,1)}, u32[]{:S(2)}, u32[]{:S(2)}) collective-permute-start(bf16[24,64,128]{2,1,0:T(8,128)(2,1)} %copy-done.13), channel_id=1, source_target_pairs={{0,4},{1,5},{2,6},{3,7},{4,0},{5,1},{6,2},{7,3},{8,12},{9,13},{10,... | collective-permute-start | bytes 1179656 | tf_op jit(solution)/shard_map/ppermute | solution.py:386
  101.3 61.9 %collective-permute-start.18 = (bf16[24,64,128]{2,1,0:T(8,128)(2,1)}, bf16[24,64,128]{2,1,0:T(8,128)(2,1)}, u32[]{:S(2)}, u32[]{:S(2)}) collective-permute-start(bf16[24,64,128]{2,1,0:T(8,128)(2,1)} %copy-done.12), channel_id=1, source_target_pairs={{0,8},{1,9},{2,10},{3,11},{4,12},{5,13},{6,14},{7,15},{8,0},{9,1},... | collective-permute-start | bytes 1179656 | tf_op jit(solution)/shard_map/ppermute | solution.py:386
  101.3 61.9 %collective-permute-start.19 = (bf16[24,64,128]{2,1,0:T(8,128)(2,1)}, bf16[24,64,128]{2,1,0:T(8,128)(2,1)}, u32[]{:S(2)}, u32[]{:S(2)}) collective-permute-start(bf16[24,64,128]{2,1,0:T(8,128)(2,1)} %copy-done.11), channel_id=1, source_target_pairs={{0,12},{1,13},{2,14},{3,15},{4,8},{5,9},{6,10},{7,11},{8,4},{9,5},... | collective-permute-start | bytes 1179656 | tf_op jit(solution)/shard_map/ppermute | solution.py:386
  103.8 62.4 %collective-permute-start.6 = (bf16[16,64,128]{2,1,0:T(8,128)(2,1)}, bf16[16,64,128]{2,1,0:T(8,128)(2,1)S(1)}, u32[]{:S(2)}, u32[]{:S(2)}) collective-permute-start(bf16[16,64,128]{2,1,0:T(8,128)(2,1)} %copy-done.23), channel_id=1, source_target_pairs={{0,4},{1,5},{2,6},{3,7},{4,0},{5,1},{6,2},{7,3},{8,12},{9,13},{10,... | collective-permute-start | bytes 786440 | tf_op jit(solution)/shard_map/ppermute | solution.py:386
  104.9 61.3 %collective-permute-start.7 = (bf16[16,64,128]{2,1,0:T(8,128)(2,1)}, bf16[16,64,128]{2,1,0:T(8,128)(2,1)S(1)}, u32[]{:S(2)}, u32[]{:S(2)}) collective-permute-start(bf16[16,64,128]{2,1,0:T(8,128)(2,1)} %copy-done.22), channel_id=1, source_target_pairs={{0,8},{1,9},{2,10},{3,11},{4,12},{5,13},{6,14},{7,15},{8,0},{9,1},... | collective-permute-start | bytes 786440 | tf_op jit(solution)/shard_map/ppermute | solution.py:386
  144.8 23.9 %collective-permute-start.8 = (bf16[16,64,128]{2,1,0:T(8,128)(2,1)S(1)}, bf16[16,64,128]{2,1,0:T(8,128)(2,1)S(1)}, u32[]{:S(2)}, u32[]{:S(2)}) collective-permute-start(bf16[16,64,128]{2,1,0:T(8,128)(2,1)S(1)} %copy-done.21), channel_id=1, source_target_pairs={{0,12},{1,13},{2,14},{3,15},{4,8},{5,9},{6,10},{7,11},{8,4},{9,5},... | collective-permute-start | bytes 786440 | tf_op jit(solution)/shard_map/ppermute | solution.py:386
  173.2 47.9 %collective-permute-start.27 = (bf16[32,64,256]{2,1,0:T(8,128)(2,1)}, bf16[32,64,256]{2,1,0:T(8,128)(2,1)S(1)}, u32[]{:S(2)}, u32[]{:S(2)}) collective-permute-start(bf16[32,64,256]{2,1,0:T(8,128)(2,1)} %get-tuple-element.92), channel_id=1, source_target_pairs={{0,1},{1,0},{2,3},{3,2},{4,5},{5,4},{6,7},{7,6},{8,9},{9,8},{10,11... | collective-permute-start | bytes 3145736 | tf_op jit(solution)/shard_map/ppermute | solution.py:386
  180.2 14.8 %collective-permute-start.21 = (bf16[16,64,256]{2,1,0:T(8,128)(2,1)S(1)}, bf16[16,64,256]{2,1,0:T(8,128)(2,1)S(1)}, u32[]{:S(2)}, u32[]{:S(2)}) collective-permute-start(bf16[16,64,256]{2,1,0:T(8,128)(2,1)S(1)} %get-tuple-element.99), channel_id=1, source_target_pairs={{0,2},{1,3},{2,0},{3,1},{4,6},{5,7},{6,4},{7,5},{8,10},{9,11},{10,... | collective-permute-start | bytes 1572872 | tf_op jit(solution)/shard_map/ppermute | solution.py:386
  182.2 38.9 %collective-permute-start.29 = (bf16[32,64,256]{2,1,0:T(8,128)(2,1)S(1)}, bf16[32,64,256]{2,1,0:T(8,128)(2,1)S(1)}, u32[]{:S(2)}, u32[]{:S(2)}) collective-permute-start(bf16[32,64,256]{2,1,0:T(8,128)(2,1)S(1)} %add_convert_fusion), channel_id=1, source_target_pairs={{0,2},{1,3},{2,0},{3,1},{4,6},{5,7},{6,4},{7,5},{8,10},{9,11},{10,... | collective-permute-start | bytes 3145736 | tf_op jit(solution)/shard_map/ppermute | solution.py:386
  182.8 17.0 %collective-permute-start.22 = (bf16[16,64,256]{2,1,0:T(8,128)(2,1)S(1)}, bf16[16,64,256]{2,1,0:T(8,128)(2,1)S(1)}, u32[]{:S(2)}, u32[]{:S(2)}) collective-permute-start(bf16[16,64,256]{2,1,0:T(8,128)(2,1)S(1)} %get-tuple-element.98), channel_id=1, source_target_pairs={{0,8},{1,9},{2,10},{3,11},{4,12},{5,13},{6,14},{7,15},{8,0},{9,1},... | collective-permute-start | bytes 1572872 | tf_op jit(solution)/shard_map/ppermute | solution.py:386
  200.0 23.0 %collective-permute-start.23 = (bf16[8,64,256]{2,1,0:T(8,128)(2,1)S(1)}, bf16[8,64,256]{2,1,0:T(8,128)(2,1)S(1)}, u32[]{:S(2)}, u32[]{:S(2)}) collective-permute-start(bf16[8,64,256]{2,1,0:T(8,128)(2,1)S(1)} %slice.130), channel_id=1, source_target_pairs={{0,8},{1,9},{2,10},{3,11},{4,12},{5,13},{6,14},{7,15},{8,0},{9,1},... | collective-permute-start | bytes 786440 | tf_op jit(solution)/shard_map/ppermute | solution.py:386
  202.7 24.2 %collective-permute-start.24 = (bf16[8,64,256]{2,1,0:T(8,128)(2,1)S(1)}, bf16[8,64,256]{2,1,0:T(8,128)(2,1)S(1)}, u32[]{:S(2)}, u32[]{:S(2)}) collective-permute-start(bf16[8,64,256]{2,1,0:T(8,128)(2,1)S(1)} %slice.129), channel_id=1, source_target_pairs={{0,4},{1,5},{2,6},{3,7},{4,0},{5,1},{6,2},{7,3},{8,12},{9,13},{10,... | collective-permute-start | bytes 786440 | tf_op jit(solution)/shard_map/ppermute | solution.py:386
  (32 other events, 291.8 us)

commit v2 on v0

--- a/solution.py
+++ b/solution.py
@@ -157,7 +157,14 @@
         rest = rest[7:]
     outs = rest[:3] if final else ()
     rest = rest[len(outs) :]
-    obs, pix, green_a, hats_a, green_b, hats_b, wide, sights, items, sems = rest
+    obs, pix = rest[:2]
+    buffers = rest[2 : 2 + 9 * PAIR]
+    wide, sights = rest[2 + 9 * PAIR : 2 + 10 * PAIR], rest[2 + 10 * PAIR : 2 + 11 * PAIR]
+    items, sems = rest[2 + 11 * PAIR :]
+    sets = [
+        [buffers[3 * (PAIR * i + lane) : 3 * (PAIR * i + lane) + 3] for lane in range(PAIR)]
+        for i in range(3)
+    ]
     epochs = obs.shape[1]
     base = groups[0][0]
     span = sum(size for _, _, size in groups)
@@ -199,10 +206,10 @@
         tile = info_of(slot, 1)
         return slot, [cutoffs[tile * NEAR + k] for k in range(NEAR)]
 
-    def spread(rows, sights):
+    def spread(rows, lane):
         columns = rows.T
         for i in range(2):
-            wide[i] = jnp.broadcast_to(columns[:, i : i + 1], (CHUNK, CHUNK))
+            wide[lane][i] = jnp.broadcast_to(columns[:, i : i + 1], (CHUNK, CHUNK))
         le, ln = rows[4:5], rows[5:6]
         along = le * (rows[0:1] - origin[0]) + ln * (rows[1:2] - origin[1])
         row = lax.broadcasted_iota(jnp.int32, (8, CHUNK), 0)
@@ -216,20 +223,21 @@
             upper = jnp.concatenate([parts[second_part[0]][:4]] * 2, axis=0)
             tiles.append(jnp.where(low, parts[first_part[0]], upper))
         tiles.append(jnp.zeros((8, CHUNK), jnp.float32))
-        sights[...] = jnp.concatenate(tiles, axis=0).T.astype(jnp.bfloat16)
-
-    def make_strips(near, k, lows, sights, green):
+        sights[lane][...] = jnp.concatenate(tiles, axis=0).T.astype(jnp.bfloat16)
+
+    def make_strips(near, k, begin, end, lane, green):
         patch = [
             jnp.broadcast_to(patches[near[k], r : r + 1], (8, PBLK)) for r in range(3)
         ]
-        begin, end = lows[0], lows[-1] + 16
-        alongs = jnp.dot(sights[begin:end], forms[near[k]], preferred_element_type=jnp.float32)
-        for low in lows:
+        alongs = jnp.dot(
+            sights[lane][begin:end], forms[near[k]], preferred_element_type=jnp.float32
+        )
+        for low in range(begin, end, 16):
             along = alongs[low - begin : low - begin + 16]
             inverses = []
             for at in (low, low + 8):
                 east, north = (
-                    jnp.concatenate([wide[i, at : at + 8]] * (PBLK // CHUNK), axis=1)
+                    jnp.concatenate([wide[lane][i, at : at + 8]] * (PBLK // CHUNK), axis=1)
                     for i in range(2)
                 )
                 dx = east - patch[0]
@@ -247,25 +255,19 @@
         for a in range(SG):
             hats[a * SG : (a + 1) * SG] = (across[a : a + 1] * upward).astype(jnp.bfloat16)
 
-    def make_all(i, green, hats):
+    def make_head(i, lane, buffers):
         slot, near = item_of(i)
         rows = pix[slot]
-        make_hats(rows, hats)
-        spread(rows, sights)
-        for k in range(NEAR):
-            for low in (0, CHUNK // 2):
-                make_strips(near, k, range(low, low + CHUNK // 2, 16), sights, green)
-
-    def turn(i, green, hats, green_next, hats_next):
+        make_hats(rows, buffers[1])
+        spread(rows, lane)
+        return near
+
+    def predict(i, buffers):
+        green, hats = buffers[:2]
         slot, near = item_of(i)
-        slot_next, near_next = item_of(i + 1)
-        rows = pix[slot_next]
-        screen = info_of(slot, 2)
-
-        def fill(k, low, high):
-            make_strips(near_next, k, range(low, high, 16), sights, green_next)
-
-        model = jnp.dot(screens[screen], hats[...], preferred_element_type=jnp.float32)
+        model = jnp.dot(
+            screens[info_of(slot, 2)], hats[...], preferred_element_type=jnp.float32
+        )
         for k in range(NEAR):
             model += lax.dot_general(
                 stress[pl.ds(pl.multiple_of(spots[near[k]], 16), epochs), :],
@@ -273,43 +275,93 @@
                 (((1,), (1,)), ((), ())),
                 preferred_element_type=jnp.float32,
             )
-        make_hats(rows, hats_next)
-        spread(rows, sights)
-        fill(0, 0, CHUNK // 2)
-        fill(0, CHUNK // 2, CHUNK)
+        return model
+
+    def weigh(i, model, buffers):
+        slot, _ = item_of(i)
         live = jnp.where(i < total, info_of(slot, 0), 0)
         lane = lax.broadcasted_iota(jnp.int32, (1, CHUNK), 1)
         scale = jnp.where(lane < live, pix[slot, 7:8, :], 0.0)
-        weighted = ((model - obs[slot].astype(jnp.float32)) * scale).astype(jnp.bfloat16)
-
-        def add(k):
-            grad[places[near[k]]] += jnp.dot(
-                weighted,
-                green[:, k * PBLK : (k + 1) * PBLK],
-                preferred_element_type=jnp.float32,
-            )
-
-        add(0)
-        fill(1, 0, CHUNK // 2)
-        add(1)
-        fill(1, CHUNK // 2, CHUNK)
-        add(2)
-        fill(2, 0, CHUNK // 2)
-        screen_grad[screen] += lax.dot_general(
-            weighted, hats[...], (((1,), (1,)), ((), ())), preferred_element_type=jnp.float32
+        buffers[2][...] = ((model - obs[slot].astype(jnp.float32)) * scale).astype(jnp.bfloat16)
+
+    def add_patch(near, k, buffers):
+        grad[places[near[k]]] += jnp.dot(
+            buffers[2][...],
+            buffers[0][:, k * PBLK : (k + 1) * PBLK],
+            preferred_element_type=jnp.float32,
         )
-        fill(2, CHUNK // 2, CHUNK)
+
+    def add_screen(slot, buffers):
+        screen_grad[info_of(slot, 2)] += lax.dot_general(
+            buffers[2][...],
+            buffers[1][...],
+            (((1,), (1,)), ((), ())),
+            preferred_element_type=jnp.float32,
+        )
+
+    lanes = range(PAIR)
+    half = CHUNK // 2
+
+    def make_pair(j, buffers):
+        for lane in lanes:
+            near = make_head(PAIR * j + lane, lane, buffers[lane])
+            for k in range(NEAR):
+                for low in (0, half):
+                    make_strips(near, k, low, low + half, lane, buffers[lane][0])
+
+    def model_pair(j, buffers):
+        for lane in lanes:
+            model = predict(PAIR * j + lane, buffers[lane])
+            weigh(PAIR * j + lane, model, buffers[lane])
+
+    def turn(j, using, middle, making):
+        now = [item_of(PAIR * j + lane) for lane in lanes]
+        coming = [PAIR * (j + 1) + lane for lane in lanes]
+        near = [
+            make_head(PAIR * (j + 2) + lane, lane, making[lane]) for lane in lanes
+        ]
+        models = [predict(coming[lane], middle[lane]) for lane in lanes]
+
+        def strips(k, lane):
+            for low in (0, half):
+                make_strips(near[lane], k, low, low + half, lane, making[lane][0])
+
+        def adds(k):
+            for lane in lanes:
+                add_patch(now[lane][1], k, using[lane])
+
+        strips(0, 0)
+        adds(0)
+        strips(0, 1)
+        adds(1)
+        strips(1, 0)
+        for lane in lanes:
+            weigh(coming[lane], models[lane], middle[lane])
+        strips(1, 1)
+        adds(2)
+        strips(2, 0)
+        for lane in lanes:
+            add_screen(now[lane][0], using[lane])
+        strips(2, 1)
 
     @pl.when(total > 0)
     def _():
-        make_all(0, green_a, hats_a)
-
-        def step(j, _):
-            turn(2 * j, green_a, hats_a, green_b, hats_b)
-            turn(2 * j + 1, green_b, hats_b, green_a, hats_a)
+        pairs = lax.div(total + PAIR - 1, PAIR)
+        make_pair(0, sets[0])
+        make_pair(1, sets[1])
+        model_pair(0, sets[0])
+
+        def step(i, _):
+            for at in range(3):
+                j = 3 * i + at
+
+                @pl.when(j < pairs)
+                def _():
+                    turn(j, sets[at], sets[(at + 1) % 3], sets[(at + 2) % 3])
+
             return 0
 
-        lax.fori_loop(0, lax.div(total + 1, 2), step, 0)
+        lax.fori_loop(0, lax.div(pairs + 2, 3), step, 0)
 
     if final:
         half = grad.shape[0] // 2
@@ -358,11 +410,12 @@
         + [
             pltpu.VMEM((CHUNK, NEAR * PBLK), jnp.bfloat16),
             pltpu.VMEM((SG * SG, CHUNK), jnp.bfloat16),
+            pltpu.VMEM((epochs, CHUNK), jnp.bfloat16),
         ]
-        * 2
+        * (3 * PAIR)
+        + [pltpu.VMEM((2, CHUNK, CHUNK), jnp.float32)] * PAIR
+        + [pltpu.VMEM((CHUNK, TERMS), jnp.bfloat16)] * PAIR
         + [
-            pltpu.VMEM((2, CHUNK, CHUNK), jnp.float32),
-            pltpu.VMEM((CHUNK, TERMS), jnp.bfloat16),
             pltpu.SMEM((layers * span + 1,), jnp.int32),
             pltpu.SemaphoreType.DMA((2 * layers * len(groups) + 2 * LAYER,)),
         ],
@@ -413,7 +466,7 @@
     parts = [total[:middle], total[middle:]]
     both = orders(devices)
     stages = len(both[0])
-    back = None
+    back = partner(there, devices, PAIR)
     for stage in range(stages):
         got = []
         for side in range(2):
@@ -426,9 +479,6 @@
                 parts[0], got[1] = lax.optimization_barrier((parts[0], got[1]))
             size = parts[side].shape[0] // 2
             parts[side] = parts[side][:size] + got[side].astype(jnp.float32)
-            if back is None:
-                parts[0], there = lax.optimization_barrier((parts[0], there))
-                back = partner(there, devices, PAIR)
     return jnp.concatenate(parts, axis=0), back
 
 

time: 246 us -> 222 us (0.902)
  the two profiles are of different devices: /device:TPU:26 before, /device:TPU:0 now
where the time goes in v2:
time: 222 us; the launch traced here: 226 us
  starting transfers between devices  73.4 us (33%)
  waiting for transfers between devices  72.3 us (33%)
  Pallas kernels  45.8 us (21%)
  local copies, waits for them, and re-layouts  23.3 us (10%)
  other arithmetic  10 us (5%)
    ppermute x30, starting transfers between devices, partner(): lax.ppermute(values, 'tile', [(i, i ^ distance) for i in range(devices)])  73.4 us
    ppermute x30, waiting for transfers between devices, partner(): lax.ppermute(values, 'tile', [(i, i ^ distance) for i in range(devices)])  72.3 us
    pallas_call x3, Pallas kernels, fit(): pl.pallas_call(functools.partial(fit_kernel, first, final, layers, slots,...  40.8 us
    unnamed x53, local copies, waits for them, and re-layouts  12.6 us
    pallas_call x1, Pallas kernels, pack(): pl.pallas_call(functools.partial(pack_kernel, local_tiles, layers, slots)...  5.04 us
    concatenate x1, local copies, waits for them, and re-layouts, on_device(): jnp.concatenate([faces[second] for _, second in CROSS] + [jnp.zeros((8,)...  4.73 us
  transfers between devices with their start and end apart: 30, of which 14 were waited for; matrix products, arithmetic and copies ran while one was open for 8% of the time, Pallas kernels for 19%

profile of v2, /device:TPU:0, one launch (start us, length us, event | category | flops | bytes accessed | tf_op | source)
XLA Modules:
  0.0 226.0 jit_solution(8632172553614923212)
XLA Ops:
  1.7 4.1 %collective-permute-start = (bf16[512,256]{1,0:T(8,128)(2,1)S(1)}, bf16[512,256]{1,0:T(8,128)(2,1)S(1)}, u32[]{:S(2)}, u32[]{:S(2)}) collective-permute-start(bf16[512,256]{1,0:T(8,128)(2,1)S(1)} %bitcast.26), channel_id=1, source_target_pairs={{0,8},{1,9},{2,10},{3,11},{4,12},{5,13},{6,14},{7,15},{8,0},{9,1},... | collective-permute-start | bytes 786440 | tf_op jit(solution)/shard_map/ppermute | solution.py:434
  11.2 5.0 %pack.1 = (bf16[24,64,128]{2,1,0:T(8,128)(2,1)S(1)}, bf16[24,64,128]{2,1,0:T(8,128)(2,1)S(1)}, bf16[24,64,128]{2,1,0:T(8,128)(2,1)S(1)}, bf16[24,64,128]{2,1,0:T...) custom-call(s32[1]{0:T(128)} %bitcast.3.here, ...), custom_call_target="tpu_custom_call" | custom-call | tf_op jit(solution)/shard_map/pack/pallas_call | solution.py:96
  22.0 3.4 %collective-permute-start.4 = (f32[65,8,128]{2,1,0:T(8,128)S(1)}, f32[65,8,128]{2,1,0:T(8,128)}, u32[]{:S(2)}, u32[]{:S(2)}) collective-permute-start(f32[65,8,128]{2,1,0:T(8,128)S(1)} %get-tuple-element.56), channel_id=1, source_target_pairs={{0,12},{1,13},{2,14},{3,15},{4,8},{5,9},{6,10},{7,11},{8,4},{9,5},... | collective-permute-start | bytes 798728 | tf_op jit(solution)/shard_map/ppermute | solution.py:434
  26.0 14.1 %collective-permute-done.1 = bf16[1024,256]{1,0:T(8,128)(2,1)S(1)} collective-permute-done((bf16[1024,256]{1,0:T(8,128)(2,1)S(1)}, bf16[1024,256]{1,0:T(8,128)(2,1)S(1)}, u32[]{:S(2)}, u32[]{:S(2)}) %collective-permute-start.1) | collective-permute-done | bytes 524320 | tf_op jit(solution)/shard_map/ppermute | solution.py:434
  41.1 2.9 %collective-permute-done.2.refs_10_ = f32[65,8,128]{2,1,0:T(8,128)S(1)} collective-permute-done((f32[65,8,128]{2,1,0:T(8,128)S(1)}, f32[65,8,128]{2,1,0:T(8,128)S(1)}, u32[]{:S(2)}, u32[]{:S(2)}) %collective-permute-start.2) | collective-permute-done | bytes 266272 | tf_op jit(solution)/shard_map/ppermute | solution.py:434
  44.9 3.4 %collective-permute-start.11 = (bf16[24,64,128]{2,1,0:T(8,128)(2,1)S(1)}, bf16[24,64,128]{2,1,0:T(8,128)(2,1)S(1)}, u32[]{:S(2)}, u32[]{:S(2)}) collective-permute-start(bf16[24,64,128]{2,1,0:T(8,128)(2,1)S(1)} %get-tuple-element.69), channel_id=1, source_target_pairs={{0,8},{1,9},{2,10},{3,11},{4,12},{5,13},{6,14},{7,15},{8,0},{9,1},... | collective-permute-start | bytes 1179656 | tf_op jit(solution)/shard_map/ppermute | solution.py:434
  48.2 3.2 %collective-permute-done.4.refs_12_ = f32[65,8,128]{2,1,0:T(8,128)} collective-permute-done((f32[65,8,128]{2,1,0:T(8,128)S(1)}, f32[65,8,128]{2,1,0:T(8,128)}, u32[]{:S(2)}, u32[]{:S(2)}) %collective-permute-start.4) | collective-permute-done | bytes 266272 | tf_op jit(solution)/shard_map/ppermute | solution.py:434
  51.4 7.2 %collective-permute-start.9 = (bf16[2048,256]{1,0:T(8,128)(2,1)}, bf16[2048,256]{1,0:T(8,128)(2,1)}, u32[]{:S(2)}, u32[]{:S(2)}) collective-permute-start(bf16[2048,256]{1,0:T(8,128)(2,1)} %pad_maximum_fusion.refs_19_), channel_id=1, source_target_pairs={{0,2},{1,3},{2,0},{3,1},{4,6},{5,7},{6,4},{7,5},{8,10},{9,11},{10,... | collective-permute-start | bytes 3145736 | tf_op jit(solution)/shard_map/ppermute | solution.py:434
  59.7 7.4 %collective-permute-done.10.refs_6_ = bf16[24,64,128]{2,1,0:T(8,128)(2,1)S(1)} collective-permute-done((bf16[24,64,128]{2,1,0:T(8,128)(2,1)S(1)}, bf16[24,64,128]{2,1,0:T(8,128)(2,1)S(1)}, u32[]{:S(2)}, u32[]{:S(2)}) %collective-permute-start.10) | collective-permute-done | bytes 393248 | tf_op jit(solution)/shard_map/ppermute | solution.py:434
  67.9 7.7 %collective-permute-done.9.refs_20_ = bf16[2048,256]{1,0:T(8,128)(2,1)} collective-permute-done((bf16[2048,256]{1,0:T(8,128)(2,1)}, bf16[2048,256]{1,0:T(8,128)(2,1)}, u32[]{:S(2)}, u32[]{:S(2)}) %collective-permute-start.9) | collective-permute-done | bytes 1048608 | tf_op jit(solution)/shard_map/ppermute | solution.py:434
  82.8 4.7 %concatenate.21 = bf16[32,128,256]{2,0,1:T(8,128)(2,1)S(1)} concatenate(bf16[4,128,256]{2,0,1:T(4,128)(2,1)S(1)} %get-tuple-element.104, bf16[4,128,256]{2,0,1:T(4,128)(2,1)S(1)} %get-tuple-element.103, bf16[4,128,256]{2,0,1:T(4,128)(2,1)S(1)} %get-tuple-element.104, bf16[4,128,256]{2,0,1:T(4,128)(2,1)} %get-tuple-element.102, bf16[4,128,256]{2,0,1:T(4,128)(2,1)S(1)} %get-tuple-element.103, ...), dimensions={0} | concatenate | bytes 4194304 | tf_op jit(solution)/shard_map/concatenate | solution.py:555
  91.8 3.2 %collective-permute-start.17 = (bf16[24,64,128]{2,1,0:T(8,128)(2,1)}, bf16[24,64,128]{2,1,0:T(8,128)(2,1)}, u32[]{:S(2)}, u32[]{:S(2)}) collective-permute-start(bf16[24,64,128]{2,1,0:T(8,128)(2,1)} %copy-done.13), channel_id=1, source_target_pairs={{0,4},{1,5},{2,6},{3,7},{4,0},{5,1},{6,2},{7,3},{8,12},{9,13},{10,... | collective-permute-start | bytes 1179656 | tf_op jit(solution)/shard_map/ppermute | solution.py:434
  103.5 33.9 %fit.3 = (f32[128,64,256]{2,1,0:T(8,128)S(1)}, f32[128,64,256]{2,1,0:T(8,128)S(1)}, bf16[128,64,256]{2,1,0:T(8,128)(2,1)S(1)}, bf16[8192,256]{1,0:T(8,128)(2,1)S(1)}) custom-call(s32[768]{0:T(1024)S(1)} %convert_element_type.49.refs_0_, s32[1536]{0:T(1024)S(1)} %reshape.52.refs_1_, s32[128]{0:T(128)S(1)} %get-tuple-element.108.refs_2_, ...), custom_call_target="tpu_custom_call" | custom-call | flops 3221225472 | bytes 20971520 | tf_op jit(solution)/shard_map/fit/pallas_call | solution.py:397
  137.6 2.9 %fit.4 = (f32[128,64,256]{2,1,0:T(8,128)S(1)}, f32[128,64,256]{2,1,0:T(8,128)S(1)}) custom-call(s32[768]{0:T(1024)S(1)} %convert_element_type.49.refs_0_, s32[1536]{0:T(1024)S(1)} %reshape.52.refs_1_, s32[128]{0:T(128)S(1)} %get-tuple-element.108.refs_2_, s32[128]{0:T(128)S(1)} %get-tuple-element.109.refs_3_, ...), custom_call_target="tpu_custom_call", output_to_operand_aliasing={{0}: (17, {}), {1}: (18, {})} | custom-call | flops 3221225472 | bytes 20971520 | tf_op jit(solution)/shard_map/fit/pallas_call | solution.py:397
  140.5 9.9 %collective-permute-done.7.refs_7_ = bf16[16,64,128]{2,1,0:T(8,128)(2,1)S(1)} collective-permute-done((bf16[16,64,128]{2,1,0:T(8,128)(2,1)}, bf16[16,64,128]{2,1,0:T(8,128)(2,1)S(1)}, u32[]{:S(2)}, u32[]{:S(2)}) %collective-permute-start.7) | collective-permute-done | bytes 262176 | tf_op jit(solution)/shard_map/ppermute | solution.py:434
  150.4 4.0 %fit.5 = (f32[128,64,256]{2,1,0:T(8,128)S(1)}, f32[128,64,256]{2,1,0:T(8,128)S(1)}, bf16[64,64,256]{2,1,0:T(8,128)(2,1)S(1)}, bf16[32,64,256]{2,1,0:T(8,128)(2,1)}, bf16[32,64,256]{2,1,0:T(8,128)(2,1)}) custom-call(s32[768]{0:T(1024)S(1)} %convert_element_type.49.refs_0_, s32[1536]{0:T(1024)S(1)} %reshape.52.refs_1_, ...), custom_call_target="tpu_custom_call", output_to_operand_aliasing={{0}: (17, {}), {1}: (18, {})} | custom-call | flops 2147483648 | bytes 20971520 | tf_op jit(solution)/shard_map/fit/pallas_call | solution.py:397
  155.0 5.8 %collective-permute-done.20 = bf16[64,64,256]{2,1,0:T(8,128)(2,1)S(1)} collective-permute-done((bf16[64,64,256]{2,1,0:T(8,128)(2,1)S(1)}, bf16[64,64,256]{2,1,0:T(8,128)(2,1)S(1)}, u32[]{:S(2)}, u32[]{:S(2)}) %collective-permute-start.20) | collective-permute-done | bytes 2097184 | tf_op jit(solution)/shard_map/ppermute | solution.py:434
  164.5 4.6 %collective-permute-start.22 = (bf16[16,64,256]{2,1,0:T(8,128)(2,1)S(1)}, bf16[16,64,256]{2,1,0:T(8,128)(2,1)S(1)}, u32[]{:S(2)}, u32[]{:S(2)}) collective-permute-start(bf16[16,64,256]{2,1,0:T(8,128)(2,1)S(1)} %get-tuple-element.98), channel_id=1, source_target_pairs={{0,8},{1,9},{2,10},{3,11},{4,12},{5,13},{6,14},{7,15},{8,0},{9,1},... | collective-permute-start | bytes 1572872 | tf_op jit(solution)/shard_map/ppermute | solution.py:434
  169.1 7.7 %collective-permute-done.21 = bf16[16,64,256]{2,1,0:T(8,128)(2,1)S(1)} collective-permute-done((bf16[16,64,256]{2,1,0:T(8,128)(2,1)S(1)}, bf16[16,64,256]{2,1,0:T(8,128)(2,1)S(1)}, u32[]{:S(2)}, u32[]{:S(2)}) %collective-permute-start.21) | collective-permute-done | bytes 524320 | tf_op jit(solution)/shard_map/ppermute | solution.py:434
  176.9 3.9 %collective-permute-done.22 = bf16[16,64,256]{2,1,0:T(8,128)(2,1)S(1)} collective-permute-done((bf16[16,64,256]{2,1,0:T(8,128)(2,1)S(1)}, bf16[16,64,256]{2,1,0:T(8,128)(2,1)S(1)}, u32[]{:S(2)}, u32[]{:S(2)}) %collective-permute-start.22) | collective-permute-done | bytes 524320 | tf_op jit(solution)/shard_map/ppermute | solution.py:434
  181.1 2.7 %collective-permute-start.23 = (bf16[8,64,256]{2,1,0:T(8,128)(2,1)S(1)}, bf16[8,64,256]{2,1,0:T(8,128)(2,1)S(1)}, u32[]{:S(2)}, u32[]{:S(2)}) collective-permute-start(bf16[8,64,256]{2,1,0:T(8,128)(2,1)S(1)} %slice.130), channel_id=1, source_target_pairs={{0,8},{1,9},{2,10},{3,11},{4,12},{5,13},{6,14},{7,15},{8,0},{9,1},... | collective-permute-start | bytes 786440 | tf_op jit(solution)/shard_map/ppermute | solution.py:434
  183.8 20.8 %collective-permute-start.24 = (bf16[8,64,256]{2,1,0:T(8,128)(2,1)S(1)}, bf16[8,64,256]{2,1,0:T(8,128)(2,1)S(1)}, u32[]{:S(2)}, u32[]{:S(2)}) collective-permute-start(bf16[8,64,256]{2,1,0:T(8,128)(2,1)S(1)} %slice.129), channel_id=1, source_target_pairs={{0,4},{1,5},{2,6},{3,7},{4,0},{5,1},{6,2},{7,3},{8,12},{9,13},{10,... | collective-permute-start | bytes 786440 | tf_op jit(solution)/shard_map/ppermute | solution.py:434
  206.4 4.2 %collective-permute-done.24 = bf16[8,64,256]{2,1,0:T(8,128)(2,1)S(1)} collective-permute-done((bf16[8,64,256]{2,1,0:T(8,128)(2,1)S(1)}, bf16[8,64,256]{2,1,0:T(8,128)(2,1)S(1)}, u32[]{:S(2)}, u32[]{:S(2)}) %collective-permute-start.24) | collective-permute-done | bytes 262176 | tf_op jit(solution)/shard_map/ppermute | solution.py:434
  210.7 9.3 %collective-permute-start.25 = (bf16[4,64,256]{2,1,0:T(8,128)(2,1)S(1)}, bf16[4,64,256]{2,1,0:T(8,128)(2,1)S(1)}, u32[]{:S(2)}, u32[]{:S(2)}) collective-permute-start(bf16[4,64,256]{2,1,0:T(8,128)(2,1)S(1)} %slice.132), channel_id=1, source_target_pairs={{0,4},{1,5},{2,6},{3,7},{4,0},{5,1},{6,2},{7,3},{8,12},{9,13},{10,... | collective-permute-start | bytes 393224 | tf_op jit(solution)/shard_map/ppermute | solution.py:434
  (129 shorter events, 48.9 us)
Async XLA Ops:
  1.7 17.7 %collective-permute-start = (bf16[512,256]{1,0:T(8,128)(2,1)S(1)}, bf16[512,256]{1,0:T(8,128)(2,1)S(1)}, u32[]{:S(2)}, u32[]{:S(2)}) collective-permute-start(bf16[512,256]{1,0:T(8,128)(2,1)S(1)} %bitcast.26), channel_id=1, source_target_pairs={{0,8},{1,9},{2,10},{3,11},{4,12},{5,13},{6,14},{7,15},{8,0},{9,1},... | collective-permute-start | bytes 786440 | tf_op jit(solution)/shard_map/ppermute | solution.py:434
  5.8 45.7 %collective-permute-start.5 = (bf16[32,64,256]{2,1,0:T(8,128)(2,1)}, bf16[32,64,256]{2,1,0:T(8,128)(2,1)}, u32[]{:S(2)}, u32[]{:S(2)}) collective-permute-start(bf16[32,64,256]{2,1,0:T(8,128)(2,1)} %refs_15_.1), channel_id=1, source_target_pairs={{0,2},{1,3},{2,0},{3,1},{4,6},{5,7},{6,4},{7,5},{8,10},{9,11},{10,... | collective-permute-start | bytes 3145736 | tf_op jit(solution)/shard_map/ppermute | solution.py:434
  19.4 20.6 %collective-permute-start.1 = (bf16[1024,256]{1,0:T(8,128)(2,1)S(1)}, bf16[1024,256]{1,0:T(8,128)(2,1)S(1)}, u32[]{:S(2)}, u32[]{:S(2)}) collective-permute-start(bf16[1024,256]{1,0:T(8,128)(2,1)S(1)} %pad_maximum_fusion.1), channel_id=1, source_target_pairs={{0,4},{1,5},{2,6},{3,7},{4,0},{5,1},{6,2},{7,3},{8,12},{9,13},{10,... | collective-permute-start | bytes 1572872 | tf_op jit(solution)/shard_map/ppermute | solution.py:434
  21.1 22.9 %collective-permute-start.2 = (f32[65,8,128]{2,1,0:T(8,128)S(1)}, f32[65,8,128]{2,1,0:T(8,128)S(1)}, u32[]{:S(2)}, u32[]{:S(2)}) collective-permute-start(f32[65,8,128]{2,1,0:T(8,128)S(1)} %get-tuple-element.54), channel_id=1, source_target_pairs={{0,4},{1,5},{2,6},{3,7},{4,0},{5,1},{6,2},{7,3},{8,12},{9,13},{10,... | collective-permute-start | bytes 798728 | tf_op jit(solution)/shard_map/ppermute | solution.py:434
  21.7 23.2 %collective-permute-start.3 = (f32[65,8,128]{2,1,0:T(8,128)S(1)}, f32[65,8,128]{2,1,0:T(8,128)S(1)}, u32[]{:S(2)}, u32[]{:S(2)}) collective-permute-start(f32[65,8,128]{2,1,0:T(8,128)S(1)} %get-tuple-element.55), channel_id=1, source_target_pairs={{0,8},{1,9},{2,10},{3,11},{4,12},{5,13},{6,14},{7,15},{8,0},{9,1},... | collective-permute-start | bytes 798728 | tf_op jit(solution)/shard_map/ppermute | solution.py:434
  22.0 29.4 %collective-permute-start.4 = (f32[65,8,128]{2,1,0:T(8,128)S(1)}, f32[65,8,128]{2,1,0:T(8,128)}, u32[]{:S(2)}, u32[]{:S(2)}) collective-permute-start(f32[65,8,128]{2,1,0:T(8,128)S(1)} %get-tuple-element.56), channel_id=1, source_target_pairs={{0,12},{1,13},{2,14},{3,15},{4,8},{5,9},{6,10},{7,11},{8,4},{9,5},... | collective-permute-start | bytes 798728 | tf_op jit(solution)/shard_map/ppermute | solution.py:434
  40.1 55.0 %collective-permute-start.13 = (bf16[32,64,256]{2,1,0:T(8,128)(2,1)}, bf16[32,64,256]{2,1,0:T(8,128)(2,1)}, u32[]{:S(2)}, u32[]{:S(2)}) collective-permute-start(bf16[32,64,256]{2,1,0:T(8,128)(2,1)} %refs_15_.1), channel_id=1, source_target_pairs={{0,1},{1,0},{2,3},{3,2},{4,5},{5,4},{6,7},{7,6},{8,9},{9,8},{10,11... | collective-permute-start | bytes 3145736 | tf_op jit(solution)/shard_map/ppermute | solution.py:434
  44.0 23.1 %collective-permute-start.10 = (bf16[24,64,128]{2,1,0:T(8,128)(2,1)S(1)}, bf16[24,64,128]{2,1,0:T(8,128)(2,1)S(1)}, u32[]{:S(2)}, u32[]{:S(2)}) collective-permute-start(bf16[24,64,128]{2,1,0:T(8,128)(2,1)S(1)} %get-tuple-element.67), channel_id=1, source_target_pairs={{0,4},{1,5},{2,6},{3,7},{4,0},{5,1},{6,2},{7,3},{8,12},{9,13},{10,... | collective-permute-start | bytes 1179656 | tf_op jit(solution)/shard_map/ppermute | solution.py:434
  44.9 32.4 %collective-permute-start.11 = (bf16[24,64,128]{2,1,0:T(8,128)(2,1)S(1)}, bf16[24,64,128]{2,1,0:T(8,128)(2,1)S(1)}, u32[]{:S(2)}, u32[]{:S(2)}) collective-permute-start(bf16[24,64,128]{2,1,0:T(8,128)(2,1)S(1)} %get-tuple-element.69), channel_id=1, source_target_pairs={{0,8},{1,9},{2,10},{3,11},{4,12},{5,13},{6,14},{7,15},{8,0},{9,1},... | collective-permute-start | bytes 1179656 | tf_op jit(solution)/shard_map/ppermute | solution.py:434
  51.4 24.2 %collective-permute-start.9 = (bf16[2048,256]{1,0:T(8,128)(2,1)}, bf16[2048,256]{1,0:T(8,128)(2,1)}, u32[]{:S(2)}, u32[]{:S(2)}) collective-permute-start(bf16[2048,256]{1,0:T(8,128)(2,1)} %pad_maximum_fusion.refs_19_), channel_id=1, source_target_pairs={{0,2},{1,3},{2,0},{3,1},{4,6},{5,7},{6,4},{7,5},{8,10},{9,11},{10,... | collective-permute-start | bytes 3145736 | tf_op jit(solution)/shard_map/ppermute | solution.py:434
  59.6 37.9 %collective-permute-start.15 = (bf16[2048,256]{1,0:T(8,128)(2,1)}, bf16[2048,256]{1,0:T(8,128)(2,1)}, u32[]{:S(2)}, u32[]{:S(2)}) collective-permute-start(bf16[2048,256]{1,0:T(8,128)(2,1)} %pad_maximum_fusion.refs_19_), channel_id=1, source_target_pairs={{0,1},{1,0},{2,3},{3,2},{4,5},{5,4},{6,7},{7,6},{8,9},{9,8},{10,11... | collective-permute-start | bytes 3145736 | tf_op jit(solution)/shard_map/ppermute | solution.py:434
  67.9 27.1 %collective-permute-start.14 = (bf16[32,64,256]{2,1,0:T(8,128)(2,1)}, bf16[32,64,256]{2,1,0:T(8,128)(2,1)}, u32[]{:S(2)}, u32[]{:S(2)}) collective-permute-start(bf16[32,64,256]{2,1,0:T(8,128)(2,1)} %collective-permute-done.5.refs_16_), channel_id=1, source_target_pairs={{0,1},{1,0},{2,3},{3,2},{4,5},{5,4},{6,7},{7,6},{8,9},{9,8},{10,11... | collective-permute-start | bytes 3145736 | tf_op jit(solution)/shard_map/ppermute | solution.py:434
  75.6 23.0 %collective-permute-start.16 = (bf16[2048,256]{1,0:T(8,128)(2,1)}, bf16[2048,256]{1,0:T(8,128)(2,1)}, u32[]{:S(2)}, u32[]{:S(2)}) collective-permute-start(bf16[2048,256]{1,0:T(8,128)(2,1)} %collective-permute-done.9.refs_20_), channel_id=1, source_target_pairs={{0,1},{1,0},{2,3},{3,2},{4,5},{5,4},{6,7},{7,6},{8,9},{9,8},{10,11... | collective-permute-start | bytes 3145736 | tf_op jit(solution)/shard_map/ppermute | solution.py:434
  91.8 45.6 %collective-permute-start.17 = (bf16[24,64,128]{2,1,0:T(8,128)(2,1)}, bf16[24,64,128]{2,1,0:T(8,128)(2,1)}, u32[]{:S(2)}, u32[]{:S(2)}) collective-permute-start(bf16[24,64,128]{2,1,0:T(8,128)(2,1)} %copy-done.13), channel_id=1, source_target_pairs={{0,4},{1,5},{2,6},{3,7},{4,0},{5,1},{6,2},{7,3},{8,12},{9,13},{10,... | collective-permute-start | bytes 1179656 | tf_op jit(solution)/shard_map/ppermute | solution.py:434
  95.0 42.5 %collective-permute-start.18 = (bf16[24,64,128]{2,1,0:T(8,128)(2,1)}, bf16[24,64,128]{2,1,0:T(8,128)(2,1)}, u32[]{:S(2)}, u32[]{:S(2)}) collective-permute-start(bf16[24,64,128]{2,1,0:T(8,128)(2,1)} %copy-done.12), channel_id=1, source_target_pairs={{0,8},{1,9},{2,10},{3,11},{4,12},{5,13},{6,14},{7,15},{8,0},{9,1},... | collective-permute-start | bytes 1179656 | tf_op jit(solution)/shard_map/ppermute | solution.py:434
  95.1 42.5 %collective-permute-start.19 = (bf16[24,64,128]{2,1,0:T(8,128)(2,1)}, bf16[24,64,128]{2,1,0:T(8,128)(2,1)}, u32[]{:S(2)}, u32[]{:S(2)}) collective-permute-start(bf16[24,64,128]{2,1,0:T(8,128)(2,1)} %copy-done.11), channel_id=1, source_target_pairs={{0,12},{1,13},{2,14},{3,15},{4,8},{5,9},{6,10},{7,11},{8,4},{9,5},... | collective-permute-start | bytes 1179656 | tf_op jit(solution)/shard_map/ppermute | solution.py:434
  97.5 43.0 %collective-permute-start.6 = (bf16[16,64,128]{2,1,0:T(8,128)(2,1)}, bf16[16,64,128]{2,1,0:T(8,128)(2,1)S(1)}, u32[]{:S(2)}, u32[]{:S(2)}) collective-permute-start(bf16[16,64,128]{2,1,0:T(8,128)(2,1)} %copy-done.23), channel_id=1, source_target_pairs={{0,4},{1,5},{2,6},{3,7},{4,0},{5,1},{6,2},{7,3},{8,12},{9,13},{10,... | collective-permute-start | bytes 786440 | tf_op jit(solution)/shard_map/ppermute | solution.py:434
  98.6 51.7 %collective-permute-start.7 = (bf16[16,64,128]{2,1,0:T(8,128)(2,1)}, bf16[16,64,128]{2,1,0:T(8,128)(2,1)S(1)}, u32[]{:S(2)}, u32[]{:S(2)}) collective-permute-start(bf16[16,64,128]{2,1,0:T(8,128)(2,1)} %copy-done.22), channel_id=1, source_target_pairs={{0,8},{1,9},{2,10},{3,11},{4,12},{5,13},{6,14},{7,15},{8,0},{9,1},... | collective-permute-start | bytes 786440 | tf_op jit(solution)/shard_map/ppermute | solution.py:434
  154.9 49.6 %collective-permute-start.27 = (bf16[32,64,256]{2,1,0:T(8,128)(2,1)}, bf16[32,64,256]{2,1,0:T(8,128)(2,1)S(1)}, u32[]{:S(2)}, u32[]{:S(2)}) collective-permute-start(bf16[32,64,256]{2,1,0:T(8,128)(2,1)} %get-tuple-element.92), channel_id=1, source_target_pairs={{0,1},{1,0},{2,3},{3,2},{4,5},{5,4},{6,7},{7,6},{8,9},{9,8},{10,11... | collective-permute-start | bytes 3145736 | tf_op jit(solution)/shard_map/ppermute | solution.py:434
  162.0 14.8 %collective-permute-start.21 = (bf16[16,64,256]{2,1,0:T(8,128)(2,1)S(1)}, bf16[16,64,256]{2,1,0:T(8,128)(2,1)S(1)}, u32[]{:S(2)}, u32[]{:S(2)}) collective-permute-start(bf16[16,64,256]{2,1,0:T(8,128)(2,1)S(1)} %get-tuple-element.99), channel_id=1, source_target_pairs={{0,2},{1,3},{2,0},{3,1},{4,6},{5,7},{6,4},{7,5},{8,10},{9,11},{10,... | collective-permute-start | bytes 1572872 | tf_op jit(solution)/shard_map/ppermute | solution.py:434
  164.2 40.4 %collective-permute-start.29 = (bf16[32,64,256]{2,1,0:T(8,128)(2,1)S(1)}, bf16[32,64,256]{2,1,0:T(8,128)(2,1)S(1)}, u32[]{:S(2)}, u32[]{:S(2)}) collective-permute-start(bf16[32,64,256]{2,1,0:T(8,128)(2,1)S(1)} %add_convert_fusion), channel_id=1, source_target_pairs={{0,2},{1,3},{2,0},{3,1},{4,6},{5,7},{6,4},{7,5},{8,10},{9,11},{10,... | collective-permute-start | bytes 3145736 | tf_op jit(solution)/shard_map/ppermute | solution.py:434
  164.5 16.4 %collective-permute-start.22 = (bf16[16,64,256]{2,1,0:T(8,128)(2,1)S(1)}, bf16[16,64,256]{2,1,0:T(8,128)(2,1)S(1)}, u32[]{:S(2)}, u32[]{:S(2)}) collective-permute-start(bf16[16,64,256]{2,1,0:T(8,128)(2,1)S(1)} %get-tuple-element.98), channel_id=1, source_target_pairs={{0,8},{1,9},{2,10},{3,11},{4,12},{5,13},{6,14},{7,15},{8,0},{9,1},... | collective-permute-start | bytes 1572872 | tf_op jit(solution)/shard_map/ppermute | solution.py:434
  181.1 25.3 %collective-permute-start.23 = (bf16[8,64,256]{2,1,0:T(8,128)(2,1)S(1)}, bf16[8,64,256]{2,1,0:T(8,128)(2,1)S(1)}, u32[]{:S(2)}, u32[]{:S(2)}) collective-permute-start(bf16[8,64,256]{2,1,0:T(8,128)(2,1)S(1)} %slice.130), channel_id=1, source_target_pairs={{0,8},{1,9},{2,10},{3,11},{4,12},{5,13},{6,14},{7,15},{8,0},{9,1},... | collective-permute-start | bytes 786440 | tf_op jit(solution)/shard_map/ppermute | solution.py:434
  183.8 26.9 %collective-permute-start.24 = (bf16[8,64,256]{2,1,0:T(8,128)(2,1)S(1)}, bf16[8,64,256]{2,1,0:T(8,128)(2,1)S(1)}, u32[]{:S(2)}, u32[]{:S(2)}) collective-permute-start(bf16[8,64,256]{2,1,0:T(8,128)(2,1)S(1)} %slice.129), channel_id=1, source_target_pairs={{0,4},{1,5},{2,6},{3,7},{4,0},{5,1},{6,2},{7,3},{8,12},{9,13},{10,... | collective-permute-start | bytes 786440 | tf_op jit(solution)/shard_map/ppermute | solution.py:434
  (32 other events, 399.8 us)

commit v3 on v2

--- a/solution.py
+++ b/solution.py
@@ -147,8 +147,8 @@
     patches, forms = rest[:2]
     rest = rest[1:]
     if first:
-        screen_parts, stress_parts = rest[1 : 1 + LAYER], rest[1 + LAYER : 1 + 2 * LAYER]
-        rest = rest[1 + 2 * LAYER :]
+        screen_parts, stress_parts = rest[1 : 1 + PAIR], rest[1 + PAIR : 1 + 2 * PAIR]
+        rest = rest[1 + 2 * PAIR :]
         grad, screen_grad, screens, stress = rest[:4]
         rest = rest[4:]
     else:
@@ -179,7 +179,7 @@
             at += size
     if first:
         for parts, whole in ((screen_parts, screens), (stress_parts, stress)):
-            size = whole.shape[0] // LAYER
+            size = whole.shape[0] // PAIR
             for i, part in enumerate(parts):
                 loads.append((part, whole.at[pl.ds(i * size, size)]))
     loads = [pltpu.make_async_copy(a, b, sems.at[i]) for i, (a, b) in enumerate(loads)]
@@ -385,7 +385,7 @@
     if first:
         state = ()
         for parts in (screens, stress):
-            shape = (LAYER * parts[0].shape[0],) + parts[0].shape[1:]
+            shape = (PAIR * parts[0].shape[0],) + parts[0].shape[1:]
             out_shape.append(jax.ShapeDtypeStruct(shape, parts[0].dtype))
     else:
         screens, stress = [screens], [stress]
@@ -423,7 +423,7 @@
         compiler_params=pltpu.CompilerParams(vmem_limit_bytes=8 * MIB),
         cost_estimate=pl.CostEstimate(
             flops=layers * span * 4 * epochs * CHUNK * (NEAR + 1) * PBLK,
-            bytes_accessed=20 * MIB,
+            bytes_accessed=1024,
             transcendentals=layers * span * CHUNK * NEAR * PBLK,
         ),
         name="fit",
@@ -436,7 +436,7 @@
 
 def orders(devices):
     stages = devices.bit_length() - 1
-    high = list(range(stages - 1, 1, -1))
+    high = list(range(2, stages))
     return [1] + high, high + [1]
 
 
@@ -466,7 +466,7 @@
     parts = [total[:middle], total[middle:]]
     both = orders(devices)
     stages = len(both[0])
-    back = partner(there, devices, PAIR)
+    back = None
     for stage in range(stages):
         got = []
         for side in range(2):
@@ -476,9 +476,12 @@
             got.append(partner(given, devices, 1 << both[side][stage]))
         for side in range(2):
             if side:
-                parts[0], got[1] = lax.optimization_barrier((parts[0], got[1]))
+                _, got[1] = lax.optimization_barrier((parts[0], got[1]))
             size = parts[side].shape[0] // 2
             parts[side] = parts[side][:size] + got[side].astype(jnp.float32)
+            if back is None:
+                _, there = lax.optimization_barrier((parts[0], there))
+                back = partner(there, devices, PAIR)
     return jnp.concatenate(parts, axis=0), back
 
 
@@ -516,7 +519,8 @@
     )
 
     def exchange(parts):
-        return [parts[0]] + [partner(parts[x], devices, x * LAYER) for x in range(1, layers)]
+        got = [partner(parts[x], devices, x * LAYER) for x in range(layers - 1, 0, -1)]
+        return [parts[0]] + got[::-1]
 
     other, pix = lax.optimization_barrier((other, pix))
     pix = exchange(pix)
@@ -530,13 +534,10 @@
     got = [exchange(o) for o in obs]
     across = partner(held, devices, PAIR)
     across, got[0][1] = lax.optimization_barrier((across, got[0][1]))
-    all_stress = [held, across, partner(held, devices, 1), partner(across, devices, 1)]
-    all_screens = [
-        screens,
-        across_screens,
-        partner(screens, devices, 1),
-        partner(across_screens, devices, 1),
-    ]
+    held = jnp.concatenate([held, across], axis=0)
+    all_stress = [held, partner(held, devices, 1)]
+    near_screens = jnp.concatenate([screens, across_screens], axis=0)
+    all_screens = [near_screens, partner(near_screens, devices, 1)]
 
     patch_blocks = devices * local
     east, north, depth, compliance = patch_geometry

time: 222 us -> 216 us (0.973); the launches traced: 226 us -> 215 us
  starting transfers between devices: 73.4 us -> 50.2 us
  local copies, waits for them, and re-layouts: 23.3 us -> 28.6 us
  waiting for transfers between devices: 72.3 us -> 77.2 us
  Pallas kernels: 45.8 us -> 49 us
    ppermute x30 -> x28, starting transfers between devices: 73.4 us -> 50.2 us  [partner(): lax.ppermute(values, 'tile', [(i, i ^ distance) for i in range(devices)])]
    ppermute x30 -> x28, waiting for transfers between devices: 72.3 us -> 77.2 us  [partner(): lax.ppermute(values, 'tile', [(i, i ^ distance) for i in range(devices)])]
    pallas_call x3, Pallas kernels: 40.8 us -> 44.4 us  [fit(): pl.pallas_call(functools.partial(fit_kernel, first, final, layers, slots,...]
    unnamed x53 -> x63, local copies, waits for them, and re-layouts: 12.6 us -> 15.7 us
  transfers between devices with their start and end apart: 30 -> 28, of which waited for: 14 -> 11; matrix products, arithmetic and copies ran while one was open for 8% -> 9% of each run, Pallas kernels for 19% -> 22%
where the time goes in v3:
time: 216 us; the launch traced here: 215 us
  waiting for transfers between devices  77.2 us (36%)
  starting transfers between devices  50.2 us (23%)
  Pallas kernels  49 us (23%)
  local copies, waits for them, and re-layouts  28.6 us (13%)
  other arithmetic  9.02 us (4%)
    ppermute x28, waiting for transfers between devices, partner(): lax.ppermute(values, 'tile', [(i, i ^ distance) for i in range(devices)])  77.2 us
    ppermute x28, starting transfers between devices, partner(): lax.ppermute(values, 'tile', [(i, i ^ distance) for i in range(devices)])  50.2 us
    pallas_call x3, Pallas kernels, fit(): pl.pallas_call(functools.partial(fit_kernel, first, final, layers, slots,...  44.4 us
    unnamed x63, local copies, waits for them, and re-layouts  15.7 us
    concatenate x1, local copies, waits for them, and re-layouts, on_device(): jnp.concatenate([faces[second] for _, second in CROSS] + [jnp.zeros((8,)...  4.73 us
    pallas_call x1, Pallas kernels, pack(): pl.pallas_call(functools.partial(pack_kernel, local_tiles, layers, slots)...  4.63 us
  transfers between devices with their start and end apart: 28, of which 11 were waited for; matrix products, arithmetic and copies ran while one was open for 9% of the time, Pallas kernels for 22%

profile of v3, /device:TPU:0, one launch (start us, length us, event | category | flops | bytes accessed | tf_op | source)
XLA Modules:
  0.0 215.0 jit_solution(972972932309874686)
XLA Ops:
  1.7 4.1 %collective-permute-start = (bf16[512,256]{1,0:T(8,128)(2,1)S(1)}, bf16[512,256]{1,0:T(8,128)(2,1)S(1)}, u32[]{:S(2)}, u32[]{:S(2)}) collective-permute-start(bf16[512,256]{1,0:T(8,128)(2,1)S(1)} %bitcast.26), channel_id=1, source_target_pairs={{0,8},{1,9},{2,10},{3,11},{4,12},{5,13},{6,14},{7,15},{8,0},{9,1},... | collective-permute-start | bytes 786440 | tf_op jit(solution)/shard_map/ppermute | solution.py:434
  11.2 4.6 %pack.1 = (bf16[24,64,128]{2,1,0:T(8,128)(2,1)S(1)}, bf16[24,64,128]{2,1,0:T(8,128)(2,1)S(1)}, bf16[24,64,128]{2,1,0:T(8,128)(2,1)}, bf16[24,64,128]{2,1,0:T(8,1...) custom-call(s32[1]{0:T(128)} %bitcast.3.here, ...), custom_call_target="tpu_custom_call" | custom-call | tf_op jit(solution)/shard_map/pack/pallas_call | solution.py:96
  22.0 3.6 %collective-permute-start.4 = (f32[65,8,128]{2,1,0:T(8,128)S(1)}, f32[65,8,128]{2,1,0:T(8,128)S(1)}, u32[]{:S(2)}, u32[]{:S(2)}) collective-permute-start(f32[65,8,128]{2,1,0:T(8,128)S(1)} %get-tuple-element.54), channel_id=1, source_target_pairs={{0,12},{1,13},{2,14},{3,15},{4,8},{5,9},{6,10},{7,11},{8,4},{9,5},... | collective-permute-start | bytes 798728 | tf_op jit(solution)/shard_map/ppermute | solution.py:434
  26.1 14.1 %collective-permute-done.1 = bf16[1024,256]{1,0:T(8,128)(2,1)S(1)} collective-permute-done((bf16[1024,256]{1,0:T(8,128)(2,1)S(1)}, bf16[1024,256]{1,0:T(8,128)(2,1)S(1)}, u32[]{:S(2)}, u32[]{:S(2)}) %collective-permute-start.1) | collective-permute-done | bytes 524320 | tf_op jit(solution)/shard_map/ppermute | solution.py:434
  40.3 15.5 %collective-permute-done.2.refs_10_ = f32[65,8,128]{2,1,0:T(8,128)S(1)} collective-permute-done((f32[65,8,128]{2,1,0:T(8,128)S(1)}, f32[65,8,128]{2,1,0:T(8,128)S(1)}, u32[]{:S(2)}, u32[]{:S(2)}) %collective-permute-start.2) | collective-permute-done | bytes 266272 | tf_op jit(solution)/shard_map/ppermute | solution.py:434
  55.8 1.9 collective-permute-start.12
  64.4 10.8 %collective-permute-done.9 = bf16[2048,256]{1,0:T(8,128)(2,1)S(1)} collective-permute-done((bf16[2048,256]{1,0:T(8,128)(2,1)S(1)}, bf16[2048,256]{1,0:T(8,128)(2,1)S(1)}, u32[]{:S(2)}, u32[]{:S(2)}) %collective-permute-start.9) | collective-permute-done | bytes 1048608 | tf_op jit(solution)/shard_map/ppermute | solution.py:434
  81.3 4.7 %concatenate.27 = bf16[32,128,256]{2,0,1:T(8,128)(2,1)S(1)} concatenate(bf16[4,128,256]{2,0,1:T(4,128)(2,1)S(1)} %get-tuple-element.100, bf16[4,128,256]{2,0,1:T(4,128)(2,1)S(1)} %get-tuple-element.99, bf16[4,128,256]{2,0,1:T(4,128)(2,1)S(1)} %get-tuple-element.100, bf16[4,128,256]{2,0,1:T(4,128)(2,1)} %get-tuple-element.98, bf16[4,128,256]{2,0,1:T(4,128)(2,1)S(1)} %get-tuple-element.99, ...), dimensions={0} | concatenate | bytes 4194304 | tf_op jit(solution)/shard_map/concatenate | solution.py:556
  88.8 1.8 collective-permute-start.16
  90.7 2.2 %collective-permute-start.17 = (bf16[24,64,128]{2,1,0:T(8,128)(2,1)}, bf16[24,64,128]{2,1,0:T(8,128)(2,1)}, u32[]{:S(2)}, u32[]{:S(2)}) collective-permute-start(bf16[24,64,128]{2,1,0:T(8,128)(2,1)} %copy-done.17), channel_id=1, source_target_pairs={{0,12},{1,13},{2,14},{3,15},{4,8},{5,9},{6,10},{7,11},{8,4},{9,5},... | collective-permute-start | bytes 1179656 | tf_op jit(solution)/shard_map/ppermute | solution.py:434
  93.0 2.2 %collective-permute-start.7 = (bf16[16,64,128]{2,1,0:T(8,128)(2,1)}, bf16[16,64,128]{2,1,0:T(8,128)(2,1)S(1)}, u32[]{:S(2)}, u32[]{:S(2)}) collective-permute-start(bf16[16,64,128]{2,1,0:T(8,128)(2,1)} %copy-done.25), channel_id=1, source_target_pairs={{0,8},{1,9},{2,10},{3,11},{4,12},{5,13},{6,14},{7,15},{8,0},{9,1},... | collective-permute-start | bytes 786440 | tf_op jit(solution)/shard_map/ppermute | solution.py:434
  99.1 36.4 %fit.3 = (f32[128,64,256]{2,1,0:T(8,128)S(1)}, f32[128,64,256]{2,1,0:T(8,128)S(1)}, bf16[128,64,256]{2,1,0:T(8,128)(2,1)S(1)}, bf16[8192,256]{1,0:T(8,128)(2,1)S(1)}) custom-call(s32[768]{0:T(1024)S(1)} %convert_element_type.49.refs_0_, s32[1536]{0:T(1024)S(1)} %reshape.52.refs_1_, s32[128]{0:T(128)S(1)} %get-tuple-element.104.refs_2_, ...), custom_call_target="tpu_custom_call" | custom-call | flops 3221225472 | bytes 1024 | tf_op jit(solution)/shard_map/fit/pallas_call | solution.py:397
  135.5 3.5 %collective-permute-start.8 = (bf16[16,64,128]{2,1,0:T(8,128)(2,1)S(1)}, bf16[16,64,128]{2,1,0:T(8,128)(2,1)S(1)}, u32[]{:S(2)}, u32[]{:S(2)}) collective-permute-start(bf16[16,64,128]{2,1,0:T(8,128)(2,1)S(1)} %copy-done.24), channel_id=1, source_target_pairs={{0,12},{1,13},{2,14},{3,15},{4,8},{5,9},{6,10},{7,11},{8,4},{9,5},... | collective-permute-start | bytes 786440 | tf_op jit(solution)/shard_map/ppermute | solution.py:434
  139.1 5.3 %fit.4 = (f32[128,64,256]{2,1,0:T(8,128)S(1)}, f32[128,64,256]{2,1,0:T(8,128)S(1)}) custom-call(s32[768]{0:T(1024)S(1)} %convert_element_type.49.refs_0_, s32[1536]{0:T(1024)S(1)} %reshape.52.refs_1_, s32[128]{0:T(128)S(1)} %get-tuple-element.104.refs_2_, s32[128]{0:T(128)S(1)} %get-tuple-element.105.refs_3_, ...), custom_call_target="tpu_custom_call", output_to_operand_aliasing={{0}: (17, {}), {1}: (18, {})} | custom-call | flops 3221225472 | bytes 1024 | tf_op jit(solution)/shard_map/fit/pallas_call | solution.py:397
  145.7 2.7 %fit.5 = (f32[128,64,256]{2,1,0:T(8,128)S(1)}, f32[128,64,256]{2,1,0:T(8,128)S(1)}, bf16[64,64,256]{2,1,0:T(8,128)(2,1)S(1)}, bf16[32,64,256]{2,1,0:T(8,128)(2,1)S(1)}, bf16[32,64,256]{2,1,0:T(8,128)(2,1)S(1)}) custom-call(s32[768]{0:T(1024)S(1)} %convert_element_type.49.refs_0_, ...), custom_call_target="tpu_custom_call", output_to_operand_aliasing={{0}: (17, {}), {1}: (18, {})} | custom-call | flops 2147483648 | bytes 1024 | tf_op jit(solution)/shard_map/fit/pallas_call | solution.py:397
  150.4 4.2 %collective-permute-done.18 = bf16[64,64,256]{2,1,0:T(8,128)(2,1)S(1)} collective-permute-done((bf16[64,64,256]{2,1,0:T(8,128)(2,1)S(1)}, bf16[64,64,256]{2,1,0:T(8,128)(2,1)S(1)}, u32[]{:S(2)}, u32[]{:S(2)}) %collective-permute-start.18) | collective-permute-done | bytes 2097184 | tf_op jit(solution)/shard_map/ppermute | solution.py:434
  157.5 4.4 %collective-permute-start.22 = (bf16[16,64,256]{2,1,0:T(8,128)(2,1)S(1)}, bf16[16,64,256]{2,1,0:T(8,128)(2,1)S(1)}, u32[]{:S(2)}, u32[]{:S(2)}) collective-permute-start(bf16[16,64,256]{2,1,0:T(8,128)(2,1)S(1)} %get-tuple-element.94), channel_id=1, source_target_pairs={{0,4},{1,5},{2,6},{3,7},{4,0},{5,1},{6,2},{7,3},{8,12},{9,13},{10,... | collective-permute-start | bytes 1572872 | tf_op jit(solution)/shard_map/ppermute | solution.py:434
  162.1 7.7 %collective-permute-done.19 = bf16[16,64,256]{2,1,0:T(8,128)(2,1)S(1)} collective-permute-done((bf16[16,64,256]{2,1,0:T(8,128)(2,1)S(1)}, bf16[16,64,256]{2,1,0:T(8,128)(2,1)S(1)}, u32[]{:S(2)}, u32[]{:S(2)}) %collective-permute-start.19) | collective-permute-done | bytes 524320 | tf_op jit(solution)/shard_map/ppermute | solution.py:434
  169.9 4.5 %collective-permute-done.22 = bf16[16,64,256]{2,1,0:T(8,128)(2,1)S(1)} collective-permute-done((bf16[16,64,256]{2,1,0:T(8,128)(2,1)S(1)}, bf16[16,64,256]{2,1,0:T(8,128)(2,1)S(1)}, u32[]{:S(2)}, u32[]{:S(2)}) %collective-permute-start.22) | collective-permute-done | bytes 524320 | tf_op jit(solution)/shard_map/ppermute | solution.py:434
  174.7 1.8 collective-permute-start.20
  176.5 8.5 %collective-permute-start.23 = (bf16[8,64,256]{2,1,0:T(8,128)(2,1)S(1)}, bf16[8,64,256]{2,1,0:T(8,128)(2,1)S(1)}, u32[]{:S(2)}, u32[]{:S(2)}) collective-permute-start(bf16[8,64,256]{2,1,0:T(8,128)(2,1)S(1)} %slice.131), channel_id=1, source_target_pairs={{0,8},{1,9},{2,10},{3,11},{4,12},{5,13},{6,14},{7,15},{8,0},{9,1},... | collective-permute-start | bytes 786440 | tf_op jit(solution)/shard_map/ppermute | solution.py:434
  186.5 6.1 %collective-permute-start.21 = (bf16[4,64,256]{2,1,0:T(8,128)(2,1)S(1)}, bf16[4,64,256]{2,1,0:T(8,128)(2,1)S(1)}, u32[]{:S(2)}, u32[]{:S(2)}) collective-permute-start(bf16[4,64,256]{2,1,0:T(8,128)(2,1)S(1)} %slice.134), channel_id=1, source_target_pairs={{0,8},{1,9},{2,10},{3,11},{4,12},{5,13},{6,14},{7,15},{8,0},{9,1},... | collective-permute-start | bytes 393224 | tf_op jit(solution)/shard_map/ppermute | solution.py:434
  192.6 6.9 %collective-permute-done.23 = bf16[8,64,256]{2,1,0:T(8,128)(2,1)S(1)} collective-permute-done((bf16[8,64,256]{2,1,0:T(8,128)(2,1)S(1)}, bf16[8,64,256]{2,1,0:T(8,128)(2,1)S(1)}, u32[]{:S(2)}, u32[]{:S(2)}) %collective-permute-start.23) | collective-permute-done | bytes 262176 | tf_op jit(solution)/shard_map/ppermute | solution.py:434
  202.0 10.3 %collective-permute-done.24 = bf16[4,64,256]{2,1,0:T(8,128)(2,1)S(1)} collective-permute-done((bf16[4,64,256]{2,1,0:T(8,128)(2,1)S(1)}, bf16[4,64,256]{2,1,0:T(8,128)(2,1)S(1)}, u32[]{:S(2)}, u32[]{:S(2)}) %collective-permute-start.24) | collective-permute-done | bytes 131104 | tf_op jit(solution)/shard_map/ppermute | solution.py:434
  (137 shorter events, 46.0 us)
Async XLA Ops:
  1.7 17.8 %collective-permute-start = (bf16[512,256]{1,0:T(8,128)(2,1)S(1)}, bf16[512,256]{1,0:T(8,128)(2,1)S(1)}, u32[]{:S(2)}, u32[]{:S(2)}) collective-permute-start(bf16[512,256]{1,0:T(8,128)(2,1)S(1)} %bitcast.26), channel_id=1, source_target_pairs={{0,8},{1,9},{2,10},{3,11},{4,12},{5,13},{6,14},{7,15},{8,0},{9,1},... | collective-permute-start | bytes 786440 | tf_op jit(solution)/shard_map/ppermute | solution.py:434
  5.8 53.6 %collective-permute-start.5 = (bf16[32,64,256]{2,1,0:T(8,128)(2,1)}, bf16[32,64,256]{2,1,0:T(8,128)(2,1)S(1)}, u32[]{:S(2)}, u32[]{:S(2)}) collective-permute-start(bf16[32,64,256]{2,1,0:T(8,128)(2,1)} %param.15), channel_id=1, source_target_pairs={{0,2},{1,3},{2,0},{3,1},{4,6},{5,7},{6,4},{7,5},{8,10},{9,11},{10,... | collective-permute-start | bytes 3145736 | tf_op jit(solution)/shard_map/ppermute | solution.py:434
  19.6 20.6 %collective-permute-start.1 = (bf16[1024,256]{1,0:T(8,128)(2,1)S(1)}, bf16[1024,256]{1,0:T(8,128)(2,1)S(1)}, u32[]{:S(2)}, u32[]{:S(2)}) collective-permute-start(bf16[1024,256]{1,0:T(8,128)(2,1)S(1)} %pad_maximum_fusion.1), channel_id=1, source_target_pairs={{0,4},{1,5},{2,6},{3,7},{4,0},{5,1},{6,2},{7,3},{8,12},{9,13},{10,... | collective-permute-start | bytes 1572872 | tf_op jit(solution)/shard_map/ppermute | solution.py:434
  21.2 34.6 %collective-permute-start.2 = (f32[65,8,128]{2,1,0:T(8,128)S(1)}, f32[65,8,128]{2,1,0:T(8,128)S(1)}, u32[]{:S(2)}, u32[]{:S(2)}) collective-permute-start(f32[65,8,128]{2,1,0:T(8,128)S(1)} %get-tuple-element.52), channel_id=1, source_target_pairs={{0,4},{1,5},{2,6},{3,7},{4,0},{5,1},{6,2},{7,3},{8,12},{9,13},{10,... | collective-permute-start | bytes 798728 | tf_op jit(solution)/shard_map/ppermute | solution.py:434
  21.7 34.2 %collective-permute-start.3 = (f32[65,8,128]{2,1,0:T(8,128)S(1)}, f32[65,8,128]{2,1,0:T(8,128)S(1)}, u32[]{:S(2)}, u32[]{:S(2)}) collective-permute-start(f32[65,8,128]{2,1,0:T(8,128)S(1)} %get-tuple-element.53), channel_id=1, source_target_pairs={{0,8},{1,9},{2,10},{3,11},{4,12},{5,13},{6,14},{7,15},{8,0},{9,1},... | collective-permute-start | bytes 798728 | tf_op jit(solution)/shard_map/ppermute | solution.py:434
  22.0 35.7 %collective-permute-start.4 = (f32[65,8,128]{2,1,0:T(8,128)S(1)}, f32[65,8,128]{2,1,0:T(8,128)S(1)}, u32[]{:S(2)}, u32[]{:S(2)}) collective-permute-start(f32[65,8,128]{2,1,0:T(8,128)S(1)} %get-tuple-element.54), channel_id=1, source_target_pairs={{0,12},{1,13},{2,14},{3,15},{4,8},{5,9},{6,10},{7,11},{8,4},{9,5},... | collective-permute-start | bytes 798728 | tf_op jit(solution)/shard_map/ppermute | solution.py:434
  40.2 24.1 %collective-permute-start.10 = (bf16[24,64,128]{2,1,0:T(8,128)(2,1)S(1)}, bf16[24,64,128]{2,1,0:T(8,128)(2,1)S(1)}, u32[]{:S(2)}, u32[]{:S(2)}) collective-permute-start(bf16[24,64,128]{2,1,0:T(8,128)(2,1)S(1)} %get-tuple-element.65), channel_id=1, source_target_pairs={{0,4},{1,5},{2,6},{3,7},{4,0},{5,1},{6,2},{7,3},{8,12},{9,13},{10,... | collective-permute-start | bytes 1179656 | tf_op jit(solution)/shard_map/ppermute | solution.py:434
  55.8 33.0 %collective-permute-start.11 = (bf16[24,64,128]{2,1,0:T(8,128)(2,1)}, bf16[24,64,128]{2,1,0:T(8,128)(2,1)}, u32[]{:S(2)}, u32[]{:S(2)}) collective-permute-start(bf16[24,64,128]{2,1,0:T(8,128)(2,1)} %get-tuple-element.67), channel_id=1, source_target_pairs={{0,8},{1,9},{2,10},{3,11},{4,12},{5,13},{6,14},{7,15},{8,0},{9,1},... | collective-permute-start | bytes 1179656 | tf_op jit(solution)/shard_map/ppermute | solution.py:434
  55.8 34.8 %collective-permute-start.12 = (bf16[24,64,128]{2,1,0:T(8,128)(2,1)}, bf16[24,64,128]{2,1,0:T(8,128)(2,1)}, u32[]{:S(2)}, u32[]{:S(2)}) collective-permute-start(bf16[24,64,128]{2,1,0:T(8,128)(2,1)} %get-tuple-element.68), channel_id=1, source_target_pairs={{0,12},{1,13},{2,14},{3,15},{4,8},{5,9},{6,10},{7,11},{8,4},{9,5},... | collective-permute-start | bytes 1179656 | tf_op jit(solution)/shard_map/ppermute | solution.py:434
  57.7 77.7 %collective-permute-start.15 = (bf16[24,64,128]{2,1,0:T(8,128)(2,1)}, bf16[24,64,128]{2,1,0:T(8,128)(2,1)}, u32[]{:S(2)}, u32[]{:S(2)}) collective-permute-start(bf16[24,64,128]{2,1,0:T(8,128)(2,1)} %get-tuple-element.74), channel_id=1, source_target_pairs={{0,4},{1,5},{2,6},{3,7},{4,0},{5,1},{6,2},{7,3},{8,12},{9,13},{10,... | collective-permute-start | bytes 1179656 | tf_op jit(solution)/shard_map/ppermute | solution.py:434
  59.3 15.8 %collective-permute-start.9 = (bf16[2048,256]{1,0:T(8,128)(2,1)S(1)}, bf16[2048,256]{1,0:T(8,128)(2,1)S(1)}, u32[]{:S(2)}, u32[]{:S(2)}) collective-permute-start(bf16[2048,256]{1,0:T(8,128)(2,1)S(1)} %pad_maximum_fusion), channel_id=1, source_target_pairs={{0,2},{1,3},{2,0},{3,1},{4,6},{5,7},{6,4},{7,5},{8,10},{9,11},{10,... | collective-permute-start | bytes 3145736 | tf_op jit(solution)/shard_map/ppermute | solution.py:434
  64.4 28.6 %collective-permute-start.13 = (bf16[64,64,256]{2,1,0:T(8,128)(2,1)}, bf16[64,64,256]{2,1,0:T(8,128)(2,1)}, u32[]{:S(2)}, u32[]{:S(2)}) collective-permute-start(bf16[64,64,256]{2,1,0:T(8,128)(2,1)} %constant_dynamic-update-slice_fusion.refs_15_), channel_id=1, source_target_pairs={{0,1},{1,0},{2,3},{3,2},{4,5},{5,4},{6,7},{7,6},{8,9},{9,8},{10,11... | collective-permute-start | bytes 6291464 | tf_op jit(solution)/shard_map/ppermute | solution.py:434
  76.2 16.7 %collective-permute-start.14 = (bf16[4096,256]{1,0:T(8,128)(2,1)}, bf16[4096,256]{1,0:T(8,128)(2,1)}, u32[]{:S(2)}, u32[]{:S(2)}) collective-permute-start(bf16[4096,256]{1,0:T(8,128)(2,1)} %constant_dynamic-update-slice_fusion.2.refs_17_), channel_id=1, source_target_pairs={{0,1},{1,0},{2,3},{3,2},{4,5},{5,4},{6,7},{7,6},{8,9},{9,8},{10,11... | collective-permute-start | bytes 6291464 | tf_op jit(solution)/shard_map/ppermute | solution.py:434
  88.8 50.2 %collective-permute-start.16 = (bf16[24,64,128]{2,1,0:T(8,128)(2,1)}, bf16[24,64,128]{2,1,0:T(8,128)(2,1)}, u32[]{:S(2)}, u32[]{:S(2)}) collective-permute-start(bf16[24,64,128]{2,1,0:T(8,128)(2,1)} %copy-done.18), channel_id=1, source_target_pairs={{0,8},{1,9},{2,10},{3,11},{4,12},{5,13},{6,14},{7,15},{8,0},{9,1},... | collective-permute-start | bytes 1179656 | tf_op jit(solution)/shard_map/ppermute | solution.py:434
  90.7 48.4 %collective-permute-start.17 = (bf16[24,64,128]{2,1,0:T(8,128)(2,1)}, bf16[24,64,128]{2,1,0:T(8,128)(2,1)}, u32[]{:S(2)}, u32[]{:S(2)}) collective-permute-start(bf16[24,64,128]{2,1,0:T(8,128)(2,1)} %copy-done.17), channel_id=1, source_target_pairs={{0,12},{1,13},{2,14},{3,15},{4,8},{5,9},{6,10},{7,11},{8,4},{9,5},... | collective-permute-start | bytes 1179656 | tf_op jit(solution)/shard_map/ppermute | solution.py:434
  93.0 51.4 %collective-permute-start.6 = (bf16[16,64,128]{2,1,0:T(8,128)(2,1)}, bf16[16,64,128]{2,1,0:T(8,128)(2,1)S(1)}, u32[]{:S(2)}, u32[]{:S(2)}) collective-permute-start(bf16[16,64,128]{2,1,0:T(8,128)(2,1)} %copy-done.26), channel_id=1, source_target_pairs={{0,4},{1,5},{2,6},{3,7},{4,0},{5,1},{6,2},{7,3},{8,12},{9,13},{10,... | collective-permute-start | bytes 786440 | tf_op jit(solution)/shard_map/ppermute | solution.py:434
  93.0 51.4 %collective-permute-start.7 = (bf16[16,64,128]{2,1,0:T(8,128)(2,1)}, bf16[16,64,128]{2,1,0:T(8,128)(2,1)S(1)}, u32[]{:S(2)}, u32[]{:S(2)}) collective-permute-start(bf16[16,64,128]{2,1,0:T(8,128)(2,1)} %copy-done.25), channel_id=1, source_target_pairs={{0,8},{1,9},{2,10},{3,11},{4,12},{5,13},{6,14},{7,15},{8,0},{9,1},... | collective-permute-start | bytes 786440 | tf_op jit(solution)/shard_map/ppermute | solution.py:434
  155.7 14.0 %collective-permute-start.19 = (bf16[16,64,256]{2,1,0:T(8,128)(2,1)S(1)}, bf16[16,64,256]{2,1,0:T(8,128)(2,1)S(1)}, u32[]{:S(2)}, u32[]{:S(2)}) collective-permute-start(bf16[16,64,256]{2,1,0:T(8,128)(2,1)S(1)} %get-tuple-element.95), channel_id=1, source_target_pairs={{0,2},{1,3},{2,0},{3,1},{4,6},{5,7},{6,4},{7,5},{8,10},{9,11},{10,... | collective-permute-start | bytes 1572872 | tf_op jit(solution)/shard_map/ppermute | solution.py:434
  157.4 27.6 %collective-permute-start.26 = (bf16[32,64,256]{2,1,0:T(8,128)(2,1)S(1)}, bf16[32,64,256]{2,1,0:T(8,128)(2,1)S(1)}, u32[]{:S(2)}, u32[]{:S(2)}) collective-permute-start(bf16[32,64,256]{2,1,0:T(8,128)(2,1)S(1)} %copy-done.16), channel_id=1, source_target_pairs={{0,1},{1,0},{2,3},{3,2},{4,5},{5,4},{6,7},{7,6},{8,9},{9,8},{10,11... | collective-permute-start | bytes 3145736 | tf_op jit(solution)/shard_map/ppermute | solution.py:434
  157.5 17.0 %collective-permute-start.22 = (bf16[16,64,256]{2,1,0:T(8,128)(2,1)S(1)}, bf16[16,64,256]{2,1,0:T(8,128)(2,1)S(1)}, u32[]{:S(2)}, u32[]{:S(2)}) collective-permute-start(bf16[16,64,256]{2,1,0:T(8,128)(2,1)S(1)} %get-tuple-element.94), channel_id=1, source_target_pairs={{0,4},{1,5},{2,6},{3,7},{4,0},{5,1},{6,2},{7,3},{8,12},{9,13},{10,... | collective-permute-start | bytes 1572872 | tf_op jit(solution)/shard_map/ppermute | solution.py:434
  161.9 51.4 %collective-permute-start.25 = (bf16[32,64,256]{2,1,0:T(8,128)(2,1)S(1)}, bf16[32,64,256]{2,1,0:T(8,128)(2,1)S(1)}, u32[]{:S(2)}, u32[]{:S(2)}) collective-permute-start(bf16[32,64,256]{2,1,0:T(8,128)(2,1)S(1)} %copy-done.14), channel_id=1, source_target_pairs={{0,1},{1,0},{2,3},{3,2},{4,5},{5,4},{6,7},{7,6},{8,9},{9,8},{10,11... | collective-permute-start | bytes 3145736 | tf_op jit(solution)/shard_map/ppermute | solution.py:434
  176.5 23.0 %collective-permute-start.23 = (bf16[8,64,256]{2,1,0:T(8,128)(2,1)S(1)}, bf16[8,64,256]{2,1,0:T(8,128)(2,1)S(1)}, u32[]{:S(2)}, u32[]{:S(2)}) collective-permute-start(bf16[8,64,256]{2,1,0:T(8,128)(2,1)S(1)} %slice.131), channel_id=1, source_target_pairs={{0,8},{1,9},{2,10},{3,11},{4,12},{5,13},{6,14},{7,15},{8,0},{9,1},... | collective-permute-start | bytes 786440 | tf_op jit(solution)/shard_map/ppermute | solution.py:434
  185.4 27.9 %collective-permute-start.27 = (bf16[32,64,256]{2,1,0:T(8,128)(2,1)S(1)}, bf16[32,64,256]{2,1,0:T(8,128)(2,1)S(1)}, u32[]{:S(2)}, u32[]{:S(2)}) collective-permute-start(bf16[32,64,256]{2,1,0:T(8,128)(2,1)S(1)} %add_convert_fusion), channel_id=1, source_target_pairs={{0,2},{1,3},{2,0},{3,1},{4,6},{5,7},{6,4},{7,5},{8,10},{9,11},{10,... | collective-permute-start | bytes 3145736 | tf_op jit(solution)/shard_map/ppermute | solution.py:434
  186.5 15.5 %collective-permute-start.21 = (bf16[4,64,256]{2,1,0:T(8,128)(2,1)S(1)}, bf16[4,64,256]{2,1,0:T(8,128)(2,1)S(1)}, u32[]{:S(2)}, u32[]{:S(2)}) collective-permute-start(bf16[4,64,256]{2,1,0:T(8,128)(2,1)S(1)} %slice.134), channel_id=1, source_target_pairs={{0,8},{1,9},{2,10},{3,11},{4,12},{5,13},{6,14},{7,15},{8,0},{9,1},... | collective-permute-start | bytes 393224 | tf_op jit(solution)/shard_map/ppermute | solution.py:434
  (34 other events, 295.4 us)

commit v4 on v3

--- a/solution.py
+++ b/solution.py
@@ -111,7 +111,7 @@
             pltpu.SMEM((layers,), jnp.int32),
             pltpu.SemaphoreType.DMA(((len(sizes) + 1) * layers,)),
         ],
-        compiler_params=pltpu.CompilerParams(vmem_limit_bytes=10 * MIB),
+        compiler_params=pltpu.CompilerParams(vmem_limit_bytes=9 * MIB),
         name="pack",
     )(here, block_tiles, block_counts, observations, pixel_geometry)
     rounds = len(sizes)
@@ -420,7 +420,7 @@
             pltpu.SemaphoreType.DMA((2 * layers * len(groups) + 2 * LAYER,)),
         ],
         input_output_aliases={} if first else {before: 0, before + 1: 1},
-        compiler_params=pltpu.CompilerParams(vmem_limit_bytes=8 * MIB),
+        compiler_params=pltpu.CompilerParams(vmem_limit_bytes=6 * MIB),
         cost_estimate=pl.CostEstimate(
             flops=layers * span * 4 * epochs * CHUNK * (NEAR + 1) * PBLK,
             bytes_accessed=1024,
@@ -530,15 +530,6 @@
             other = partner(held, devices, distance)
         held = jnp.concatenate([held, other], axis=0)
         distance //= 2
-    held, pix, across_screens = lax.optimization_barrier((held, pix, across_screens))
-    got = [exchange(o) for o in obs]
-    across = partner(held, devices, PAIR)
-    across, got[0][1] = lax.optimization_barrier((across, got[0][1]))
-    held = jnp.concatenate([held, across], axis=0)
-    all_stress = [held, partner(held, devices, 1)]
-    near_screens = jnp.concatenate([screens, across_screens], axis=0)
-    all_screens = [near_screens, partner(near_screens, devices, 1)]
-
     patch_blocks = devices * local
     east, north, depth, compliance = patch_geometry
     origin = patch_geometry[:2, 0]
@@ -559,9 +550,22 @@
     forms = jnp.swapaxes(forms.reshape(TERMS, patch_blocks, PBLK), 0, 1)
     patches = jnp.stack([east, north, depth * depth])
     patches = jnp.swapaxes(patches.reshape(3, patch_blocks, PBLK), 0, 1)
+    cutoffs = cutoff_lists.reshape(-1)
+    held, pix[1], across_screens = lax.optimization_barrier((held, pix[1], across_screens))
+    across_screens, forms, patches, cutoffs = lax.optimization_barrier(
+        (across_screens, forms, patches, cutoffs)
+    )
+    got = [exchange(o) for o in obs]
+    across = partner(held, devices, PAIR)
+    across, pix, got[0] = lax.optimization_barrier((across, pix, got[0]))
+    held = jnp.concatenate([held, across], axis=0)
+    all_stress = [held, partner(held, devices, 1)]
+    near_screens = jnp.concatenate([screens, across_screens], axis=0)
+    all_screens = [near_screens, partner(near_screens, devices, 1)]
+
     places, spots = block_places(devices, here, patch_blocks, local, epochs)
     info = jnp.stack([p[slots, :3, :slots] for p in pix]).astype(jnp.int32).reshape(-1)
-    tables = (info, cutoff_lists.reshape(-1), places, spots, origin)
+    tables = (info, cutoffs, places, spots, origin)
 
     state = (
         jax.ShapeDtypeStruct((patch_blocks, epochs, PBLK), jnp.float32),

time: 216 us -> 225 us (1.042); the launches traced: 215 us -> 221 us
  waiting for transfers between devices: 77.2 us -> 92.9 us
  starting transfers between devices: 50.2 us -> 42.8 us
  Pallas kernels: 49 us -> 44.5 us
  local copies, waits for them, and re-layouts: 28.6 us -> 31.6 us
    ppermute x28, waiting for transfers between devices: 77.2 us -> 92.9 us  [partner(): lax.ppermute(values, 'tile', [(i, i ^ distance) for i in range(devices)])]
    ppermute x28, starting transfers between devices: 50.2 us -> 42.8 us  [partner(): lax.ppermute(values, 'tile', [(i, i ^ distance) for i in range(devices)])]
    pallas_call x3, Pallas kernels: 44.4 us -> 39.8 us  [fit(): pl.pallas_call(functools.partial(fit_kernel, first, final, layers, slots,...]
    concatenate x1, local copies, waits for them, and re-layouts: 4.73 us -> 7.84 us  [on_device(): jnp.concatenate([faces[second] for _, second in CROSS] + [jnp.zeros((8,)...]
    unnamed x63 -> x49, local copies, waits for them, and re-layouts: 15.7 us -> 15.3 us
  transfers between devices with their start and end apart: 28 -> 28, of which waited for: 11 -> 10; matrix products, arithmetic and copies ran while one was open for 9% -> 11% of each run, Pallas kernels for 22% -> 19%
where the time goes in v4:
time: 225 us; the launch traced here: 221 us
  waiting for transfers between devices  92.9 us (41%)
  Pallas kernels  44.5 us (20%)
  starting transfers between devices  42.8 us (19%)
  local copies, waits for them, and re-layouts  31.6 us (14%)
  other arithmetic  8.44 us (4%)
    ppermute x28, waiting for transfers between devices, partner(): lax.ppermute(values, 'tile', [(i, i ^ distance) for i in range(devices)])  92.9 us
    ppermute x28, starting transfers between devices, partner(): lax.ppermute(values, 'tile', [(i, i ^ distance) for i in range(devices)])  42.8 us
    pallas_call x3, Pallas kernels, fit(): pl.pallas_call(functools.partial(fit_kernel, first, final, layers, slots,...  39.8 us
    unnamed x49, local copies, waits for them, and re-layouts  15.3 us
    concatenate x1, local copies, waits for them, and re-layouts, on_device(): jnp.concatenate([faces[second] for _, second in CROSS] + [jnp.zeros((8,)...  7.84 us
    pallas_call x1, Pallas kernels, pack(): pl.pallas_call(functools.partial(pack_kernel, local_tiles, layers, slots)...  4.78 us
  transfers between devices with their start and end apart: 28, of which 10 were waited for; matrix products, arithmetic and copies ran while one was open for 11% of the time, Pallas kernels for 19%

profile of v4, /device:TPU:0, one launch (start us, length us, event | category | flops | bytes accessed | tf_op | source)
XLA Modules:
  0.0 221.4 jit_solution(1838092756475098273)
XLA Ops:
  1.7 4.1 %collective-permute-start = (bf16[512,256]{1,0:T(8,128)(2,1)S(1)}, bf16[512,256]{1,0:T(8,128)(2,1)S(1)}, u32[]{:S(2)}, u32[]{:S(2)}) collective-permute-start(bf16[512,256]{1,0:T(8,128)(2,1)S(1)} %bitcast.26), channel_id=1, source_target_pairs={{0,8},{1,9},{2,10},{3,11},{4,12},{5,13},{6,14},{7,15},{8,0},{9,1},... | collective-permute-start | bytes 786440 | tf_op jit(solution)/shard_map/ppermute | solution.py:434
  11.2 4.8 %pack.1 = (bf16[24,64,128]{2,1,0:T(8,128)(2,1)S(1)}, bf16[24,64,128]{2,1,0:T(8,128)(2,1)}, bf16[24,64,128]{2,1,0:T(8,128)(2,1)}, bf16[24,64,128]{2,1,0:T(8,128)(...) custom-call(s32[1]{0:T(128)} %bitcast.3.here, ...), custom_call_target="tpu_custom_call" | custom-call | tf_op jit(solution)/shard_map/pack/pallas_call | solution.py:96
  27.4 30.3 %collective-permute-done.1 = bf16[1024,256]{1,0:T(8,128)(2,1)S(1)} collective-permute-done((bf16[1024,256]{1,0:T(8,128)(2,1)S(1)}, bf16[1024,256]{1,0:T(8,128)(2,1)S(1)}, u32[]{:S(2)}, u32[]{:S(2)}) %collective-permute-start.1) | collective-permute-done | bytes 524320 | tf_op jit(solution)/shard_map/ppermute | solution.py:434
  65.6 7.8 %concatenate.27 = bf16[32,128,256]{2,0,1:T(8,128)(2,1)S(1)} concatenate(bf16[4,128,256]{2,0,1:T(4,128)(2,1)S(1)} %get-tuple-element.117, bf16[4,128,256]{2,0,1:T(4,128)(2,1)} %get-tuple-element.116, bf16[4,128,256]{2,0,1:T(4,128)(2,1)S(1)} %get-tuple-element.117, bf16[4,128,256]{2,0,1:T(4,128)(2,1)} %get-tuple-element.115, bf16[4,128,256]{2,0,1:T(4,128)(2,1)} %get-tuple-element.116, ...), dimensions={0} | concatenate | bytes 4194304 | tf_op jit(solution)/shard_map/concatenate | solution.py:547
  76.1 2.3 %constant_dynamic-update-slice_fusion.refs_15_ = bf16[64,64,256]{2,1,0:T(8,128)(2,1)} fusion(bf16[64,64,256]{2,1,0:T(8,128)(2,1)} %constant_dynamic-update-slice_fusion.1, bf16[32,64,256]{2,1,0:T(8,128)(2,1)} %collective-permute-done.3), kind=kLoop, calls=%fused_computation.28 | loop fusion | bytes 2097152 | tf_op jit(solution)/shard_map/concatenate | solution.py:563
  78.4 2.4 %constant_dynamic-update-slice_fusion.3 = bf16[4096,256]{1,0:T(8,128)(2,1)} fusion(bf16[2048,256]{1,0:T(8,128)(2,1)} %pad_maximum_fusion), kind=kLoop, calls=%fused_computation.31 | loop fusion | bytes 2097152
  80.8 14.0 %collective-permute-done.5.refs_11_ = f32[65,8,128]{2,1,0:T(8,128)S(1)} collective-permute-done((f32[65,8,128]{2,1,0:T(8,128)}, f32[65,8,128]{2,1,0:T(8,128)S(1)}, u32[]{:S(2)}, u32[]{:S(2)}) %collective-permute-start.5) | collective-permute-done | bytes 266272 | tf_op jit(solution)/shard_map/ppermute | solution.py:434
  94.8 2.4 %constant_dynamic-update-slice_fusion.2.refs_17_ = bf16[4096,256]{1,0:T(8,128)(2,1)} fusion(bf16[4096,256]{1,0:T(8,128)(2,1)} %constant_dynamic-update-slice_fusion.3, bf16[2048,256]{1,0:T(8,128)(2,1)} %collective-permute-done.4), kind=kLoop, calls=%fused_computation.30 | loop fusion | bytes 2097152 | tf_op jit(solution)/shard_map/concatenate | solution.py:561
  97.2 5.3 %collective-permute-start.15 = (bf16[24,64,128]{2,1,0:T(8,128)(2,1)}, bf16[24,64,128]{2,1,0:T(8,128)(2,1)}, u32[]{:S(2)}, u32[]{:S(2)}) collective-permute-start(bf16[24,64,128]{2,1,0:T(8,128)(2,1)} %get-tuple-element.90), channel_id=1, source_target_pairs={{0,4},{1,5},{2,6},{3,7},{4,0},{5,1},{6,2},{7,3},{8,12},{9,13},{10,... | collective-permute-start | bytes 1179656 | tf_op jit(solution)/shard_map/ppermute | solution.py:434
  102.5 2.4 %collective-permute-start.17 = (bf16[24,64,128]{2,1,0:T(8,128)(2,1)}, bf16[24,64,128]{2,1,0:T(8,128)(2,1)}, u32[]{:S(2)}, u32[]{:S(2)}) collective-permute-start(bf16[24,64,128]{2,1,0:T(8,128)(2,1)} %get-tuple-element.92), channel_id=1, source_target_pairs={{0,12},{1,13},{2,14},{3,15},{4,8},{5,9},{6,10},{7,11},{8,4},{9,5},... | collective-permute-start | bytes 1179656 | tf_op jit(solution)/shard_map/ppermute | solution.py:434
  109.1 34.0 %fit.3 = (f32[128,64,256]{2,1,0:T(8,128)S(1)}, f32[128,64,256]{2,1,0:T(8,128)S(1)}, bf16[128,64,256]{2,1,0:T(8,128)(2,1)S(1)}, bf16[8192,256]{1,0:T(8,128)(2,1)S(1)}) custom-call(s32[768]{0:T(1024)S(1)} %convert_element_type.49.refs_0_, s32[1536]{0:T(1024)S(1)} %reshape.52.refs_1_, s32[128]{0:T(128)S(1)} %get-tuple-element.120.refs_2_, ...), custom_call_target="tpu_custom_call" | custom-call | flops 3221225472 | bytes 1024 | tf_op jit(solution)/shard_map/fit/pallas_call | solution.py:397
  143.2 5.1 %collective-permute-start.12 = (bf16[16,64,128]{2,1,0:T(8,128)(2,1)S(1)}, bf16[16,64,128]{2,1,0:T(8,128)(2,1)S(1)}, u32[]{:S(2)}, u32[]{:S(2)}) collective-permute-start(bf16[16,64,128]{2,1,0:T(8,128)(2,1)S(1)} %copy-done.16), channel_id=1, source_target_pairs={{0,12},{1,13},{2,14},{3,15},{4,8},{5,9},{6,10},{7,11},{8,4},{9,5},... | collective-permute-start | bytes 786440 | tf_op jit(solution)/shard_map/ppermute | solution.py:434
  148.4 3.0 %fit.4 = (f32[128,64,256]{2,1,0:T(8,128)S(1)}, f32[128,64,256]{2,1,0:T(8,128)S(1)}) custom-call(s32[768]{0:T(1024)S(1)} %convert_element_type.49.refs_0_, s32[1536]{0:T(1024)S(1)} %reshape.52.refs_1_, s32[128]{0:T(128)S(1)} %get-tuple-element.120.refs_2_, s32[128]{0:T(128)S(1)} %get-tuple-element.121.refs_3_, ...), custom_call_target="tpu_custom_call", output_to_operand_aliasing={{0}: (17, {}), {1}: (18, {})} | custom-call | flops 3221225472 | bytes 1024 | tf_op jit(solution)/shard_map/fit/pallas_call | solution.py:397
  151.4 6.3 %collective-permute-done.11.refs_7_ = bf16[16,64,128]{2,1,0:T(8,128)(2,1)S(1)} collective-permute-done((bf16[16,64,128]{2,1,0:T(8,128)(2,1)}, bf16[16,64,128]{2,1,0:T(8,128)(2,1)S(1)}, u32[]{:S(2)}, u32[]{:S(2)}) %collective-permute-start.11) | collective-permute-done | bytes 262176 | tf_op jit(solution)/shard_map/ppermute | solution.py:434
  157.8 2.7 %fit.5 = (f32[128,64,256]{2,1,0:T(8,128)S(1)}, f32[128,64,256]{2,1,0:T(8,128)S(1)}, bf16[64,64,256]{2,1,0:T(8,128)(2,1)S(1)}, bf16[32,64,256]{2,1,0:T(8,128)(2,1)S(1)}, bf16[32,64,256]{2,1,0:T(8,128)(2,1)S(1)}) custom-call(s32[768]{0:T(1024)S(1)} %convert_element_type.49.refs_0_, ...), custom_call_target="tpu_custom_call", output_to_operand_aliasing={{0}: (17, {}), {1}: (18, {})} | custom-call | flops 2147483648 | bytes 1024 | tf_op jit(solution)/shard_map/fit/pallas_call | solution.py:397
  160.6 4.1 %collective-permute-done.18 = bf16[64,64,256]{2,1,0:T(8,128)(2,1)S(1)} collective-permute-done((bf16[64,64,256]{2,1,0:T(8,128)(2,1)S(1)}, bf16[64,64,256]{2,1,0:T(8,128)(2,1)S(1)}, u32[]{:S(2)}, u32[]{:S(2)}) %collective-permute-start.18) | collective-permute-done | bytes 2097184 | tf_op jit(solution)/shard_map/ppermute | solution.py:434
  166.5 10.0 %collective-permute-start.22 = (bf16[16,64,256]{2,1,0:T(8,128)(2,1)S(1)}, bf16[16,64,256]{2,1,0:T(8,128)(2,1)S(1)}, u32[]{:S(2)}, u32[]{:S(2)}) collective-permute-start(bf16[16,64,256]{2,1,0:T(8,128)(2,1)S(1)} %get-tuple-element.110), channel_id=1, source_target_pairs={{0,4},{1,5},{2,6},{3,7},{4,0},{5,1},{6,2},{7,3},{8,12},{9,13},{10,... | collective-permute-start | bytes 1572872 | tf_op jit(solution)/shard_map/ppermute | solution.py:434
  176.6 3.3 %collective-permute-done.19 = bf16[16,64,256]{2,1,0:T(8,128)(2,1)S(1)} collective-permute-done((bf16[16,64,256]{2,1,0:T(8,128)(2,1)S(1)}, bf16[16,64,256]{2,1,0:T(8,128)(2,1)S(1)}, u32[]{:S(2)}, u32[]{:S(2)}) %collective-permute-start.19) | collective-permute-done | bytes 524320 | tf_op jit(solution)/shard_map/ppermute | solution.py:434
  180.1 8.8 %collective-permute-done.22 = bf16[16,64,256]{2,1,0:T(8,128)(2,1)S(1)} collective-permute-done((bf16[16,64,256]{2,1,0:T(8,128)(2,1)S(1)}, bf16[16,64,256]{2,1,0:T(8,128)(2,1)S(1)}, u32[]{:S(2)}, u32[]{:S(2)}) %collective-permute-start.22) | collective-permute-done | bytes 524320 | tf_op jit(solution)/shard_map/ppermute | solution.py:434
  189.1 1.8 collective-permute-start.20
  191.4 6.3 %collective-permute-done.20 = bf16[8,64,256]{2,1,0:T(8,128)(2,1)S(1)} collective-permute-done((bf16[8,64,256]{2,1,0:T(8,128)(2,1)S(1)}, bf16[8,64,256]{2,1,0:T(8,128)(2,1)S(1)}, u32[]{:S(2)}, u32[]{:S(2)}) %collective-permute-start.20) | collective-permute-done | bytes 262176 | tf_op jit(solution)/shard_map/ppermute | solution.py:434
  198.6 9.8 %collective-permute-done.23 = bf16[8,64,256]{2,1,0:T(8,128)(2,1)S(1)} collective-permute-done((bf16[8,64,256]{2,1,0:T(8,128)(2,1)S(1)}, bf16[8,64,256]{2,1,0:T(8,128)(2,1)S(1)}, u32[]{:S(2)}, u32[]{:S(2)}) %collective-permute-start.23) | collective-permute-done | bytes 262176 | tf_op jit(solution)/shard_map/ppermute | solution.py:434
  210.7 8.0 %collective-permute-done.24 = bf16[4,64,256]{2,1,0:T(8,128)(2,1)S(1)} collective-permute-done((bf16[4,64,256]{2,1,0:T(8,128)(2,1)S(1)}, bf16[4,64,256]{2,1,0:T(8,128)(2,1)S(1)}, u32[]{:S(2)}, u32[]{:S(2)}) %collective-permute-start.24) | collective-permute-done | bytes 131104 | tf_op jit(solution)/shard_map/ppermute | solution.py:434
  219.5 1.8 convert_add_fusion.1
  (124 shorter events, 39.3 us)
Async XLA Ops:
  1.7 22.6 %collective-permute-start = (bf16[512,256]{1,0:T(8,128)(2,1)S(1)}, bf16[512,256]{1,0:T(8,128)(2,1)S(1)}, u32[]{:S(2)}, u32[]{:S(2)}) collective-permute-start(bf16[512,256]{1,0:T(8,128)(2,1)S(1)} %bitcast.26), channel_id=1, source_target_pairs={{0,8},{1,9},{2,10},{3,11},{4,12},{5,13},{6,14},{7,15},{8,0},{9,1},... | collective-permute-start | bytes 786440 | tf_op jit(solution)/shard_map/ppermute | solution.py:434
  5.8 54.3 %collective-permute-start.3 = (bf16[32,64,256]{2,1,0:T(8,128)(2,1)}, bf16[32,64,256]{2,1,0:T(8,128)(2,1)}, u32[]{:S(2)}, u32[]{:S(2)}) collective-permute-start(bf16[32,64,256]{2,1,0:T(8,128)(2,1)} %param.15), channel_id=1, source_target_pairs={{0,2},{1,3},{2,0},{3,1},{4,6},{5,7},{6,4},{7,5},{8,10},{9,11},{10,... | collective-permute-start | bytes 3145736 | tf_op jit(solution)/shard_map/ppermute | solution.py:434
  21.8 53.4 %collective-permute-start.7 = (bf16[24,64,128]{2,1,0:T(8,128)(2,1)}, bf16[24,64,128]{2,1,0:T(8,128)(2,1)}, u32[]{:S(2)}, u32[]{:S(2)}) collective-permute-start(bf16[24,64,128]{2,1,0:T(8,128)(2,1)} %get-tuple-element.66), channel_id=1, source_target_pairs={{0,4},{1,5},{2,6},{3,7},{4,0},{5,1},{6,2},{7,3},{8,12},{9,13},{10,... | collective-permute-start | bytes 1179656 | tf_op jit(solution)/shard_map/ppermute | solution.py:434
  23.4 57.4 %collective-permute-start.8 = (bf16[24,64,128]{2,1,0:T(8,128)(2,1)}, bf16[24,64,128]{2,1,0:T(8,128)(2,1)}, u32[]{:S(2)}, u32[]{:S(2)}) collective-permute-start(bf16[24,64,128]{2,1,0:T(8,128)(2,1)} %get-tuple-element.67), channel_id=1, source_target_pairs={{0,8},{1,9},{2,10},{3,11},{4,12},{5,13},{6,14},{7,15},{8,0},{9,1},... | collective-permute-start | bytes 1179656 | tf_op jit(solution)/shard_map/ppermute | solution.py:434
  24.3 35.8 %collective-permute-start.2 = (f32[65,8,128]{2,1,0:T(8,128)S(1)}, f32[65,8,128]{2,1,0:T(8,128)S(1)}, u32[]{:S(2)}, u32[]{:S(2)}) collective-permute-start(f32[65,8,128]{2,1,0:T(8,128)S(1)} %get-tuple-element.59), channel_id=1, source_target_pairs={{0,4},{1,5},{2,6},{3,7},{4,0},{5,1},{6,2},{7,3},{8,12},{9,13},{10,... | collective-permute-start | bytes 798728 | tf_op jit(solution)/shard_map/ppermute | solution.py:434
  24.8 32.9 %collective-permute-start.1 = (bf16[1024,256]{1,0:T(8,128)(2,1)S(1)}, bf16[1024,256]{1,0:T(8,128)(2,1)S(1)}, u32[]{:S(2)}, u32[]{:S(2)}) collective-permute-start(bf16[1024,256]{1,0:T(8,128)(2,1)S(1)} %pad_maximum_fusion.1), channel_id=1, source_target_pairs={{0,4},{1,5},{2,6},{3,7},{4,0},{5,1},{6,2},{7,3},{8,12},{9,13},{10,... | collective-permute-start | bytes 1572872 | tf_op jit(solution)/shard_map/ppermute | solution.py:434
  57.7 23.1 %collective-permute-start.9 = (bf16[24,64,128]{2,1,0:T(8,128)(2,1)}, bf16[24,64,128]{2,1,0:T(8,128)(2,1)}, u32[]{:S(2)}, u32[]{:S(2)}) collective-permute-start(bf16[24,64,128]{2,1,0:T(8,128)(2,1)} %get-tuple-element.68), channel_id=1, source_target_pairs={{0,12},{1,13},{2,14},{3,15},{4,8},{5,9},{6,10},{7,11},{8,4},{9,5},... | collective-permute-start | bytes 1179656 | tf_op jit(solution)/shard_map/ppermute | solution.py:434
  60.1 34.7 %collective-permute-start.4 = (bf16[2048,256]{1,0:T(8,128)(2,1)}, bf16[2048,256]{1,0:T(8,128)(2,1)}, u32[]{:S(2)}, u32[]{:S(2)}) collective-permute-start(bf16[2048,256]{1,0:T(8,128)(2,1)} %pad_maximum_fusion), channel_id=1, source_target_pairs={{0,2},{1,3},{2,0},{3,1},{4,6},{5,7},{6,4},{7,5},{8,10},{9,11},{10,... | collective-permute-start | bytes 3145736 | tf_op jit(solution)/shard_map/ppermute | solution.py:434
  73.5 21.3 %collective-permute-start.5 = (f32[65,8,128]{2,1,0:T(8,128)}, f32[65,8,128]{2,1,0:T(8,128)S(1)}, u32[]{:S(2)}, u32[]{:S(2)}) collective-permute-start(f32[65,8,128]{2,1,0:T(8,128)} %copy-done.14), channel_id=1, source_target_pairs={{0,8},{1,9},{2,10},{3,11},{4,12},{5,13},{6,14},{7,15},{8,0},{9,1},... | collective-permute-start | bytes 798728 | tf_op jit(solution)/shard_map/ppermute | solution.py:434
  75.2 19.6 %collective-permute-start.6 = (f32[65,8,128]{2,1,0:T(8,128)}, f32[65,8,128]{2,1,0:T(8,128)S(1)}, u32[]{:S(2)}, u32[]{:S(2)}) collective-permute-start(f32[65,8,128]{2,1,0:T(8,128)} %copy-done.13), channel_id=1, source_target_pairs={{0,12},{1,13},{2,14},{3,15},{4,8},{5,9},{6,10},{7,11},{8,4},{9,5},... | collective-permute-start | bytes 798728 | tf_op jit(solution)/shard_map/ppermute | solution.py:434
  80.8 24.4 %collective-permute-start.13 = (bf16[64,64,256]{2,1,0:T(8,128)(2,1)}, bf16[64,64,256]{2,1,0:T(8,128)(2,1)}, u32[]{:S(2)}, u32[]{:S(2)}) collective-permute-start(bf16[64,64,256]{2,1,0:T(8,128)(2,1)} %constant_dynamic-update-slice_fusion.refs_15_), channel_id=1, source_target_pairs={{0,1},{1,0},{2,3},{3,2},{4,5},{5,4},{6,7},{7,6},{8,9},{9,8},{10,11... | collective-permute-start | bytes 6291464 | tf_op jit(solution)/shard_map/ppermute | solution.py:434
  97.2 46.0 %collective-permute-start.15 = (bf16[24,64,128]{2,1,0:T(8,128)(2,1)}, bf16[24,64,128]{2,1,0:T(8,128)(2,1)}, u32[]{:S(2)}, u32[]{:S(2)}) collective-permute-start(bf16[24,64,128]{2,1,0:T(8,128)(2,1)} %get-tuple-element.90), channel_id=1, source_target_pairs={{0,4},{1,5},{2,6},{3,7},{4,0},{5,1},{6,2},{7,3},{8,12},{9,13},{10,... | collective-permute-start | bytes 1179656 | tf_op jit(solution)/shard_map/ppermute | solution.py:434
  102.5 45.9 %collective-permute-start.16 = (bf16[24,64,128]{2,1,0:T(8,128)(2,1)}, bf16[24,64,128]{2,1,0:T(8,128)(2,1)}, u32[]{:S(2)}, u32[]{:S(2)}) collective-permute-start(bf16[24,64,128]{2,1,0:T(8,128)(2,1)} %get-tuple-element.91), channel_id=1, source_target_pairs={{0,8},{1,9},{2,10},{3,11},{4,12},{5,13},{6,14},{7,15},{8,0},{9,1},... | collective-permute-start | bytes 1179656 | tf_op jit(solution)/shard_map/ppermute | solution.py:434
  102.5 45.9 %collective-permute-start.17 = (bf16[24,64,128]{2,1,0:T(8,128)(2,1)}, bf16[24,64,128]{2,1,0:T(8,128)(2,1)}, u32[]{:S(2)}, u32[]{:S(2)}) collective-permute-start(bf16[24,64,128]{2,1,0:T(8,128)(2,1)} %get-tuple-element.92), channel_id=1, source_target_pairs={{0,12},{1,13},{2,14},{3,15},{4,8},{5,9},{6,10},{7,11},{8,4},{9,5},... | collective-permute-start | bytes 1179656 | tf_op jit(solution)/shard_map/ppermute | solution.py:434
  105.2 46.3 %collective-permute-start.10 = (bf16[16,64,128]{2,1,0:T(8,128)(2,1)}, bf16[16,64,128]{2,1,0:T(8,128)(2,1)S(1)}, u32[]{:S(2)}, u32[]{:S(2)}) collective-permute-start(bf16[16,64,128]{2,1,0:T(8,128)(2,1)} %copy-done.18), channel_id=1, source_target_pairs={{0,4},{1,5},{2,6},{3,7},{4,0},{5,1},{6,2},{7,3},{8,12},{9,13},{10,... | collective-permute-start | bytes 786440 | tf_op jit(solution)/shard_map/ppermute | solution.py:434
  106.3 51.5 %collective-permute-start.11 = (bf16[16,64,128]{2,1,0:T(8,128)(2,1)}, bf16[16,64,128]{2,1,0:T(8,128)(2,1)S(1)}, u32[]{:S(2)}, u32[]{:S(2)}) collective-permute-start(bf16[16,64,128]{2,1,0:T(8,128)(2,1)} %copy-done.17), channel_id=1, source_target_pairs={{0,8},{1,9},{2,10},{3,11},{4,12},{5,13},{6,14},{7,15},{8,0},{9,1},... | collective-permute-start | bytes 786440 | tf_op jit(solution)/shard_map/ppermute | solution.py:434
  143.2 14.6 %collective-permute-start.12 = (bf16[16,64,128]{2,1,0:T(8,128)(2,1)S(1)}, bf16[16,64,128]{2,1,0:T(8,128)(2,1)S(1)}, u32[]{:S(2)}, u32[]{:S(2)}) collective-permute-start(bf16[16,64,128]{2,1,0:T(8,128)(2,1)S(1)} %copy-done.16), channel_id=1, source_target_pairs={{0,12},{1,13},{2,14},{3,15},{4,8},{5,9},{6,10},{7,11},{8,4},{9,5},... | collective-permute-start | bytes 786440 | tf_op jit(solution)/shard_map/ppermute | solution.py:434
  165.9 14.0 %collective-permute-start.19 = (bf16[16,64,256]{2,1,0:T(8,128)(2,1)S(1)}, bf16[16,64,256]{2,1,0:T(8,128)(2,1)S(1)}, u32[]{:S(2)}, u32[]{:S(2)}) collective-permute-start(bf16[16,64,256]{2,1,0:T(8,128)(2,1)S(1)} %get-tuple-element.111), channel_id=1, source_target_pairs={{0,2},{1,3},{2,0},{3,1},{4,6},{5,7},{6,4},{7,5},{8,10},{9,11},{10,... | collective-permute-start | bytes 1572872 | tf_op jit(solution)/shard_map/ppermute | solution.py:434
  166.5 24.5 %collective-permute-start.26 = (bf16[32,64,256]{2,1,0:T(8,128)(2,1)S(1)}, bf16[32,64,256]{2,1,0:T(8,128)(2,1)S(1)}, u32[]{:S(2)}, u32[]{:S(2)}) collective-permute-start(bf16[32,64,256]{2,1,0:T(8,128)(2,1)S(1)} %get-tuple-element.104), channel_id=1, source_target_pairs={{0,1},{1,0},{2,3},{3,2},{4,5},{5,4},{6,7},{7,6},{8,9},{9,8},{10,11... | collective-permute-start | bytes 3145736 | tf_op jit(solution)/shard_map/ppermute | solution.py:434
  166.5 22.5 %collective-permute-start.22 = (bf16[16,64,256]{2,1,0:T(8,128)(2,1)S(1)}, bf16[16,64,256]{2,1,0:T(8,128)(2,1)S(1)}, u32[]{:S(2)}, u32[]{:S(2)}) collective-permute-start(bf16[16,64,256]{2,1,0:T(8,128)(2,1)S(1)} %get-tuple-element.110), channel_id=1, source_target_pairs={{0,4},{1,5},{2,6},{3,7},{4,0},{5,1},{6,2},{7,3},{8,12},{9,13},{10,... | collective-permute-start | bytes 1572872 | tf_op jit(solution)/shard_map/ppermute | solution.py:434
  176.4 43.1 %collective-permute-start.25 = (bf16[32,64,256]{2,1,0:T(8,128)(2,1)S(1)}, bf16[32,64,256]{2,1,0:T(8,128)(2,1)S(1)}, u32[]{:S(2)}, u32[]{:S(2)}) collective-permute-start(bf16[32,64,256]{2,1,0:T(8,128)(2,1)S(1)} %get-tuple-element.103), channel_id=1, source_target_pairs={{0,1},{1,0},{2,3},{3,2},{4,5},{5,4},{6,7},{7,6},{8,9},{9,8},{10,11... | collective-permute-start | bytes 3145736 | tf_op jit(solution)/shard_map/ppermute | solution.py:434
  190.9 17.5 %collective-permute-start.23 = (bf16[8,64,256]{2,1,0:T(8,128)(2,1)S(1)}, bf16[8,64,256]{2,1,0:T(8,128)(2,1)S(1)}, u32[]{:S(2)}, u32[]{:S(2)}) collective-permute-start(bf16[8,64,256]{2,1,0:T(8,128)(2,1)S(1)} %slice.131), channel_id=1, source_target_pairs={{0,8},{1,9},{2,10},{3,11},{4,12},{5,13},{6,14},{7,15},{8,0},{9,1},... | collective-permute-start | bytes 786440 | tf_op jit(solution)/shard_map/ppermute | solution.py:434
  191.3 28.2 %collective-permute-start.27 = (bf16[32,64,256]{2,1,0:T(8,128)(2,1)S(1)}, bf16[32,64,256]{2,1,0:T(8,128)(2,1)S(1)}, u32[]{:S(2)}, u32[]{:S(2)}) collective-permute-start(bf16[32,64,256]{2,1,0:T(8,128)(2,1)S(1)} %add_convert_fusion), channel_id=1, source_target_pairs={{0,2},{1,3},{2,0},{3,1},{4,6},{5,7},{6,4},{7,5},{8,10},{9,11},{10,... | collective-permute-start | bytes 3145736 | tf_op jit(solution)/shard_map/ppermute | solution.py:434
  197.8 12.8 %collective-permute-start.21 = (bf16[4,64,256]{2,1,0:T(8,128)(2,1)S(1)}, bf16[4,64,256]{2,1,0:T(8,128)(2,1)S(1)}, u32[]{:S(2)}, u32[]{:S(2)}) collective-permute-start(bf16[4,64,256]{2,1,0:T(8,128)(2,1)S(1)} %slice.134), channel_id=1, source_target_pairs={{0,8},{1,9},{2,10},{3,11},{4,12},{5,13},{6,14},{7,15},{8,0},{9,1},... | collective-permute-start | bytes 393224 | tf_op jit(solution)/shard_map/ppermute | solution.py:434
  (28 other events, 206.6 us)

commit v5 on v4

--- a/solution.py
+++ b/solution.py
@@ -111,7 +111,7 @@
             pltpu.SMEM((layers,), jnp.int32),
             pltpu.SemaphoreType.DMA(((len(sizes) + 1) * layers,)),
         ],
-        compiler_params=pltpu.CompilerParams(vmem_limit_bytes=9 * MIB),
+        compiler_params=pltpu.CompilerParams(vmem_limit_bytes=10 * MIB),
         name="pack",
     )(here, block_tiles, block_counts, observations, pixel_geometry)
     rounds = len(sizes)
@@ -420,7 +420,7 @@
             pltpu.SemaphoreType.DMA((2 * layers * len(groups) + 2 * LAYER,)),
         ],
         input_output_aliases={} if first else {before: 0, before + 1: 1},
-        compiler_params=pltpu.CompilerParams(vmem_limit_bytes=6 * MIB),
+        compiler_params=pltpu.CompilerParams(vmem_limit_bytes=8 * MIB),
         cost_estimate=pl.CostEstimate(
             flops=layers * span * 4 * epochs * CHUNK * (NEAR + 1) * PBLK,
             bytes_accessed=1024,
@@ -551,13 +551,13 @@
     patches = jnp.stack([east, north, depth * depth])
     patches = jnp.swapaxes(patches.reshape(3, patch_blocks, PBLK), 0, 1)
     cutoffs = cutoff_lists.reshape(-1)
-    held, pix[1], across_screens = lax.optimization_barrier((held, pix[1], across_screens))
+    held, pix, across_screens = lax.optimization_barrier((held, pix, across_screens))
     across_screens, forms, patches, cutoffs = lax.optimization_barrier(
         (across_screens, forms, patches, cutoffs)
     )
     got = [exchange(o) for o in obs]
     across = partner(held, devices, PAIR)
-    across, pix, got[0] = lax.optimization_barrier((across, pix, got[0]))
+    across, got[0] = lax.optimization_barrier((across, got[0]))
     held = jnp.concatenate([held, across], axis=0)
     all_stress = [held, partner(held, devices, 1)]
     near_screens = jnp.concatenate([screens, across_screens], axis=0)

time: 225 us -> 237 us (1.053)
  the two profiles are of different devices: /device:TPU:0 before, /device:TPU:2 now
where the time goes in v5:
time: 237 us; the launch traced here: 238 us
  starting transfers between devices  72.4 us (31%)
  waiting for transfers between devices  70.2 us (30%)
  Pallas kernels  53.3 us (22%)
  local copies, waits for them, and re-layouts  33.1 us (14%)
  other arithmetic  8.41 us (4%)
    ppermute x28, starting transfers between devices, partner(): lax.ppermute(values, 'tile', [(i, i ^ distance) for i in range(devices)])  72.4 us
    ppermute x28, waiting for transfers between devices, partner(): lax.ppermute(values, 'tile', [(i, i ^ distance) for i in range(devices)])  70.2 us
    pallas_call x3, Pallas kernels, fit(): pl.pallas_call(functools.partial(fit_kernel, first, final, layers, slots,...  48.5 us
    unnamed x59, local copies, waits for them, and re-layouts  15.2 us
    concatenate x1, local copies, waits for them, and re-layouts, on_device(): jnp.concatenate([faces[second] for _, second in CROSS] + [jnp.zeros((8,)...  8.04 us
    pallas_call x1, Pallas kernels, pack(): pl.pallas_call(functools.partial(pack_kernel, local_tiles, layers, slots)...  4.83 us
  transfers between devices with their start and end apart: 28, of which 8 were waited for; matrix products, arithmetic and copies ran while one was open for 11% of the time, Pallas kernels for 21%

profile of v5, /device:TPU:2, one launch (start us, length us, event | category | flops | bytes accessed | tf_op | source)
XLA Modules:
  0.0 238.4 jit_solution(1886605622172081757)
XLA Ops:
  1.7 2.7 %collective-permute-start = (bf16[512,256]{1,0:T(8,128)(2,1)S(1)}, bf16[512,256]{1,0:T(8,128)(2,1)S(1)}, u32[]{:S(2)}, u32[]{:S(2)}) collective-permute-start(bf16[512,256]{1,0:T(8,128)(2,1)S(1)} %bitcast.26), channel_id=1, source_target_pairs={{0,8},{1,9},{2,10},{3,11},{4,12},{5,13},{6,14},{7,15},{8,0},{9,1},... | collective-permute-start | bytes 786440 | tf_op jit(solution)/shard_map/ppermute | solution.py:434
  9.8 4.8 %pack.1 = (bf16[24,64,128]{2,1,0:T(8,128)(2,1)S(1)}, bf16[24,64,128]{2,1,0:T(8,128)(2,1)}, bf16[24,64,128]{2,1,0:T(8,128)(2,1)}, bf16[24,64,128]{2,1,0:T(8,128)(...) custom-call(s32[1]{0:T(128)} %bitcast.3.here, ...), custom_call_target="tpu_custom_call" | custom-call | tf_op jit(solution)/shard_map/pack/pallas_call | solution.py:96
  23.6 24.1 %collective-permute-done.1 = bf16[1024,256]{1,0:T(8,128)(2,1)S(1)} collective-permute-done((bf16[1024,256]{1,0:T(8,128)(2,1)S(1)}, bf16[1024,256]{1,0:T(8,128)(2,1)S(1)}, u32[]{:S(2)}, u32[]{:S(2)}) %collective-permute-start.1) | collective-permute-done | bytes 524320 | tf_op jit(solution)/shard_map/ppermute | solution.py:434
  50.4 2.0 collective-permute-start.11
  59.2 8.0 %concatenate.27 = bf16[32,128,256]{2,0,1:T(8,128)(2,1)S(1)} concatenate(bf16[4,128,256]{2,0,1:T(4,128)(2,1)} %get-tuple-element.115, bf16[4,128,256]{2,0,1:T(4,128)(2,1)} %get-tuple-element.114, bf16[4,128,256]{2,0,1:T(4,128)(2,1)} %get-tuple-element.115, bf16[4,128,256]{2,0,1:T(4,128)(2,1)} %get-tuple-element.113, bf16[4,128,256]{2,0,1:T(4,128)(2,1)} %get-tuple-element.114, ...), dimensions={0} | concatenate | bytes 4194304 | tf_op jit(solution)/shard_map/concatenate | solution.py:547
  67.2 2.3 constant_dynamic-update-slice_fusion.refs_15_
  69.5 2.4 constant_dynamic-update-slice_fusion.3
  71.9 8.6 %collective-permute-done.11.refs_7_ = bf16[24,64,128]{2,1,0:T(8,128)(2,1)} collective-permute-done((bf16[24,64,128]{2,1,0:T(8,128)(2,1)}, bf16[24,64,128]{2,1,0:T(8,128)(2,1)}, u32[]{:S(2)}, u32[]{:S(2)}) %collective-permute-start.11) | collective-permute-done | bytes 393248 | tf_op jit(solution)/shard_map/ppermute | solution.py:434
  80.5 2.3 constant_dynamic-update-slice_fusion.2.refs_17_
  82.8 6.3 %collective-permute-start.15 = (bf16[24,64,128]{2,1,0:T(8,128)(2,1)}, bf16[24,64,128]{2,1,0:T(8,128)(2,1)}, u32[]{:S(2)}, u32[]{:S(2)}) collective-permute-start(bf16[24,64,128]{2,1,0:T(8,128)(2,1)} %get-tuple-element.88), channel_id=1, source_target_pairs={{0,4},{1,5},{2,6},{3,7},{4,0},{5,1},{6,2},{7,3},{8,12},{9,13},{10,... | collective-permute-start | bytes 1179656 | tf_op jit(solution)/shard_map/ppermute | solution.py:434
  94.2 2.2 collective-permute-start.7
  101.8 37.7 %fit.3 = (f32[128,64,256]{2,1,0:T(8,128)S(1)}, f32[128,64,256]{2,1,0:T(8,128)S(1)}, bf16[128,64,256]{2,1,0:T(8,128)(2,1)S(1)}, bf16[8192,256]{1,0:T(8,128)(2,1)S(1)}) custom-call(s32[768]{0:T(1024)S(1)} %convert_element_type.49.refs_0_, s32[1536]{0:T(1024)S(1)} %reshape.52.refs_1_, s32[128]{0:T(128)S(1)} %get-tuple-element.118.refs_2_, ...), custom_call_target="tpu_custom_call" | custom-call | flops 3221225472 | bytes 1024 | tf_op jit(solution)/shard_map/fit/pallas_call | solution.py:397
  141.1 8.0 %fit.4 = (f32[128,64,256]{2,1,0:T(8,128)S(1)}, f32[128,64,256]{2,1,0:T(8,128)S(1)}) custom-call(s32[768]{0:T(1024)S(1)} %convert_element_type.49.refs_0_, s32[1536]{0:T(1024)S(1)} %reshape.52.refs_1_, s32[128]{0:T(128)S(1)} %get-tuple-element.118.refs_2_, s32[128]{0:T(128)S(1)} %get-tuple-element.119.refs_3_, ...), custom_call_target="tpu_custom_call", output_to_operand_aliasing={{0}: (17, {}), {1}: (18, {})} | custom-call | flops 3221225472 | bytes 1024 | tf_op jit(solution)/shard_map/fit/pallas_call | solution.py:397
  149.2 2.7 %fit.5 = (f32[128,64,256]{2,1,0:T(8,128)S(1)}, f32[128,64,256]{2,1,0:T(8,128)S(1)}, bf16[64,64,256]{2,1,0:T(8,128)(2,1)S(1)}, bf16[32,64,256]{2,1,0:T(8,128)(2,1)S(1)}, bf16[32,64,256]{2,1,0:T(8,128)(2,1)S(1)}) custom-call(s32[768]{0:T(1024)S(1)} %convert_element_type.49.refs_0_, ...), custom_call_target="tpu_custom_call", output_to_operand_aliasing={{0}: (17, {}), {1}: (18, {})} | custom-call | flops 2147483648 | bytes 1024 | tf_op jit(solution)/shard_map/fit/pallas_call | solution.py:397
  152.0 4.1 %collective-permute-done.18 = bf16[64,64,256]{2,1,0:T(8,128)(2,1)S(1)} collective-permute-done((bf16[64,64,256]{2,1,0:T(8,128)(2,1)S(1)}, bf16[64,64,256]{2,1,0:T(8,128)(2,1)S(1)}, u32[]{:S(2)}, u32[]{:S(2)}) %collective-permute-start.18) | collective-permute-done | bytes 2097184 | tf_op jit(solution)/shard_map/ppermute | solution.py:434
  157.1 2.9 %collective-permute-start.19 = (bf16[16,64,256]{2,1,0:T(8,128)(2,1)S(1)}, bf16[16,64,256]{2,1,0:T(8,128)(2,1)S(1)}, u32[]{:S(2)}, u32[]{:S(2)}) collective-permute-start(bf16[16,64,256]{2,1,0:T(8,128)(2,1)S(1)} %get-tuple-element.109), channel_id=1, source_target_pairs={{0,2},{1,3},{2,0},{3,1},{4,6},{5,7},{6,4},{7,5},{8,10},{9,11},{10,... | collective-permute-start | bytes 1572872 | tf_op jit(solution)/shard_map/ppermute | solution.py:434
  160.5 11.7 %collective-permute-done.19 = bf16[16,64,256]{2,1,0:T(8,128)(2,1)S(1)} collective-permute-done((bf16[16,64,256]{2,1,0:T(8,128)(2,1)S(1)}, bf16[16,64,256]{2,1,0:T(8,128)(2,1)S(1)}, u32[]{:S(2)}, u32[]{:S(2)}) %collective-permute-start.19) | collective-permute-done | bytes 524320 | tf_op jit(solution)/shard_map/ppermute | solution.py:434
  172.4 1.9 collective-permute-done.22
  174.9 33.3 %collective-permute-start.23 = (bf16[8,64,256]{2,1,0:T(8,128)(2,1)S(1)}, bf16[8,64,256]{2,1,0:T(8,128)(2,1)S(1)}, u32[]{:S(2)}, u32[]{:S(2)}) collective-permute-start(bf16[8,64,256]{2,1,0:T(8,128)(2,1)S(1)} %slice.131), channel_id=1, source_target_pairs={{0,8},{1,9},{2,10},{3,11},{4,12},{5,13},{6,14},{7,15},{8,0},{9,1},... | collective-permute-start | bytes 786440 | tf_op jit(solution)/shard_map/ppermute | solution.py:434
  208.8 7.0 %collective-permute-start.21 = (bf16[4,64,256]{2,1,0:T(8,128)(2,1)S(1)}, bf16[4,64,256]{2,1,0:T(8,128)(2,1)S(1)}, u32[]{:S(2)}, u32[]{:S(2)}) collective-permute-start(bf16[4,64,256]{2,1,0:T(8,128)(2,1)S(1)} %slice.134), channel_id=1, source_target_pairs={{0,8},{1,9},{2,10},{3,11},{4,12},{5,13},{6,14},{7,15},{8,0},{9,1},... | collective-permute-start | bytes 393224 | tf_op jit(solution)/shard_map/ppermute | solution.py:434
  215.7 7.0 %collective-permute-done.23 = bf16[8,64,256]{2,1,0:T(8,128)(2,1)S(1)} collective-permute-done((bf16[8,64,256]{2,1,0:T(8,128)(2,1)S(1)}, bf16[8,64,256]{2,1,0:T(8,128)(2,1)S(1)}, u32[]{:S(2)}, u32[]{:S(2)}) %collective-permute-start.23) | collective-permute-done | bytes 262176 | tf_op jit(solution)/shard_map/ppermute | solution.py:434
  222.9 2.4 %collective-permute-done.21 = bf16[4,64,256]{2,1,0:T(8,128)(2,1)S(1)} collective-permute-done((bf16[4,64,256]{2,1,0:T(8,128)(2,1)S(1)}, bf16[4,64,256]{2,1,0:T(8,128)(2,1)S(1)}, u32[]{:S(2)}, u32[]{:S(2)}) %collective-permute-start.21) | collective-permute-done | bytes 131104 | tf_op jit(solution)/shard_map/ppermute | solution.py:434
  225.3 10.3 %collective-permute-done.24 = bf16[4,64,256]{2,1,0:T(8,128)(2,1)S(1)} collective-permute-done((bf16[4,64,256]{2,1,0:T(8,128)(2,1)S(1)}, bf16[4,64,256]{2,1,0:T(8,128)(2,1)S(1)}, u32[]{:S(2)}, u32[]{:S(2)}) %collective-permute-start.24) | collective-permute-done | bytes 131104 | tf_op jit(solution)/shard_map/ppermute | solution.py:434
  236.6 1.8 convert_add_fusion.1
  (134 shorter events, 40.8 us)
Async XLA Ops:
  1.7 15.8 %collective-permute-start = (bf16[512,256]{1,0:T(8,128)(2,1)S(1)}, bf16[512,256]{1,0:T(8,128)(2,1)S(1)}, u32[]{:S(2)}, u32[]{:S(2)}) collective-permute-start(bf16[512,256]{1,0:T(8,128)(2,1)S(1)} %bitcast.26), channel_id=1, source_target_pairs={{0,8},{1,9},{2,10},{3,11},{4,12},{5,13},{6,14},{7,15},{8,0},{9,1},... | collective-permute-start | bytes 786440 | tf_op jit(solution)/shard_map/ppermute | solution.py:434
  4.3 48.8 %collective-permute-start.5 = (bf16[32,64,256]{2,1,0:T(8,128)(2,1)}, bf16[32,64,256]{2,1,0:T(8,128)(2,1)}, u32[]{:S(2)}, u32[]{:S(2)}) collective-permute-start(bf16[32,64,256]{2,1,0:T(8,128)(2,1)} %param.15), channel_id=1, source_target_pairs={{0,2},{1,3},{2,0},{3,1},{4,6},{5,7},{6,4},{7,5},{8,10},{9,11},{10,... | collective-permute-start | bytes 3145736 | tf_op jit(solution)/shard_map/ppermute | solution.py:434
  17.4 32.9 %collective-permute-start.2 = (f32[65,8,128]{2,1,0:T(8,128)S(1)}, f32[65,8,128]{2,1,0:T(8,128)S(1)}, u32[]{:S(2)}, u32[]{:S(2)}) collective-permute-start(f32[65,8,128]{2,1,0:T(8,128)S(1)} %get-tuple-element.59), channel_id=1, source_target_pairs={{0,4},{1,5},{2,6},{3,7},{4,0},{5,1},{6,2},{7,3},{8,12},{9,13},{10,... | collective-permute-start | bytes 798728 | tf_op jit(solution)/shard_map/ppermute | solution.py:434
  19.0 33.4 %collective-permute-start.3 = (f32[65,8,128]{2,1,0:T(8,128)S(1)}, f32[65,8,128]{2,1,0:T(8,128)S(1)}, u32[]{:S(2)}, u32[]{:S(2)}) collective-permute-start(f32[65,8,128]{2,1,0:T(8,128)S(1)} %get-tuple-element.60), channel_id=1, source_target_pairs={{0,8},{1,9},{2,10},{3,11},{4,12},{5,13},{6,14},{7,15},{8,0},{9,1},... | collective-permute-start | bytes 798728 | tf_op jit(solution)/shard_map/ppermute | solution.py:434
  20.4 32.7 %collective-permute-start.4 = (f32[65,8,128]{2,1,0:T(8,128)S(1)}, f32[65,8,128]{2,1,0:T(8,128)S(1)}, u32[]{:S(2)}, u32[]{:S(2)}) collective-permute-start(f32[65,8,128]{2,1,0:T(8,128)S(1)} %get-tuple-element.61), channel_id=1, source_target_pairs={{0,12},{1,13},{2,14},{3,15},{4,8},{5,9},{6,10},{7,11},{8,4},{9,5},... | collective-permute-start | bytes 798728 | tf_op jit(solution)/shard_map/ppermute | solution.py:434
  21.8 25.8 %collective-permute-start.1 = (bf16[1024,256]{1,0:T(8,128)(2,1)S(1)}, bf16[1024,256]{1,0:T(8,128)(2,1)S(1)}, u32[]{:S(2)}, u32[]{:S(2)}) collective-permute-start(bf16[1024,256]{1,0:T(8,128)(2,1)S(1)} %pad_maximum_fusion.1), channel_id=1, source_target_pairs={{0,4},{1,5},{2,6},{3,7},{4,0},{5,1},{6,2},{7,3},{8,12},{9,13},{10,... | collective-permute-start | bytes 1572872 | tf_op jit(solution)/shard_map/ppermute | solution.py:434
  47.6 24.2 %collective-permute-start.10 = (bf16[24,64,128]{2,1,0:T(8,128)(2,1)}, bf16[24,64,128]{2,1,0:T(8,128)(2,1)}, u32[]{:S(2)}, u32[]{:S(2)}) collective-permute-start(bf16[24,64,128]{2,1,0:T(8,128)(2,1)} %get-tuple-element.76), channel_id=1, source_target_pairs={{0,4},{1,5},{2,6},{3,7},{4,0},{5,1},{6,2},{7,3},{8,12},{9,13},{10,... | collective-permute-start | bytes 1179656 | tf_op jit(solution)/shard_map/ppermute | solution.py:434
  50.4 30.1 %collective-permute-start.11 = (bf16[24,64,128]{2,1,0:T(8,128)(2,1)}, bf16[24,64,128]{2,1,0:T(8,128)(2,1)}, u32[]{:S(2)}, u32[]{:S(2)}) collective-permute-start(bf16[24,64,128]{2,1,0:T(8,128)(2,1)} %get-tuple-element.77), channel_id=1, source_target_pairs={{0,8},{1,9},{2,10},{3,11},{4,12},{5,13},{6,14},{7,15},{8,0},{9,1},... | collective-permute-start | bytes 1179656 | tf_op jit(solution)/shard_map/ppermute | solution.py:434
  52.4 28.1 %collective-permute-start.12 = (bf16[24,64,128]{2,1,0:T(8,128)(2,1)}, bf16[24,64,128]{2,1,0:T(8,128)(2,1)}, u32[]{:S(2)}, u32[]{:S(2)}) collective-permute-start(bf16[24,64,128]{2,1,0:T(8,128)(2,1)} %get-tuple-element.78), channel_id=1, source_target_pairs={{0,12},{1,13},{2,14},{3,15},{4,8},{5,9},{6,10},{7,11},{8,4},{9,5},... | collective-permute-start | bytes 1179656 | tf_op jit(solution)/shard_map/ppermute | solution.py:434
  53.1 27.4 %collective-permute-start.9 = (bf16[2048,256]{1,0:T(8,128)(2,1)}, bf16[2048,256]{1,0:T(8,128)(2,1)}, u32[]{:S(2)}, u32[]{:S(2)}) collective-permute-start(bf16[2048,256]{1,0:T(8,128)(2,1)} %pad_maximum_fusion), channel_id=1, source_target_pairs={{0,2},{1,3},{2,0},{3,1},{4,6},{5,7},{6,4},{7,5},{8,10},{9,11},{10,... | collective-permute-start | bytes 3145736 | tf_op jit(solution)/shard_map/ppermute | solution.py:434
  69.5 23.9 %collective-permute-start.13 = (bf16[64,64,256]{2,1,0:T(8,128)(2,1)}, bf16[64,64,256]{2,1,0:T(8,128)(2,1)}, u32[]{:S(2)}, u32[]{:S(2)}) collective-permute-start(bf16[64,64,256]{2,1,0:T(8,128)(2,1)} %constant_dynamic-update-slice_fusion.refs_15_), channel_id=1, source_target_pairs={{0,1},{1,0},{2,3},{3,2},{4,5},{5,4},{6,7},{7,6},{8,9},{9,8},{10,11... | collective-permute-start | bytes 6291464 | tf_op jit(solution)/shard_map/ppermute | solution.py:434
  82.8 56.8 %collective-permute-start.15 = (bf16[24,64,128]{2,1,0:T(8,128)(2,1)}, bf16[24,64,128]{2,1,0:T(8,128)(2,1)}, u32[]{:S(2)}, u32[]{:S(2)}) collective-permute-start(bf16[24,64,128]{2,1,0:T(8,128)(2,1)} %get-tuple-element.88), channel_id=1, source_target_pairs={{0,4},{1,5},{2,6},{3,7},{4,0},{5,1},{6,2},{7,3},{8,12},{9,13},{10,... | collective-permute-start | bytes 1179656 | tf_op jit(solution)/shard_map/ppermute | solution.py:434
  89.1 52.0 %collective-permute-start.16 = (bf16[24,64,128]{2,1,0:T(8,128)(2,1)}, bf16[24,64,128]{2,1,0:T(8,128)(2,1)}, u32[]{:S(2)}, u32[]{:S(2)}) collective-permute-start(bf16[24,64,128]{2,1,0:T(8,128)(2,1)} %get-tuple-element.89), channel_id=1, source_target_pairs={{0,8},{1,9},{2,10},{3,11},{4,12},{5,13},{6,14},{7,15},{8,0},{9,1},... | collective-permute-start | bytes 1179656 | tf_op jit(solution)/shard_map/ppermute | solution.py:434
  90.3 50.7 %collective-permute-start.17 = (bf16[24,64,128]{2,1,0:T(8,128)(2,1)}, bf16[24,64,128]{2,1,0:T(8,128)(2,1)}, u32[]{:S(2)}, u32[]{:S(2)}) collective-permute-start(bf16[24,64,128]{2,1,0:T(8,128)(2,1)} %get-tuple-element.90), channel_id=1, source_target_pairs={{0,12},{1,13},{2,14},{3,15},{4,8},{5,9},{6,10},{7,11},{8,4},{9,5},... | collective-permute-start | bytes 1179656 | tf_op jit(solution)/shard_map/ppermute | solution.py:434
  93.4 55.7 %collective-permute-start.6 = (bf16[16,64,128]{2,1,0:T(8,128)(2,1)}, bf16[16,64,128]{2,1,0:T(8,128)(2,1)S(1)}, u32[]{:S(2)}, u32[]{:S(2)}) collective-permute-start(bf16[16,64,128]{2,1,0:T(8,128)(2,1)} %copy-done.22), channel_id=1, source_target_pairs={{0,4},{1,5},{2,6},{3,7},{4,0},{5,1},{6,2},{7,3},{8,12},{9,13},{10,... | collective-permute-start | bytes 786440 | tf_op jit(solution)/shard_map/ppermute | solution.py:434
  94.2 55.0 %collective-permute-start.7 = (bf16[16,64,128]{2,1,0:T(8,128)(2,1)}, bf16[16,64,128]{2,1,0:T(8,128)(2,1)S(1)}, u32[]{:S(2)}, u32[]{:S(2)}) collective-permute-start(bf16[16,64,128]{2,1,0:T(8,128)(2,1)} %copy-done.21), channel_id=1, source_target_pairs={{0,8},{1,9},{2,10},{3,11},{4,12},{5,13},{6,14},{7,15},{8,0},{9,1},... | collective-permute-start | bytes 786440 | tf_op jit(solution)/shard_map/ppermute | solution.py:434
  157.1 15.1 %collective-permute-start.19 = (bf16[16,64,256]{2,1,0:T(8,128)(2,1)S(1)}, bf16[16,64,256]{2,1,0:T(8,128)(2,1)S(1)}, u32[]{:S(2)}, u32[]{:S(2)}) collective-permute-start(bf16[16,64,256]{2,1,0:T(8,128)(2,1)S(1)} %get-tuple-element.109), channel_id=1, source_target_pairs={{0,2},{1,3},{2,0},{3,1},{4,6},{5,7},{6,4},{7,5},{8,10},{9,11},{10,... | collective-permute-start | bytes 1572872 | tf_op jit(solution)/shard_map/ppermute | solution.py:434
  160.0 48.2 %collective-permute-start.26 = (bf16[32,64,256]{2,1,0:T(8,128)(2,1)S(1)}, bf16[32,64,256]{2,1,0:T(8,128)(2,1)S(1)}, u32[]{:S(2)}, u32[]{:S(2)}) collective-permute-start(bf16[32,64,256]{2,1,0:T(8,128)(2,1)S(1)} %get-tuple-element.102), channel_id=1, source_target_pairs={{0,1},{1,0},{2,3},{3,2},{4,5},{5,4},{6,7},{7,6},{8,9},{9,8},{10,11... | collective-permute-start | bytes 3145736 | tf_op jit(solution)/shard_map/ppermute | solution.py:434
  160.0 14.3 %collective-permute-start.22 = (bf16[16,64,256]{2,1,0:T(8,128)(2,1)S(1)}, bf16[16,64,256]{2,1,0:T(8,128)(2,1)S(1)}, u32[]{:S(2)}, u32[]{:S(2)}) collective-permute-start(bf16[16,64,256]{2,1,0:T(8,128)(2,1)S(1)} %get-tuple-element.108), channel_id=1, source_target_pairs={{0,4},{1,5},{2,6},{3,7},{4,0},{5,1},{6,2},{7,3},{8,12},{9,13},{10,... | collective-permute-start | bytes 1572872 | tf_op jit(solution)/shard_map/ppermute | solution.py:434
  160.0 76.6 %collective-permute-start.25 = (bf16[32,64,256]{2,1,0:T(8,128)(2,1)S(1)}, bf16[32,64,256]{2,1,0:T(8,128)(2,1)S(1)}, u32[]{:S(2)}, u32[]{:S(2)}) collective-permute-start(bf16[32,64,256]{2,1,0:T(8,128)(2,1)S(1)} %get-tuple-element.101), channel_id=1, source_target_pairs={{0,1},{1,0},{2,3},{3,2},{4,5},{5,4},{6,7},{7,6},{8,9},{9,8},{10,11... | collective-permute-start | bytes 3145736 | tf_op jit(solution)/shard_map/ppermute | solution.py:434
  174.5 34.2 %collective-permute-start.20 = (bf16[8,64,256]{2,1,0:T(8,128)(2,1)S(1)}, bf16[8,64,256]{2,1,0:T(8,128)(2,1)S(1)}, u32[]{:S(2)}, u32[]{:S(2)}) collective-permute-start(bf16[8,64,256]{2,1,0:T(8,128)(2,1)S(1)} %slice.132), channel_id=1, source_target_pairs={{0,4},{1,5},{2,6},{3,7},{4,0},{5,1},{6,2},{7,3},{8,12},{9,13},{10,... | collective-permute-start | bytes 786440 | tf_op jit(solution)/shard_map/ppermute | solution.py:434
  174.9 47.8 %collective-permute-start.23 = (bf16[8,64,256]{2,1,0:T(8,128)(2,1)S(1)}, bf16[8,64,256]{2,1,0:T(8,128)(2,1)S(1)}, u32[]{:S(2)}, u32[]{:S(2)}) collective-permute-start(bf16[8,64,256]{2,1,0:T(8,128)(2,1)S(1)} %slice.131), channel_id=1, source_target_pairs={{0,8},{1,9},{2,10},{3,11},{4,12},{5,13},{6,14},{7,15},{8,0},{9,1},... | collective-permute-start | bytes 786440 | tf_op jit(solution)/shard_map/ppermute | solution.py:434
  208.5 28.0 %collective-permute-start.27 = (bf16[32,64,256]{2,1,0:T(8,128)(2,1)S(1)}, bf16[32,64,256]{2,1,0:T(8,128)(2,1)S(1)}, u32[]{:S(2)}, u32[]{:S(2)}) collective-permute-start(bf16[32,64,256]{2,1,0:T(8,128)(2,1)S(1)} %add_convert_fusion), channel_id=1, source_target_pairs={{0,2},{1,3},{2,0},{3,1},{4,6},{5,7},{6,4},{7,5},{8,10},{9,11},{10,... | collective-permute-start | bytes 3145736 | tf_op jit(solution)/shard_map/ppermute | solution.py:434
  208.8 16.5 %collective-permute-start.21 = (bf16[4,64,256]{2,1,0:T(8,128)(2,1)S(1)}, bf16[4,64,256]{2,1,0:T(8,128)(2,1)S(1)}, u32[]{:S(2)}, u32[]{:S(2)}) collective-permute-start(bf16[4,64,256]{2,1,0:T(8,128)(2,1)S(1)} %slice.134), channel_id=1, source_target_pairs={{0,8},{1,9},{2,10},{3,11},{4,12},{5,13},{6,14},{7,15},{8,0},{9,1},... | collective-permute-start | bytes 393224 | tf_op jit(solution)/shard_map/ppermute | solution.py:434
  (33 other events, 420.7 us)

commit v6 on v5

--- a/solution.py
+++ b/solution.py
@@ -14,7 +14,7 @@
 LAYER = 4
 PAIR = 2
 NARROW = 3
-ROUNDS = (6, 6, 4)
+ROUNDS = (6, 10)
 MIB = 1 << 20
 TERMS = 32
 CROSS = ((0, 0), (0, 1), (1, 0), (0, 2), (1, 1), (2, 0))
@@ -147,8 +147,8 @@
     patches, forms = rest[:2]
     rest = rest[1:]
     if first:
-        screen_parts, stress_parts = rest[1 : 1 + PAIR], rest[1 + PAIR : 1 + 2 * PAIR]
-        rest = rest[1 + 2 * PAIR :]
+        screen_parts, stress_parts = rest[1 : 1 + LAYER], rest[1 + LAYER : 1 + 2 * LAYER]
+        rest = rest[1 + 2 * LAYER :]
         grad, screen_grad, screens, stress = rest[:4]
         rest = rest[4:]
     else:
@@ -179,7 +179,7 @@
             at += size
     if first:
         for parts, whole in ((screen_parts, screens), (stress_parts, stress)):
-            size = whole.shape[0] // PAIR
+            size = whole.shape[0] // LAYER
             for i, part in enumerate(parts):
                 loads.append((part, whole.at[pl.ds(i * size, size)]))
     loads = [pltpu.make_async_copy(a, b, sems.at[i]) for i, (a, b) in enumerate(loads)]
@@ -385,7 +385,7 @@
     if first:
         state = ()
         for parts in (screens, stress):
-            shape = (PAIR * parts[0].shape[0],) + parts[0].shape[1:]
+            shape = (LAYER * parts[0].shape[0],) + parts[0].shape[1:]
             out_shape.append(jax.ShapeDtypeStruct(shape, parts[0].dtype))
     else:
         screens, stress = [screens], [stress]
@@ -522,13 +522,14 @@
         got = [partner(parts[x], devices, x * LAYER) for x in range(layers - 1, 0, -1)]
         return [parts[0]] + got[::-1]
 
-    other, pix = lax.optimization_barrier((other, pix))
-    pix = exchange(pix)
     distance = devices // 2
     while distance >= LAYER:
         if distance < devices // 2:
             other = partner(held, devices, distance)
         held = jnp.concatenate([held, other], axis=0)
+        if distance == devices // 2:
+            held, pix = lax.optimization_barrier((held, pix))
+            pix = exchange(pix)
         distance //= 2
     patch_blocks = devices * local
     east, north, depth, compliance = patch_geometry
@@ -552,19 +553,22 @@
     patches = jnp.swapaxes(patches.reshape(3, patch_blocks, PBLK), 0, 1)
     cutoffs = cutoff_lists.reshape(-1)
     held, pix, across_screens = lax.optimization_barrier((held, pix, across_screens))
-    across_screens, forms, patches, cutoffs = lax.optimization_barrier(
-        (across_screens, forms, patches, cutoffs)
+    places, spots = block_places(devices, here, patch_blocks, local, epochs)
+    info = jnp.stack([p[slots, :3, :slots] for p in pix]).astype(jnp.int32).reshape(-1)
+    across_screens, forms, patches, cutoffs, info, places, spots = lax.optimization_barrier(
+        (across_screens, forms, patches, cutoffs, info, places, spots)
     )
     got = [exchange(o) for o in obs]
     across = partner(held, devices, PAIR)
     across, got[0] = lax.optimization_barrier((across, got[0]))
-    held = jnp.concatenate([held, across], axis=0)
-    all_stress = [held, partner(held, devices, 1)]
-    near_screens = jnp.concatenate([screens, across_screens], axis=0)
-    all_screens = [near_screens, partner(near_screens, devices, 1)]
-
-    places, spots = block_places(devices, here, patch_blocks, local, epochs)
-    info = jnp.stack([p[slots, :3, :slots] for p in pix]).astype(jnp.int32).reshape(-1)
+    all_stress = [held, across, partner(held, devices, 1), partner(across, devices, 1)]
+    all_screens = [
+        screens,
+        across_screens,
+        partner(screens, devices, 1),
+        partner(across_screens, devices, 1),
+    ]
+
     tables = (info, cutoffs, places, spots, origin)
 
     state = (

time: 237 us -> 221 us (0.932)
  the two profiles are of different devices: /device:TPU:2 before, /device:TPU:0 now
where the time goes in v6:
time: 221 us; the launch traced here: 225 us
  waiting for transfers between devices  79.3 us (36%)
  starting transfers between devices  66.8 us (30%)
  Pallas kernels  44.1 us (20%)
  local copies, waits for them, and re-layouts  23.6 us (11%)
  other arithmetic  10 us (5%)
    ppermute x27, waiting for transfers between devices, partner(): lax.ppermute(values, 'tile', [(i, i ^ distance) for i in range(devices)])  79.3 us
    ppermute x27, starting transfers between devices, partner(): lax.ppermute(values, 'tile', [(i, i ^ distance) for i in range(devices)])  66.8 us
    pallas_call x2, Pallas kernels, fit(): pl.pallas_call(functools.partial(fit_kernel, first, final, layers, slots,...  39.6 us
    unnamed x43, local copies, waits for them, and re-layouts  12.8 us
    concatenate x1, local copies, waits for them, and re-layouts, on_device(): jnp.concatenate([faces[second] for _, second in CROSS] + [jnp.zeros((8,)...  4.73 us
    pallas_call x1, Pallas kernels, pack(): pl.pallas_call(functools.partial(pack_kernel, local_tiles, layers, slots)...  4.53 us
  transfers between devices with their start and end apart: 27, of which 8 were waited for; matrix products, arithmetic and copies ran while one was open for 8% of the time, Pallas kernels for 17%

profile of v6, /device:TPU:0, one launch (start us, length us, event | category | flops | bytes accessed | tf_op | source)
XLA Modules:
  0.0 224.8 jit_solution(11417613013992043017)
XLA Ops:
  1.7 4.1 %collective-permute-start = (bf16[512,256]{1,0:T(8,128)(2,1)S(1)}, bf16[512,256]{1,0:T(8,128)(2,1)S(1)}, u32[]{:S(2)}, u32[]{:S(2)}) collective-permute-start(bf16[512,256]{1,0:T(8,128)(2,1)S(1)} %bitcast.27), channel_id=1, source_target_pairs={{0,8},{1,9},{2,10},{3,11},{4,12},{5,13},{6,14},{7,15},{8,0},{9,1},... | collective-permute-start | bytes 786440 | tf_op jit(solution)/shard_map/ppermute | solution.py:434
  11.2 4.5 %pack.1 = (bf16[24,64,128]{2,1,0:T(8,128)(2,1)S(1)}, bf16[24,64,128]{2,1,0:T(8,128)(2,1)}, bf16[24,64,128]{2,1,0:T(8,128)(2,1)}, bf16[24,64,128]{2,1,0:T(8,128)(...) custom-call(s32[1]{0:T(128)} %bitcast.3.here, ...), custom_call_target="tpu_custom_call" | custom-call | tf_op jit(solution)/shard_map/pack/pallas_call | solution.py:96
  21.9 2.4 %collective-permute-start.4 = (f32[65,8,128]{2,1,0:T(8,128)S(1)}, f32[65,8,128]{2,1,0:T(8,128)}, u32[]{:S(2)}, u32[]{:S(2)}) collective-permute-start(f32[65,8,128]{2,1,0:T(8,128)S(1)} %get-tuple-element.58), channel_id=1, source_target_pairs={{0,12},{1,13},{2,14},{3,15},{4,8},{5,9},{6,10},{7,11},{8,4},{9,5},... | collective-permute-start | bytes 798728 | tf_op jit(solution)/shard_map/ppermute | solution.py:434
  26.0 24.2 %collective-permute-done.1 = bf16[1024,256]{1,0:T(8,128)(2,1)S(1)} collective-permute-done((bf16[1024,256]{1,0:T(8,128)(2,1)S(1)}, bf16[1024,256]{1,0:T(8,128)(2,1)S(1)}, u32[]{:S(2)}, u32[]{:S(2)}) %collective-permute-start.1) | collective-permute-done | bytes 524320 | tf_op jit(solution)/shard_map/ppermute | solution.py:434
  51.2 1.7 collective-permute-start.10
  53.9 1.7 collective-permute-start.12
  61.2 4.7 %concatenate.20 = bf16[32,128,256]{2,0,1:T(8,128)(2,1)S(1)} concatenate(bf16[4,128,256]{2,0,1:T(4,128)(2,1)S(1)} %get-tuple-element.109, bf16[4,128,256]{2,0,1:T(4,128)(2,1)S(1)} %get-tuple-element.108, bf16[4,128,256]{2,0,1:T(4,128)(2,1)S(1)} %get-tuple-element.109, bf16[4,128,256]{2,0,1:T(4,128)(2,1)} %get-tuple-element.107, bf16[4,128,256]{2,0,1:T(4,128)(2,1)S(1)} %get-tuple-element.108, ...), dimensions={0} | concatenate | bytes 4194304 | tf_op jit(solution)/shard_map/concatenate | solution.py:548
  68.0 1.7 collective-permute-done.10.refs_6_
  69.7 13.2 %collective-permute-done.11.refs_7_ = bf16[24,64,128]{2,1,0:T(8,128)(2,1)} collective-permute-done((bf16[24,64,128]{2,1,0:T(8,128)(2,1)}, bf16[24,64,128]{2,1,0:T(8,128)(2,1)}, u32[]{:S(2)}, u32[]{:S(2)}) %collective-permute-start.11) | collective-permute-done | bytes 393248 | tf_op jit(solution)/shard_map/ppermute | solution.py:434
  83.5 7.8 %collective-permute-start.6 = (bf16[40,64,128]{2,1,0:T(8,128)(2,1)}, bf16[40,64,128]{2,1,0:T(8,128)(2,1)S(1)}, u32[]{:S(2)}, u32[]{:S(2)}) collective-permute-start(bf16[40,64,128]{2,1,0:T(8,128)(2,1)} %copy-done.16), channel_id=1, source_target_pairs={{0,4},{1,5},{2,6},{3,7},{4,0},{5,1},{6,2},{7,3},{8,12},{9,13},{10,... | collective-permute-start | bytes 1966088 | tf_op jit(solution)/shard_map/ppermute | solution.py:434
  91.2 2.4 %collective-permute-start.8 = (bf16[40,64,128]{2,1,0:T(8,128)(2,1)}, bf16[40,64,128]{2,1,0:T(8,128)(2,1)S(1)}, u32[]{:S(2)}, u32[]{:S(2)}) collective-permute-start(bf16[40,64,128]{2,1,0:T(8,128)(2,1)} %copy-done.14), channel_id=1, source_target_pairs={{0,12},{1,13},{2,14},{3,15},{4,8},{5,9},{6,10},{7,11},{8,4},{9,5},... | collective-permute-start | bytes 1966088 | tf_op jit(solution)/shard_map/ppermute | solution.py:434
  97.7 34.1 %fit.2 = (f32[128,64,256]{2,1,0:T(8,128)S(1)}, f32[128,64,256]{2,1,0:T(8,128)S(1)}, bf16[128,64,256]{2,1,0:T(8,128)(2,1)S(1)}, bf16[8192,256]{1,0:T(8,128)(2,1)S(1)}) custom-call(s32[768]{0:T(1024)S(1)} %convert_element_type.49.refs_0_, s32[1536]{0:T(1024)S(1)} %reshape.52.refs_1_, s32[128]{0:T(128)S(1)} %get-tuple-element.66.refs_2_, ...), custom_call_target="tpu_custom_call" | custom-call | flops 3221225472 | bytes 1024 | tf_op jit(solution)/shard_map/fit/pallas_call | solution.py:397
  131.9 6.2 %collective-permute-done.7.refs_7_ = bf16[40,64,128]{2,1,0:T(8,128)(2,1)S(1)} collective-permute-done((bf16[40,64,128]{2,1,0:T(8,128)(2,1)}, bf16[40,64,128]{2,1,0:T(8,128)(2,1)S(1)}, u32[]{:S(2)}, u32[]{:S(2)}) %collective-permute-start.7) | collective-permute-done | bytes 655392 | tf_op jit(solution)/shard_map/ppermute | solution.py:434
  138.1 5.4 %fit.3 = (f32[128,64,256]{2,1,0:T(8,128)S(1)}, f32[128,64,256]{2,1,0:T(8,128)S(1)}, bf16[64,64,256]{2,1,0:T(8,128)(2,1)S(1)}, bf16[32,64,256]{2,1,0:T(8,128)(2,1)S(1)}, bf16[32,64,256]{2,1,0:T(8,128)(2,1)S(1)}) custom-call(s32[768]{0:T(1024)S(1)} %convert_element_type.49.refs_0_, ...), custom_call_target="tpu_custom_call", output_to_operand_aliasing={{0}: (17, {}), {1}: (18, {})} | custom-call | flops 5368709120 | bytes 1024 | tf_op jit(solution)/shard_map/fit/pallas_call | solution.py:397
  145.5 4.2 %collective-permute-done.17 = bf16[64,64,256]{2,1,0:T(8,128)(2,1)S(1)} collective-permute-done((bf16[64,64,256]{2,1,0:T(8,128)(2,1)S(1)}, bf16[64,64,256]{2,1,0:T(8,128)(2,1)S(1)}, u32[]{:S(2)}, u32[]{:S(2)}) %collective-permute-start.17) | collective-permute-done | bytes 2097184 | tf_op jit(solution)/shard_map/ppermute | solution.py:434
  150.8 2.2 collective-permute-start.18
  153.1 12.9 %collective-permute-start.21 = (bf16[16,64,256]{2,1,0:T(8,128)(2,1)S(1)}, bf16[16,64,256]{2,1,0:T(8,128)(2,1)S(1)}, u32[]{:S(2)}, u32[]{:S(2)}) collective-permute-start(bf16[16,64,256]{2,1,0:T(8,128)(2,1)S(1)} %get-tuple-element.102), channel_id=1, source_target_pairs={{0,4},{1,5},{2,6},{3,7},{4,0},{5,1},{6,2},{7,3},{8,12},{9,13},{10,... | collective-permute-start | bytes 1572872 | tf_op jit(solution)/shard_map/ppermute | solution.py:434
  166.2 12.2 %collective-permute-done.21 = bf16[16,64,256]{2,1,0:T(8,128)(2,1)S(1)} collective-permute-done((bf16[16,64,256]{2,1,0:T(8,128)(2,1)S(1)}, bf16[16,64,256]{2,1,0:T(8,128)(2,1)S(1)}, u32[]{:S(2)}, u32[]{:S(2)}) %collective-permute-start.21) | collective-permute-done | bytes 524320 | tf_op jit(solution)/shard_map/ppermute | solution.py:434
  178.6 1.8 collective-permute-start.19
  180.4 14.6 %collective-permute-start.22 = (bf16[8,64,256]{2,1,0:T(8,128)(2,1)S(1)}, bf16[8,64,256]{2,1,0:T(8,128)(2,1)S(1)}, u32[]{:S(2)}, u32[]{:S(2)}) collective-permute-start(bf16[8,64,256]{2,1,0:T(8,128)(2,1)S(1)} %slice.131), channel_id=1, source_target_pairs={{0,8},{1,9},{2,10},{3,11},{4,12},{5,13},{6,14},{7,15},{8,0},{9,1},... | collective-permute-start | bytes 786440 | tf_op jit(solution)/shard_map/ppermute | solution.py:434
  196.5 6.7 %collective-permute-start.20 = (bf16[4,64,256]{2,1,0:T(8,128)(2,1)S(1)}, bf16[4,64,256]{2,1,0:T(8,128)(2,1)S(1)}, u32[]{:S(2)}, u32[]{:S(2)}) collective-permute-start(bf16[4,64,256]{2,1,0:T(8,128)(2,1)S(1)} %slice.134), channel_id=1, source_target_pairs={{0,8},{1,9},{2,10},{3,11},{4,12},{5,13},{6,14},{7,15},{8,0},{9,1},... | collective-permute-start | bytes 393224 | tf_op jit(solution)/shard_map/ppermute | solution.py:434
  204.4 7.6 %collective-permute-done.20 = bf16[4,64,256]{2,1,0:T(8,128)(2,1)S(1)} collective-permute-done((bf16[4,64,256]{2,1,0:T(8,128)(2,1)S(1)}, bf16[4,64,256]{2,1,0:T(8,128)(2,1)S(1)}, u32[]{:S(2)}, u32[]{:S(2)}) %collective-permute-start.20) | collective-permute-done | bytes 131104 | tf_op jit(solution)/shard_map/ppermute | solution.py:434
  212.0 10.0 %collective-permute-done.23 = bf16[4,64,256]{2,1,0:T(8,128)(2,1)S(1)} collective-permute-done((bf16[4,64,256]{2,1,0:T(8,128)(2,1)S(1)}, bf16[4,64,256]{2,1,0:T(8,128)(2,1)S(1)}, u32[]{:S(2)}, u32[]{:S(2)}) %collective-permute-start.23) | collective-permute-done | bytes 131104 | tf_op jit(solution)/shard_map/ppermute | solution.py:434
  223.0 1.8 convert_add_fusion.1
  (112 shorter events, 35.7 us)
Async XLA Ops:
  1.7 18.1 %collective-permute-start = (bf16[512,256]{1,0:T(8,128)(2,1)S(1)}, bf16[512,256]{1,0:T(8,128)(2,1)S(1)}, u32[]{:S(2)}, u32[]{:S(2)}) collective-permute-start(bf16[512,256]{1,0:T(8,128)(2,1)S(1)} %bitcast.27), channel_id=1, source_target_pairs={{0,8},{1,9},{2,10},{3,11},{4,12},{5,13},{6,14},{7,15},{8,0},{9,1},... | collective-permute-start | bytes 786440 | tf_op jit(solution)/shard_map/ppermute | solution.py:434
  5.8 49.8 %collective-permute-start.5 = (bf16[32,64,256]{2,1,0:T(8,128)(2,1)}, bf16[32,64,256]{2,1,0:T(8,128)(2,1)S(1)}, u32[]{:S(2)}, u32[]{:S(2)}) collective-permute-start(bf16[32,64,256]{2,1,0:T(8,128)(2,1)} %refs_15_.1), channel_id=1, source_target_pairs={{0,2},{1,3},{2,0},{3,1},{4,6},{5,7},{6,4},{7,5},{8,10},{9,11},{10,... | collective-permute-start | bytes 3145736 | tf_op jit(solution)/shard_map/ppermute | solution.py:434
  19.9 31.3 %collective-permute-start.2 = (f32[65,8,128]{2,1,0:T(8,128)S(1)}, f32[65,8,128]{2,1,0:T(8,128)S(1)}, u32[]{:S(2)}, u32[]{:S(2)}) collective-permute-start(f32[65,8,128]{2,1,0:T(8,128)S(1)} %get-tuple-element.56), channel_id=1, source_target_pairs={{0,4},{1,5},{2,6},{3,7},{4,0},{5,1},{6,2},{7,3},{8,12},{9,13},{10,... | collective-permute-start | bytes 798728 | tf_op jit(solution)/shard_map/ppermute | solution.py:434
  21.5 31.4 %collective-permute-start.3 = (f32[65,8,128]{2,1,0:T(8,128)S(1)}, f32[65,8,128]{2,1,0:T(8,128)S(1)}, u32[]{:S(2)}, u32[]{:S(2)}) collective-permute-start(f32[65,8,128]{2,1,0:T(8,128)S(1)} %get-tuple-element.57), channel_id=1, source_target_pairs={{0,8},{1,9},{2,10},{3,11},{4,12},{5,13},{6,14},{7,15},{8,0},{9,1},... | collective-permute-start | bytes 798728 | tf_op jit(solution)/shard_map/ppermute | solution.py:434
  21.9 32.0 %collective-permute-start.4 = (f32[65,8,128]{2,1,0:T(8,128)S(1)}, f32[65,8,128]{2,1,0:T(8,128)}, u32[]{:S(2)}, u32[]{:S(2)}) collective-permute-start(f32[65,8,128]{2,1,0:T(8,128)S(1)} %get-tuple-element.58), channel_id=1, source_target_pairs={{0,12},{1,13},{2,14},{3,15},{4,8},{5,9},{6,10},{7,11},{8,4},{9,5},... | collective-permute-start | bytes 798728 | tf_op jit(solution)/shard_map/ppermute | solution.py:434
  24.3 25.8 %collective-permute-start.1 = (bf16[1024,256]{1,0:T(8,128)(2,1)S(1)}, bf16[1024,256]{1,0:T(8,128)(2,1)S(1)}, u32[]{:S(2)}, u32[]{:S(2)}) collective-permute-start(bf16[1024,256]{1,0:T(8,128)(2,1)S(1)} %pad_maximum_fusion.1), channel_id=1, source_target_pairs={{0,4},{1,5},{2,6},{3,7},{4,0},{5,1},{6,2},{7,3},{8,12},{9,13},{10,... | collective-permute-start | bytes 1572872 | tf_op jit(solution)/shard_map/ppermute | solution.py:434
  50.2 41.1 %collective-permute-start.13 = (bf16[32,64,256]{2,1,0:T(8,128)(2,1)}, bf16[32,64,256]{2,1,0:T(8,128)(2,1)}, u32[]{:S(2)}, u32[]{:S(2)}) collective-permute-start(bf16[32,64,256]{2,1,0:T(8,128)(2,1)} %refs_15_.1), channel_id=1, source_target_pairs={{0,1},{1,0},{2,3},{3,2},{4,5},{5,4},{6,7},{7,6},{8,9},{9,8},{10,11... | collective-permute-start | bytes 3145736 | tf_op jit(solution)/shard_map/ppermute | solution.py:434
  51.2 18.5 %collective-permute-start.10 = (bf16[24,64,128]{2,1,0:T(8,128)(2,1)}, bf16[24,64,128]{2,1,0:T(8,128)(2,1)}, u32[]{:S(2)}, u32[]{:S(2)}) collective-permute-start(bf16[24,64,128]{2,1,0:T(8,128)(2,1)} %get-tuple-element.76), channel_id=1, source_target_pairs={{0,4},{1,5},{2,6},{3,7},{4,0},{5,1},{6,2},{7,3},{8,12},{9,13},{10,... | collective-permute-start | bytes 1179656 | tf_op jit(solution)/shard_map/ppermute | solution.py:434
  52.9 30.1 %collective-permute-start.11 = (bf16[24,64,128]{2,1,0:T(8,128)(2,1)}, bf16[24,64,128]{2,1,0:T(8,128)(2,1)}, u32[]{:S(2)}, u32[]{:S(2)}) collective-permute-start(bf16[24,64,128]{2,1,0:T(8,128)(2,1)} %get-tuple-element.77), channel_id=1, source_target_pairs={{0,8},{1,9},{2,10},{3,11},{4,12},{5,13},{6,14},{7,15},{8,0},{9,1},... | collective-permute-start | bytes 1179656 | tf_op jit(solution)/shard_map/ppermute | solution.py:434
  53.9 29.0 %collective-permute-start.12 = (bf16[24,64,128]{2,1,0:T(8,128)(2,1)}, bf16[24,64,128]{2,1,0:T(8,128)(2,1)}, u32[]{:S(2)}, u32[]{:S(2)}) collective-permute-start(bf16[24,64,128]{2,1,0:T(8,128)(2,1)} %get-tuple-element.78), channel_id=1, source_target_pairs={{0,12},{1,13},{2,14},{3,15},{4,8},{5,9},{6,10},{7,11},{8,4},{9,5},... | collective-permute-start | bytes 1179656 | tf_op jit(solution)/shard_map/ppermute | solution.py:434
  55.6 27.3 %collective-permute-start.9 = (bf16[2048,256]{1,0:T(8,128)(2,1)}, bf16[2048,256]{1,0:T(8,128)(2,1)}, u32[]{:S(2)}, u32[]{:S(2)}) collective-permute-start(bf16[2048,256]{1,0:T(8,128)(2,1)} %pad_maximum_fusion.refs_19_), channel_id=1, source_target_pairs={{0,2},{1,3},{2,0},{3,1},{4,6},{5,7},{6,4},{7,5},{8,10},{9,11},{10,... | collective-permute-start | bytes 3145736 | tf_op jit(solution)/shard_map/ppermute | solution.py:434
  69.7 21.5 %collective-permute-start.14 = (bf16[32,64,256]{2,1,0:T(8,128)(2,1)}, bf16[32,64,256]{2,1,0:T(8,128)(2,1)S(1)}, u32[]{:S(2)}, u32[]{:S(2)}) collective-permute-start(bf16[32,64,256]{2,1,0:T(8,128)(2,1)} %copy-done.8), channel_id=1, source_target_pairs={{0,1},{1,0},{2,3},{3,2},{4,5},{5,4},{6,7},{7,6},{8,9},{9,8},{10,11... | collective-permute-start | bytes 3145736 | tf_op jit(solution)/shard_map/ppermute | solution.py:434
  83.5 48.4 %collective-permute-start.6 = (bf16[40,64,128]{2,1,0:T(8,128)(2,1)}, bf16[40,64,128]{2,1,0:T(8,128)(2,1)S(1)}, u32[]{:S(2)}, u32[]{:S(2)}) collective-permute-start(bf16[40,64,128]{2,1,0:T(8,128)(2,1)} %copy-done.16), channel_id=1, source_target_pairs={{0,4},{1,5},{2,6},{3,7},{4,0},{5,1},{6,2},{7,3},{8,12},{9,13},{10,... | collective-permute-start | bytes 1966088 | tf_op jit(solution)/shard_map/ppermute | solution.py:434
  91.2 46.8 %collective-permute-start.7 = (bf16[40,64,128]{2,1,0:T(8,128)(2,1)}, bf16[40,64,128]{2,1,0:T(8,128)(2,1)S(1)}, u32[]{:S(2)}, u32[]{:S(2)}) collective-permute-start(bf16[40,64,128]{2,1,0:T(8,128)(2,1)} %copy-done.15), channel_id=1, source_target_pairs={{0,8},{1,9},{2,10},{3,11},{4,12},{5,13},{6,14},{7,15},{8,0},{9,1},... | collective-permute-start | bytes 1966088 | tf_op jit(solution)/shard_map/ppermute | solution.py:434
  91.2 46.8 %collective-permute-start.8 = (bf16[40,64,128]{2,1,0:T(8,128)(2,1)}, bf16[40,64,128]{2,1,0:T(8,128)(2,1)S(1)}, u32[]{:S(2)}, u32[]{:S(2)}) collective-permute-start(bf16[40,64,128]{2,1,0:T(8,128)(2,1)} %copy-done.14), channel_id=1, source_target_pairs={{0,12},{1,13},{2,14},{3,15},{4,8},{5,9},{6,10},{7,11},{8,4},{9,5},... | collective-permute-start | bytes 1966088 | tf_op jit(solution)/shard_map/ppermute | solution.py:434
  150.8 15.2 %collective-permute-start.18 = (bf16[16,64,256]{2,1,0:T(8,128)(2,1)S(1)}, bf16[16,64,256]{2,1,0:T(8,128)(2,1)S(1)}, u32[]{:S(2)}, u32[]{:S(2)}) collective-permute-start(bf16[16,64,256]{2,1,0:T(8,128)(2,1)S(1)} %get-tuple-element.103), channel_id=1, source_target_pairs={{0,2},{1,3},{2,0},{3,1},{4,6},{5,7},{6,4},{7,5},{8,10},{9,11},{10,... | collective-permute-start | bytes 1572872 | tf_op jit(solution)/shard_map/ppermute | solution.py:434
  153.0 41.9 %collective-permute-start.25 = (bf16[32,64,256]{2,1,0:T(8,128)(2,1)S(1)}, bf16[32,64,256]{2,1,0:T(8,128)(2,1)S(1)}, u32[]{:S(2)}, u32[]{:S(2)}) collective-permute-start(bf16[32,64,256]{2,1,0:T(8,128)(2,1)S(1)} %copy-done.13), channel_id=1, source_target_pairs={{0,1},{1,0},{2,3},{3,2},{4,5},{5,4},{6,7},{7,6},{8,9},{9,8},{10,11... | collective-permute-start | bytes 3145736 | tf_op jit(solution)/shard_map/ppermute | solution.py:434
  153.1 25.4 %collective-permute-start.21 = (bf16[16,64,256]{2,1,0:T(8,128)(2,1)S(1)}, bf16[16,64,256]{2,1,0:T(8,128)(2,1)S(1)}, u32[]{:S(2)}, u32[]{:S(2)}) collective-permute-start(bf16[16,64,256]{2,1,0:T(8,128)(2,1)S(1)} %get-tuple-element.102), channel_id=1, source_target_pairs={{0,4},{1,5},{2,6},{3,7},{4,0},{5,1},{6,2},{7,3},{8,12},{9,13},{10,... | collective-permute-start | bytes 1572872 | tf_op jit(solution)/shard_map/ppermute | solution.py:434
  166.0 57.0 %collective-permute-start.24 = (bf16[32,64,256]{2,1,0:T(8,128)(2,1)S(1)}, bf16[32,64,256]{2,1,0:T(8,128)(2,1)S(1)}, u32[]{:S(2)}, u32[]{:S(2)}) collective-permute-start(bf16[32,64,256]{2,1,0:T(8,128)(2,1)S(1)} %copy-done.11), channel_id=1, source_target_pairs={{0,1},{1,0},{2,3},{3,2},{4,5},{5,4},{6,7},{7,6},{8,9},{9,8},{10,11... | collective-permute-start | bytes 3145736 | tf_op jit(solution)/shard_map/ppermute | solution.py:434
  178.6 17.8 %collective-permute-start.19 = (bf16[8,64,256]{2,1,0:T(8,128)(2,1)S(1)}, bf16[8,64,256]{2,1,0:T(8,128)(2,1)S(1)}, u32[]{:S(2)}, u32[]{:S(2)}) collective-permute-start(bf16[8,64,256]{2,1,0:T(8,128)(2,1)S(1)} %slice.132), channel_id=1, source_target_pairs={{0,4},{1,5},{2,6},{3,7},{4,0},{5,1},{6,2},{7,3},{8,12},{9,13},{10,... | collective-permute-start | bytes 786440 | tf_op jit(solution)/shard_map/ppermute | solution.py:434
  180.4 22.8 %collective-permute-start.22 = (bf16[8,64,256]{2,1,0:T(8,128)(2,1)S(1)}, bf16[8,64,256]{2,1,0:T(8,128)(2,1)S(1)}, u32[]{:S(2)}, u32[]{:S(2)}) collective-permute-start(bf16[8,64,256]{2,1,0:T(8,128)(2,1)S(1)} %slice.131), channel_id=1, source_target_pairs={{0,8},{1,9},{2,10},{3,11},{4,12},{5,13},{6,14},{7,15},{8,0},{9,1},... | collective-permute-start | bytes 786440 | tf_op jit(solution)/shard_map/ppermute | solution.py:434
  195.3 27.6 %collective-permute-start.26 = (bf16[32,64,256]{2,1,0:T(8,128)(2,1)S(1)}, bf16[32,64,256]{2,1,0:T(8,128)(2,1)S(1)}, u32[]{:S(2)}, u32[]{:S(2)}) collective-permute-start(bf16[32,64,256]{2,1,0:T(8,128)(2,1)S(1)} %add_convert_fusion), channel_id=1, source_target_pairs={{0,2},{1,3},{2,0},{3,1},{4,6},{5,7},{6,4},{7,5},{8,10},{9,11},{10,... | collective-permute-start | bytes 3145736 | tf_op jit(solution)/shard_map/ppermute | solution.py:434
  196.5 15.5 %collective-permute-start.20 = (bf16[4,64,256]{2,1,0:T(8,128)(2,1)S(1)}, bf16[4,64,256]{2,1,0:T(8,128)(2,1)S(1)}, u32[]{:S(2)}, u32[]{:S(2)}) collective-permute-start(bf16[4,64,256]{2,1,0:T(8,128)(2,1)S(1)} %slice.134), channel_id=1, source_target_pairs={{0,8},{1,9},{2,10},{3,11},{4,12},{5,13},{6,14},{7,15},{8,0},{9,1},... | collective-permute-start | bytes 393224 | tf_op jit(solution)/shard_map/ppermute | solution.py:434
  203.3 18.7 %collective-permute-start.23 = (bf16[4,64,256]{2,1,0:T(8,128)(2,1)S(1)}, bf16[4,64,256]{2,1,0:T(8,128)(2,1)S(1)}, u32[]{:S(2)}, u32[]{:S(2)}) collective-permute-start(bf16[4,64,256]{2,1,0:T(8,128)(2,1)S(1)} %slice.133), channel_id=1, source_target_pairs={{0,2},{1,3},{2,0},{3,1},{4,6},{5,7},{6,4},{7,5},{8,10},{9,11},{10,... | collective-permute-start | bytes 393224 | tf_op jit(solution)/shard_map/ppermute | solution.py:434
  (24 other events, 175.1 us)

commit v7 on v6

--- a/solution.py
+++ b/solution.py
@@ -14,10 +14,9 @@
 LAYER = 4
 PAIR = 2
 NARROW = 3
-ROUNDS = (6, 10)
+ROUNDS = (6, 6, 4)
 MIB = 1 << 20
-TERMS = 32
-CROSS = ((0, 0), (0, 1), (1, 0), (0, 2), (1, 1), (2, 0))
+COLUMNS = (0, 1, 4, 5, 6)
 
 
 def round_sizes(slots):
@@ -118,34 +117,15 @@
     return [out[i * layers : (i + 1) * layers] for i in range(rounds)], out[rounds * layers :]
 
 
-def split(values):
-    parts = []
-    for _ in range(3):
-        part = lax.reduce_precision(values, 8, 7)
-        parts.append(part)
-        values = values - part
-    return parts
-
-
-def kernel_split(values):
-    parts = []
-    for _ in range(3):
-        part = values.astype(jnp.bfloat16).astype(jnp.float32)
-        parts.append(part)
-        values = values - part
-    return parts
-
-
 def fit_kernel(first, final, layers, slots, groups, *refs):
-    info, cutoffs, places, spots, origin = refs[:5]
-    rest = refs[5:]
+    info, cutoffs, places, spots = refs[:4]
+    rest = refs[4:]
     obs_in, pix_in = [], []
     for _ in groups:
         obs_in.append(rest[:layers])
         pix_in.append(rest[layers : 2 * layers])
         rest = rest[2 * layers :]
-    patches, forms = rest[:2]
-    rest = rest[1:]
+    patches = rest[0]
     if first:
         screen_parts, stress_parts = rest[1 : 1 + LAYER], rest[1 + LAYER : 1 + 2 * LAYER]
         rest = rest[1 + 2 * LAYER :]
@@ -159,8 +139,8 @@
     rest = rest[len(outs) :]
     obs, pix = rest[:2]
     buffers = rest[2 : 2 + 9 * PAIR]
-    wide, sights = rest[2 + 9 * PAIR : 2 + 10 * PAIR], rest[2 + 10 * PAIR : 2 + 11 * PAIR]
-    items, sems = rest[2 + 11 * PAIR :]
+    wide = rest[2 + 9 * PAIR : 2 + 10 * PAIR]
+    items, sems = rest[2 + 10 * PAIR :]
     sets = [
         [buffers[3 * (PAIR * i + lane) : 3 * (PAIR * i + lane) + 3] for lane in range(PAIR)]
         for i in range(3)
@@ -208,44 +188,27 @@
 
     def spread(rows, lane):
         columns = rows.T
-        for i in range(2):
-            wide[lane][i] = jnp.broadcast_to(columns[:, i : i + 1], (CHUNK, CHUNK))
-        le, ln = rows[4:5], rows[5:6]
-        along = le * (rows[0:1] - origin[0]) + ln * (rows[1:2] - origin[1])
-        row = lax.broadcasted_iota(jnp.int32, (8, CHUNK), 0)
-        factors = jnp.where(
-            row == 0, along, jnp.where(row == 1, le, jnp.where(row == 2, ln, rows[6:7]))
-        )
-        parts = kernel_split(factors)
-        low = row < 4
-        tiles = []
-        for first_part, second_part in zip(CROSS[::2], CROSS[1::2]):
-            upper = jnp.concatenate([parts[second_part[0]][:4]] * 2, axis=0)
-            tiles.append(jnp.where(low, parts[first_part[0]], upper))
-        tiles.append(jnp.zeros((8, CHUNK), jnp.float32))
-        sights[lane][...] = jnp.concatenate(tiles, axis=0).T.astype(jnp.bfloat16)
+        for i, c in enumerate(COLUMNS):
+            wide[lane][i] = jnp.broadcast_to(columns[:, c : c + 1], (CHUNK, CHUNK))
 
     def make_strips(near, k, begin, end, lane, green):
         patch = [
-            jnp.broadcast_to(patches[near[k], r : r + 1], (8, PBLK)) for r in range(3)
+            jnp.broadcast_to(patches[near[k], r : r + 1], (8, PBLK)) for r in range(5)
         ]
-        alongs = jnp.dot(
-            sights[lane][begin:end], forms[near[k]], preferred_element_type=jnp.float32
-        )
         for low in range(begin, end, 16):
-            along = alongs[low - begin : low - begin + 16]
-            inverses = []
+            strips = []
             for at in (low, low + 8):
-                east, north = (
+                east, north, le, ln, lu = (
                     jnp.concatenate([wide[lane][i, at : at + 8]] * (PBLK // CHUNK), axis=1)
-                    for i in range(2)
+                    for i in range(len(COLUMNS))
                 )
                 dx = east - patch[0]
                 dy = north - patch[1]
-                inverses.append(lax.rsqrt(dx * dx + dy * dy + patch[2]))
-            inverse = jnp.concatenate(inverses, axis=0)
-            green[low : low + 16, k * PBLK : (k + 1) * PBLK] = (
-                along * inverse * inverse * inverse
+                inverse = lax.rsqrt(dx * dx + dy * dy + patch[3])
+                along = le * dx + ln * dy + lu * patch[2]
+                strips.append(patch[4] * along * inverse * inverse * inverse)
+            green[low : low + 16, k * PBLK : (k + 1) * PBLK] = jnp.concatenate(
+                strips, axis=0
             ).astype(jnp.bfloat16)
 
     def make_hats(rows, hats):
@@ -371,7 +334,7 @@
             out[...] = screen_grad[low : low + local_tiles].astype(out.dtype)
 
 
-def fit(tables, groups, patches, forms, screens, stress, state, first, final):
+def fit(tables, groups, patches, screens, stress, state, first, final):
     layers = len(groups[0][1])
     slots = tables[0].shape[0] // (3 * layers)
     smem = pl.BlockSpec(memory_space=pltpu.SMEM)
@@ -393,12 +356,12 @@
         out_shape.append(jax.ShapeDtypeStruct((blocks // 2, epochs, PBLK), jnp.bfloat16))
         shape = (state[1].shape[0] // LAYER,) + state[1].shape[1:]
         out_shape += [jax.ShapeDtypeStruct(shape, jnp.bfloat16)] * 2
-    before = len(tables) + len(arrays) + 2 + len(screens) + len(stress)
+    before = len(tables) + len(arrays) + 1 + len(screens) + len(stress)
     return pl.pallas_call(
         functools.partial(fit_kernel, first, final, layers, slots, spans),
         in_specs=[smem] * len(tables)
         + [hbm] * len(arrays)
-        + [vmem] * 2
+        + [vmem]
         + [hbm if first else vmem] * (len(screens) + len(stress))
         + [vmem] * len(state),
         out_specs=[vmem] * len(out_shape),
@@ -413,8 +376,7 @@
             pltpu.VMEM((epochs, CHUNK), jnp.bfloat16),
         ]
         * (3 * PAIR)
-        + [pltpu.VMEM((2, CHUNK, CHUNK), jnp.float32)] * PAIR
-        + [pltpu.VMEM((CHUNK, TERMS), jnp.bfloat16)] * PAIR
+        + [pltpu.VMEM((len(COLUMNS), CHUNK, CHUNK), jnp.float32)] * PAIR
         + [
             pltpu.SMEM((layers * span + 1,), jnp.int32),
             pltpu.SemaphoreType.DMA((2 * layers * len(groups) + 2 * LAYER,)),
@@ -427,7 +389,7 @@
             transcendentals=layers * span * CHUNK * NEAR * PBLK,
         ),
         name="fit",
-    )(*tables, *arrays, patches, forms, *screens, *stress, *state)
+    )(*tables, *arrays, patches, *screens, *stress, *state)
 
 
 def partner(values, devices, distance):
@@ -533,30 +495,14 @@
         distance //= 2
     patch_blocks = devices * local
     east, north, depth, compliance = patch_geometry
-    origin = patch_geometry[:2, 0]
-    strength = compliance * depth * depth
-    faces = split(
-        jnp.stack(
-            [
-                strength,
-                -strength * (east - origin[0]),
-                -strength * (north - origin[1]),
-                strength * depth,
-            ]
-        )
-    )
-    forms = jnp.concatenate(
-        [faces[second] for _, second in CROSS] + [jnp.zeros((8,) + east.shape, jnp.float32)]
-    ).astype(jnp.bfloat16)
-    forms = jnp.swapaxes(forms.reshape(TERMS, patch_blocks, PBLK), 0, 1)
-    patches = jnp.stack([east, north, depth * depth])
-    patches = jnp.swapaxes(patches.reshape(3, patch_blocks, PBLK), 0, 1)
+    patches = jnp.stack([east, north, depth, depth * depth, compliance * depth * depth])
+    patches = jnp.swapaxes(patches.reshape(5, patch_blocks, PBLK), 0, 1)
     cutoffs = cutoff_lists.reshape(-1)
     held, pix, across_screens = lax.optimization_barrier((held, pix, across_screens))
     places, spots = block_places(devices, here, patch_blocks, local, epochs)
     info = jnp.stack([p[slots, :3, :slots] for p in pix]).astype(jnp.int32).reshape(-1)
-    across_screens, forms, patches, cutoffs, info, places, spots = lax.optimization_barrier(
-        (across_screens, forms, patches, cutoffs, info, places, spots)
+    across_screens, patches, cutoffs, info, places, spots = lax.optimization_barrier(
+        (across_screens, patches, cutoffs, info, places, spots)
     )
     got = [exchange(o) for o in obs]
     across = partner(held, devices, PAIR)
@@ -569,7 +515,7 @@
         partner(across_screens, devices, 1),
     ]
 
-    tables = (info, cutoffs, places, spots, origin)
+    tables = (info, cutoffs, places, spots)
 
     state = (
         jax.ShapeDtypeStruct((patch_blocks, epochs, PBLK), jnp.float32),
@@ -583,7 +529,6 @@
             tables,
             groups,
             patches,
-            forms,
             all_screens,
             all_stress,
             state[:2],

time: 221 us -> 227 us (1.027); the launches traced: 225 us -> 224 us
  starting transfers between devices: 66.8 us -> 104 us
  Pallas kernels: 44.1 us -> 15.3 us
  waiting for transfers between devices: 79.3 us -> 75.2 us
  other arithmetic: 10 us -> 7.47 us
  local copies, waits for them, and re-layouts: 23.6 us -> 21.1 us
    ppermute x27 -> x30, starting transfers between devices: 66.8 us -> 104 us  [partner(): lax.ppermute(values, 'tile', [(i, i ^ distance) for i in range(devices)])]
    pallas_call x2 -> x3, Pallas kernels: 39.6 us -> 10.7 us  [fit(): pl.pallas_call(functools.partial(fit_kernel, first, final, layers, slots,...]
    concatenate x1 -> x0, local copies, waits for them, and re-layouts: 4.73 us -> none  [on_device(): jnp.concatenate([faces[second] for _, second in CROSS] + [jnp.zeros((8,)...]
    ppermute x27 -> x30, waiting for transfers between devices: 79.3 us -> 75.2 us  [partner(): lax.ppermute(values, 'tile', [(i, i ^ distance) for i in range(devices)])]
    unnamed x43 -> x53, local copies, waits for them, and re-layouts: 12.8 us -> 16 us
  transfers between devices with their start and end apart: 27 -> 30, of which waited for: 8 -> 14; matrix products, arithmetic and copies ran while one was open for 8% -> 5% of each run, Pallas kernels for 17% -> 6%
where the time goes in v7:
time: 227 us; the launch traced here: 224 us
  starting transfers between devices  104 us (46%)
  waiting for transfers between devices  75.2 us (33%)
  local copies, waits for them, and re-layouts  21.1 us (9%)
  Pallas kernels  15.3 us (7%)
  other arithmetic  7.47 us (3%)
    ppermute x30, starting transfers between devices, partner(): lax.ppermute(values, 'tile', [(i, i ^ distance) for i in range(devices)])  104 us
    ppermute x30, waiting for transfers between devices, partner(): lax.ppermute(values, 'tile', [(i, i ^ distance) for i in range(devices)])  75.2 us
    unnamed x53, local copies, waits for them, and re-layouts  16 us
    pallas_call x3, Pallas kernels, fit(): pl.pallas_call(functools.partial(fit_kernel, first, final, layers, slots,...  10.7 us
    pallas_call x1, Pallas kernels, pack(): pl.pallas_call(functools.partial(pack_kernel, local_tiles, layers, slots)...  4.62 us
  transfers between devices with their start and end apart: 30, of which 14 were waited for; matrix products, arithmetic and copies ran while one was open for 5% of the time, Pallas kernels for 6%

profile of v7, /device:TPU:0, one launch (start us, length us, event | category | flops | bytes accessed | tf_op | source)
XLA Modules:
  0.0 224.1 jit_solution(3817009119346943647)
XLA Ops:
  1.6 4.1 %collective-permute-start = (bf16[512,256]{1,0:T(8,128)(2,1)S(1)}, bf16[512,256]{1,0:T(8,128)(2,1)S(1)}, u32[]{:S(2)}, u32[]{:S(2)}) collective-permute-start(bf16[512,256]{1,0:T(8,128)(2,1)S(1)} %bitcast.19), channel_id=1, source_target_pairs={{0,8},{1,9},{2,10},{3,11},{4,12},{5,13},{6,14},{7,15},{8,0},{9,1},... | collective-permute-start | bytes 786440 | tf_op jit(solution)/shard_map/ppermute | solution.py:396
  11.2 4.6 %pack.1 = (bf16[24,64,128]{2,1,0:T(8,128)(2,1)S(1)}, bf16[24,64,128]{2,1,0:T(8,128)(2,1)}, bf16[24,64,128]{2,1,0:T(8,128)(2,1)}, bf16[24,64,128]{2,1,0:T(8,128)(...) custom-call(s32[1]{0:T(128)} %bitcast.3.here, ...), custom_call_target="tpu_custom_call" | custom-call | tf_op jit(solution)/shard_map/pack/pallas_call | solution.py:95
  21.9 3.6 %collective-permute-start.4 = (f32[65,8,128]{2,1,0:T(8,128)S(1)}, f32[65,8,128]{2,1,0:T(8,128)S(1)}, u32[]{:S(2)}, u32[]{:S(2)}) collective-permute-start(f32[65,8,128]{2,1,0:T(8,128)S(1)} %get-tuple-element.63), channel_id=1, source_target_pairs={{0,12},{1,13},{2,14},{3,15},{4,8},{5,9},{6,10},{7,11},{8,4},{9,5},... | collective-permute-start | bytes 798728 | tf_op jit(solution)/shard_map/ppermute | solution.py:396
  25.5 14.6 %collective-permute-done.1 = bf16[1024,256]{1,0:T(8,128)(2,1)S(1)} collective-permute-done((bf16[1024,256]{1,0:T(8,128)(2,1)S(1)}, bf16[1024,256]{1,0:T(8,128)(2,1)S(1)}, u32[]{:S(2)}, u32[]{:S(2)}) %collective-permute-start.1) | collective-permute-done | bytes 524320 | tf_op jit(solution)/shard_map/ppermute | solution.py:396
  40.3 3.8 %collective-permute-done.2.refs_9_ = f32[65,8,128]{2,1,0:T(8,128)S(1)} collective-permute-done((f32[65,8,128]{2,1,0:T(8,128)S(1)}, f32[65,8,128]{2,1,0:T(8,128)S(1)}, u32[]{:S(2)}, u32[]{:S(2)}) %collective-permute-start.2) | collective-permute-done | bytes 266272 | tf_op jit(solution)/shard_map/ppermute | solution.py:396
  44.9 3.4 %collective-permute-start.11 = (bf16[24,64,128]{2,1,0:T(8,128)(2,1)}, bf16[24,64,128]{2,1,0:T(8,128)(2,1)}, u32[]{:S(2)}, u32[]{:S(2)}) collective-permute-start(bf16[24,64,128]{2,1,0:T(8,128)(2,1)} %get-tuple-element.81), channel_id=1, source_target_pairs={{0,8},{1,9},{2,10},{3,11},{4,12},{5,13},{6,14},{7,15},{8,0},{9,1},... | collective-permute-start | bytes 1179656 | tf_op jit(solution)/shard_map/ppermute | solution.py:396
  48.3 3.0 %collective-permute-done.4.refs_11_ = f32[65,8,128]{2,1,0:T(8,128)S(1)} collective-permute-done((f32[65,8,128]{2,1,0:T(8,128)S(1)}, f32[65,8,128]{2,1,0:T(8,128)S(1)}, u32[]{:S(2)}, u32[]{:S(2)}) %collective-permute-start.4) | collective-permute-done | bytes 266272 | tf_op jit(solution)/shard_map/ppermute | solution.py:396
  51.3 3.7 %collective-permute-start.12 = (bf16[24,64,128]{2,1,0:T(8,128)(2,1)}, bf16[24,64,128]{2,1,0:T(8,128)(2,1)}, u32[]{:S(2)}, u32[]{:S(2)}) collective-permute-start(bf16[24,64,128]{2,1,0:T(8,128)(2,1)} %get-tuple-element.82), channel_id=1, source_target_pairs={{0,12},{1,13},{2,14},{3,15},{4,8},{5,9},{6,10},{7,11},{8,4},{9,5},... | collective-permute-start | bytes 1179656 | tf_op jit(solution)/shard_map/ppermute | solution.py:396
  55.0 3.6 %collective-permute-start.9 = (bf16[2048,256]{1,0:T(8,128)(2,1)S(1)}, bf16[2048,256]{1,0:T(8,128)(2,1)}, u32[]{:S(2)}, u32[]{:S(2)}) collective-permute-start(bf16[2048,256]{1,0:T(8,128)(2,1)S(1)} %pad_maximum_fusion.refs_17_), channel_id=1, source_target_pairs={{0,2},{1,3},{2,0},{3,1},{4,6},{5,7},{6,4},{7,5},{8,10},{9,11},{10,... | collective-permute-start | bytes 3145736 | tf_op jit(solution)/shard_map/ppermute | solution.py:396
  68.2 7.9 %collective-permute-done.12.refs_7_ = bf16[24,64,128]{2,1,0:T(8,128)(2,1)} collective-permute-done((bf16[24,64,128]{2,1,0:T(8,128)(2,1)}, bf16[24,64,128]{2,1,0:T(8,128)(2,1)}, u32[]{:S(2)}, u32[]{:S(2)}) %collective-permute-start.12) | collective-permute-done | bytes 393248 | tf_op jit(solution)/shard_map/ppermute | solution.py:396
  76.5 8.5 %collective-permute-start.17 = (bf16[24,64,128]{2,1,0:T(8,128)(2,1)}, bf16[24,64,128]{2,1,0:T(8,128)(2,1)S(1)}, u32[]{:S(2)}, u32[]{:S(2)}) collective-permute-start(bf16[24,64,128]{2,1,0:T(8,128)(2,1)} %copy-done.18), channel_id=1, source_target_pairs={{0,4},{1,5},{2,6},{3,7},{4,0},{5,1},{6,2},{7,3},{8,12},{9,13},{10,... | collective-permute-start | bytes 1179656 | tf_op jit(solution)/shard_map/ppermute | solution.py:396
  95.5 4.5 %fit.3 = (f32[128,64,256]{2,1,0:T(8,128)S(1)}, f32[128,64,256]{2,1,0:T(8,128)S(1)}, bf16[128,64,256]{2,1,0:T(8,128)(2,1)S(1)}, bf16[8192,256]{1,0:T(8,128)(2,1)S(1)}) custom-call(s32[768]{0:T(1024)S(1)} %copy-done.5, s32[1536]{0:T(1024)S(1)} %copy-done.4, s32[128]{0:T(128)S(1)} %copy-done.6, s32[128]{0:T(128)S(1)} %copy-done.7, ...), custom_call_target="tpu_custom_call" | custom-call | flops 3221225472 | bytes 1024 | tf_op jit(solution)/shard_map/fit/pallas_call | solution.py:360
  100.0 3.2 %collective-permute-done.17.refs_5_ = bf16[24,64,128]{2,1,0:T(8,128)(2,1)S(1)} collective-permute-done((bf16[24,64,128]{2,1,0:T(8,128)(2,1)}, bf16[24,64,128]{2,1,0:T(8,128)(2,1)S(1)}, u32[]{:S(2)}, u32[]{:S(2)}) %collective-permute-start.17) | collective-permute-done | bytes 393248 | tf_op jit(solution)/shard_map/ppermute | solution.py:396
  103.2 36.4 %collective-permute-start.8 = (bf16[16,64,128]{2,1,0:T(8,128)(2,1)S(1)}, bf16[16,64,128]{2,1,0:T(8,128)(2,1)S(1)}, u32[]{:S(2)}, u32[]{:S(2)}) collective-permute-start(bf16[16,64,128]{2,1,0:T(8,128)(2,1)S(1)} %copy-done.22), channel_id=1, source_target_pairs={{0,12},{1,13},{2,14},{3,15},{4,8},{5,9},{6,10},{7,11},{8,4},{9,5},... | collective-permute-start | bytes 786440 | tf_op jit(solution)/shard_map/ppermute | solution.py:396
  139.6 3.8 %fit.4 = (f32[128,64,256]{2,1,0:T(8,128)S(1)}, f32[128,64,256]{2,1,0:T(8,128)S(1)}) custom-call(s32[768]{0:T(1024)S(1)} %copy-done.5, s32[1536]{0:T(1024)S(1)} %copy-done.4, s32[128]{0:T(128)S(1)} %copy-done.6, s32[128]{0:T(128)S(1)} %copy-done.7, ...), custom_call_target="tpu_custom_call", output_to_operand_aliasing={{0}: (15, {}), {1}: (16, {})} | custom-call | flops 3221225472 | bytes 1024 | tf_op jit(solution)/shard_map/fit/pallas_call | solution.py:360
  144.1 2.4 %fit.5 = (f32[128,64,256]{2,1,0:T(8,128)S(1)}, f32[128,64,256]{2,1,0:T(8,128)S(1)}, bf16[64,64,256]{2,1,0:T(8,128)(2,1)S(1)}, bf16[32,64,256]{2,1,0:T(8,128)(2,1)S(1)}, bf16[32,64,256]{2,1,0:T(8,128)(2,1)S(1)}) custom-call(s32[768]{0:T(1024)S(1)} %copy-done.5, s32[1536]{0:T(1024)S(1)} %copy-done.4, ...), custom_call_target="tpu_custom_call", output_to_operand_aliasing={{0}: (15, {}), {1}: (16, {})} | custom-call | flops 2147483648 | bytes 1024 | tf_op jit(solution)/shard_map/fit/pallas_call | solution.py:360
  148.5 4.2 %collective-permute-done.20 = bf16[64,64,256]{2,1,0:T(8,128)(2,1)S(1)} collective-permute-done((bf16[64,64,256]{2,1,0:T(8,128)(2,1)S(1)}, bf16[64,64,256]{2,1,0:T(8,128)(2,1)S(1)}, u32[]{:S(2)}, u32[]{:S(2)}) %collective-permute-start.20) | collective-permute-done | bytes 2097184 | tf_op jit(solution)/shard_map/ppermute | solution.py:396
  153.9 2.7 %collective-permute-start.21 = (bf16[16,64,256]{2,1,0:T(8,128)(2,1)S(1)}, bf16[16,64,256]{2,1,0:T(8,128)(2,1)S(1)}, u32[]{:S(2)}, u32[]{:S(2)}) collective-permute-start(bf16[16,64,256]{2,1,0:T(8,128)(2,1)S(1)} %get-tuple-element.111), channel_id=1, source_target_pairs={{0,2},{1,3},{2,0},{3,1},{4,6},{5,7},{6,4},{7,5},{8,10},{9,11},{10,... | collective-permute-start | bytes 1572872 | tf_op jit(solution)/shard_map/ppermute | solution.py:396
  156.6 18.5 %collective-permute-start.24 = (bf16[16,64,256]{2,1,0:T(8,128)(2,1)S(1)}, bf16[16,64,256]{2,1,0:T(8,128)(2,1)S(1)}, u32[]{:S(2)}, u32[]{:S(2)}) collective-permute-start(bf16[16,64,256]{2,1,0:T(8,128)(2,1)S(1)} %get-tuple-element.110), channel_id=1, source_target_pairs={{0,4},{1,5},{2,6},{3,7},{4,0},{5,1},{6,2},{7,3},{8,12},{9,13},{10,... | collective-permute-start | bytes 1572872 | tf_op jit(solution)/shard_map/ppermute | solution.py:396
  175.5 12.2 %collective-permute-done.24 = bf16[16,64,256]{2,1,0:T(8,128)(2,1)S(1)} collective-permute-done((bf16[16,64,256]{2,1,0:T(8,128)(2,1)S(1)}, bf16[16,64,256]{2,1,0:T(8,128)(2,1)S(1)}, u32[]{:S(2)}, u32[]{:S(2)}) %collective-permute-start.24) | collective-permute-done | bytes 524320 | tf_op jit(solution)/shard_map/ppermute | solution.py:396
  189.7 4.1 %collective-permute-start.25 = (bf16[8,64,256]{2,1,0:T(8,128)(2,1)S(1)}, bf16[8,64,256]{2,1,0:T(8,128)(2,1)S(1)}, u32[]{:S(2)}, u32[]{:S(2)}) collective-permute-start(bf16[8,64,256]{2,1,0:T(8,128)(2,1)S(1)} %slice.114), channel_id=1, source_target_pairs={{0,8},{1,9},{2,10},{3,11},{4,12},{5,13},{6,14},{7,15},{8,0},{9,1},... | collective-permute-start | bytes 786440 | tf_op jit(solution)/shard_map/ppermute | solution.py:396
  195.2 6.5 %collective-permute-done.22 = bf16[8,64,256]{2,1,0:T(8,128)(2,1)S(1)} collective-permute-done((bf16[8,64,256]{2,1,0:T(8,128)(2,1)S(1)}, bf16[8,64,256]{2,1,0:T(8,128)(2,1)S(1)}, u32[]{:S(2)}, u32[]{:S(2)}) %collective-permute-start.22) | collective-permute-done | bytes 262176 | tf_op jit(solution)/shard_map/ppermute | solution.py:396
  204.0 7.9 %collective-permute-done.23 = bf16[4,64,256]{2,1,0:T(8,128)(2,1)S(1)} collective-permute-done((bf16[4,64,256]{2,1,0:T(8,128)(2,1)S(1)}, bf16[4,64,256]{2,1,0:T(8,128)(2,1)S(1)}, u32[]{:S(2)}, u32[]{:S(2)}) %collective-permute-start.23) | collective-permute-done | bytes 131104 | tf_op jit(solution)/shard_map/ppermute | solution.py:396
  212.0 9.4 %collective-permute-done.26 = bf16[4,64,256]{2,1,0:T(8,128)(2,1)S(1)} collective-permute-done((bf16[4,64,256]{2,1,0:T(8,128)(2,1)S(1)}, bf16[4,64,256]{2,1,0:T(8,128)(2,1)S(1)}, u32[]{:S(2)}, u32[]{:S(2)}) %collective-permute-start.26) | collective-permute-done | bytes 131104 | tf_op jit(solution)/shard_map/ppermute | solution.py:396
  (122 shorter events, 46.6 us)
Async XLA Ops:
  5.7 49.3 %collective-permute-start.5 = (bf16[32,64,256]{2,1,0:T(8,128)(2,1)}, bf16[32,64,256]{2,1,0:T(8,128)(2,1)S(1)}, u32[]{:S(2)}, u32[]{:S(2)}) collective-permute-start(bf16[32,64,256]{2,1,0:T(8,128)(2,1)} %refs_13_.1), channel_id=1, source_target_pairs={{0,2},{1,3},{2,0},{3,1},{4,6},{5,7},{6,4},{7,5},{8,10},{9,11},{10,... | collective-permute-start | bytes 3145736 | tf_op jit(solution)/shard_map/ppermute | solution.py:396
  19.5 20.6 %collective-permute-start.1 = (bf16[1024,256]{1,0:T(8,128)(2,1)S(1)}, bf16[1024,256]{1,0:T(8,128)(2,1)S(1)}, u32[]{:S(2)}, u32[]{:S(2)}) collective-permute-start(bf16[1024,256]{1,0:T(8,128)(2,1)S(1)} %pad_maximum_fusion.1), channel_id=1, source_target_pairs={{0,4},{1,5},{2,6},{3,7},{4,0},{5,1},{6,2},{7,3},{8,12},{9,13},{10,... | collective-permute-start | bytes 1572872 | tf_op jit(solution)/shard_map/ppermute | solution.py:396
  21.1 22.9 %collective-permute-start.2 = (f32[65,8,128]{2,1,0:T(8,128)S(1)}, f32[65,8,128]{2,1,0:T(8,128)S(1)}, u32[]{:S(2)}, u32[]{:S(2)}) collective-permute-start(f32[65,8,128]{2,1,0:T(8,128)S(1)} %get-tuple-element.61), channel_id=1, source_target_pairs={{0,4},{1,5},{2,6},{3,7},{4,0},{5,1},{6,2},{7,3},{8,12},{9,13},{10,... | collective-permute-start | bytes 798728 | tf_op jit(solution)/shard_map/ppermute | solution.py:396
  21.5 23.3 %collective-permute-start.3 = (f32[65,8,128]{2,1,0:T(8,128)S(1)}, f32[65,8,128]{2,1,0:T(8,128)S(1)}, u32[]{:S(2)}, u32[]{:S(2)}) collective-permute-start(f32[65,8,128]{2,1,0:T(8,128)S(1)} %get-tuple-element.62), channel_id=1, source_target_pairs={{0,8},{1,9},{2,10},{3,11},{4,12},{5,13},{6,14},{7,15},{8,0},{9,1},... | collective-permute-start | bytes 798728 | tf_op jit(solution)/shard_map/ppermute | solution.py:396
  21.9 29.4 %collective-permute-start.4 = (f32[65,8,128]{2,1,0:T(8,128)S(1)}, f32[65,8,128]{2,1,0:T(8,128)S(1)}, u32[]{:S(2)}, u32[]{:S(2)}) collective-permute-start(f32[65,8,128]{2,1,0:T(8,128)S(1)} %get-tuple-element.63), channel_id=1, source_target_pairs={{0,12},{1,13},{2,14},{3,15},{4,8},{5,9},{6,10},{7,11},{8,4},{9,5},... | collective-permute-start | bytes 798728 | tf_op jit(solution)/shard_map/ppermute | solution.py:396
  40.1 44.8 %collective-permute-start.13 = (bf16[32,64,256]{2,1,0:T(8,128)(2,1)}, bf16[32,64,256]{2,1,0:T(8,128)(2,1)}, u32[]{:S(2)}, u32[]{:S(2)}) collective-permute-start(bf16[32,64,256]{2,1,0:T(8,128)(2,1)} %refs_13_.1), channel_id=1, source_target_pairs={{0,1},{1,0},{2,3},{3,2},{4,5},{5,4},{6,7},{7,6},{8,9},{9,8},{10,11... | collective-permute-start | bytes 3145736 | tf_op jit(solution)/shard_map/ppermute | solution.py:396
  44.0 23.6 %collective-permute-start.10 = (bf16[24,64,128]{2,1,0:T(8,128)(2,1)}, bf16[24,64,128]{2,1,0:T(8,128)(2,1)}, u32[]{:S(2)}, u32[]{:S(2)}) collective-permute-start(bf16[24,64,128]{2,1,0:T(8,128)(2,1)} %get-tuple-element.80), channel_id=1, source_target_pairs={{0,4},{1,5},{2,6},{3,7},{4,0},{5,1},{6,2},{7,3},{8,12},{9,13},{10,... | collective-permute-start | bytes 1179656 | tf_op jit(solution)/shard_map/ppermute | solution.py:396
  44.9 22.8 %collective-permute-start.11 = (bf16[24,64,128]{2,1,0:T(8,128)(2,1)}, bf16[24,64,128]{2,1,0:T(8,128)(2,1)}, u32[]{:S(2)}, u32[]{:S(2)}) collective-permute-start(bf16[24,64,128]{2,1,0:T(8,128)(2,1)} %get-tuple-element.81), channel_id=1, source_target_pairs={{0,8},{1,9},{2,10},{3,11},{4,12},{5,13},{6,14},{7,15},{8,0},{9,1},... | collective-permute-start | bytes 1179656 | tf_op jit(solution)/shard_map/ppermute | solution.py:396
  51.3 24.8 %collective-permute-start.12 = (bf16[24,64,128]{2,1,0:T(8,128)(2,1)}, bf16[24,64,128]{2,1,0:T(8,128)(2,1)}, u32[]{:S(2)}, u32[]{:S(2)}) collective-permute-start(bf16[24,64,128]{2,1,0:T(8,128)(2,1)} %get-tuple-element.82), channel_id=1, source_target_pairs={{0,12},{1,13},{2,14},{3,15},{4,8},{5,9},{6,10},{7,11},{8,4},{9,5},... | collective-permute-start | bytes 1179656 | tf_op jit(solution)/shard_map/ppermute | solution.py:396
  55.0 21.4 %collective-permute-start.9 = (bf16[2048,256]{1,0:T(8,128)(2,1)S(1)}, bf16[2048,256]{1,0:T(8,128)(2,1)}, u32[]{:S(2)}, u32[]{:S(2)}) collective-permute-start(bf16[2048,256]{1,0:T(8,128)(2,1)S(1)} %pad_maximum_fusion.refs_17_), channel_id=1, source_target_pairs={{0,2},{1,3},{2,0},{3,1},{4,6},{5,7},{6,4},{7,5},{8,10},{9,11},{10,... | collective-permute-start | bytes 3145736 | tf_op jit(solution)/shard_map/ppermute | solution.py:396
  67.7 18.5 %collective-permute-start.14 = (bf16[32,64,256]{2,1,0:T(8,128)(2,1)}, bf16[32,64,256]{2,1,0:T(8,128)(2,1)S(1)}, u32[]{:S(2)}, u32[]{:S(2)}) collective-permute-start(bf16[32,64,256]{2,1,0:T(8,128)(2,1)} %copy-done.10), channel_id=1, source_target_pairs={{0,1},{1,0},{2,3},{3,2},{4,5},{5,4},{6,7},{7,6},{8,9},{9,8},{10,11... | collective-permute-start | bytes 3145736 | tf_op jit(solution)/shard_map/ppermute | solution.py:396
  67.7 19.9 %collective-permute-start.15 = (bf16[2048,256]{1,0:T(8,128)(2,1)S(1)}, bf16[2048,256]{1,0:T(8,128)(2,1)S(1)}, u32[]{:S(2)}, u32[]{:S(2)}) collective-permute-start(bf16[2048,256]{1,0:T(8,128)(2,1)S(1)} %pad_maximum_fusion.refs_17_), channel_id=1, source_target_pairs={{0,1},{1,0},{2,3},{3,2},{4,5},{5,4},{6,7},{7,6},{8,9},{9,8},{10,11... | collective-permute-start | bytes 3145736 | tf_op jit(solution)/shard_map/ppermute | solution.py:396
  76.5 26.7 %collective-permute-start.17 = (bf16[24,64,128]{2,1,0:T(8,128)(2,1)}, bf16[24,64,128]{2,1,0:T(8,128)(2,1)S(1)}, u32[]{:S(2)}, u32[]{:S(2)}) collective-permute-start(bf16[24,64,128]{2,1,0:T(8,128)(2,1)} %copy-done.18), channel_id=1, source_target_pairs={{0,4},{1,5},{2,6},{3,7},{4,0},{5,1},{6,2},{7,3},{8,12},{9,13},{10,... | collective-permute-start | bytes 1179656 | tf_op jit(solution)/shard_map/ppermute | solution.py:396
  84.9 54.7 %collective-permute-start.18 = (bf16[24,64,128]{2,1,0:T(8,128)(2,1)}, bf16[24,64,128]{2,1,0:T(8,128)(2,1)S(1)}, u32[]{:S(2)}, u32[]{:S(2)}) collective-permute-start(bf16[24,64,128]{2,1,0:T(8,128)(2,1)} %copy-done.17), channel_id=1, source_target_pairs={{0,8},{1,9},{2,10},{3,11},{4,12},{5,13},{6,14},{7,15},{8,0},{9,1},... | collective-permute-start | bytes 1179656 | tf_op jit(solution)/shard_map/ppermute | solution.py:396
  86.2 53.4 %collective-permute-start.19 = (bf16[24,64,128]{2,1,0:T(8,128)(2,1)}, bf16[24,64,128]{2,1,0:T(8,128)(2,1)S(1)}, u32[]{:S(2)}, u32[]{:S(2)}) collective-permute-start(bf16[24,64,128]{2,1,0:T(8,128)(2,1)} %copy-done.16), channel_id=1, source_target_pairs={{0,12},{1,13},{2,14},{3,15},{4,8},{5,9},{6,10},{7,11},{8,4},{9,5},... | collective-permute-start | bytes 1179656 | tf_op jit(solution)/shard_map/ppermute | solution.py:396
  87.6 55.7 %collective-permute-start.6 = (bf16[16,64,128]{2,1,0:T(8,128)(2,1)}, bf16[16,64,128]{2,1,0:T(8,128)(2,1)S(1)}, u32[]{:S(2)}, u32[]{:S(2)}) collective-permute-start(bf16[16,64,128]{2,1,0:T(8,128)(2,1)} %copy-done.24), channel_id=1, source_target_pairs={{0,4},{1,5},{2,6},{3,7},{4,0},{5,1},{6,2},{7,3},{8,12},{9,13},{10,... | collective-permute-start | bytes 786440 | tf_op jit(solution)/shard_map/ppermute | solution.py:396
  88.4 55.0 %collective-permute-start.7 = (bf16[16,64,128]{2,1,0:T(8,128)(2,1)}, bf16[16,64,128]{2,1,0:T(8,128)(2,1)S(1)}, u32[]{:S(2)}, u32[]{:S(2)}) collective-permute-start(bf16[16,64,128]{2,1,0:T(8,128)(2,1)} %copy-done.23), channel_id=1, source_target_pairs={{0,8},{1,9},{2,10},{3,11},{4,12},{5,13},{6,14},{7,15},{8,0},{9,1},... | collective-permute-start | bytes 786440 | tf_op jit(solution)/shard_map/ppermute | solution.py:396
  103.2 40.9 %collective-permute-start.8 = (bf16[16,64,128]{2,1,0:T(8,128)(2,1)S(1)}, bf16[16,64,128]{2,1,0:T(8,128)(2,1)S(1)}, u32[]{:S(2)}, u32[]{:S(2)}) collective-permute-start(bf16[16,64,128]{2,1,0:T(8,128)(2,1)S(1)} %copy-done.22), channel_id=1, source_target_pairs={{0,12},{1,13},{2,14},{3,15},{4,8},{5,9},{6,10},{7,11},{8,4},{9,5},... | collective-permute-start | bytes 786440 | tf_op jit(solution)/shard_map/ppermute | solution.py:396
  153.9 21.5 %collective-permute-start.21 = (bf16[16,64,256]{2,1,0:T(8,128)(2,1)S(1)}, bf16[16,64,256]{2,1,0:T(8,128)(2,1)S(1)}, u32[]{:S(2)}, u32[]{:S(2)}) collective-permute-start(bf16[16,64,256]{2,1,0:T(8,128)(2,1)S(1)} %get-tuple-element.111), channel_id=1, source_target_pairs={{0,2},{1,3},{2,0},{3,1},{4,6},{5,7},{6,4},{7,5},{8,10},{9,11},{10,... | collective-permute-start | bytes 1572872 | tf_op jit(solution)/shard_map/ppermute | solution.py:396
  156.6 37.2 %collective-permute-start.28 = (bf16[32,64,256]{2,1,0:T(8,128)(2,1)S(1)}, bf16[32,64,256]{2,1,0:T(8,128)(2,1)S(1)}, u32[]{:S(2)}, u32[]{:S(2)}) collective-permute-start(bf16[32,64,256]{2,1,0:T(8,128)(2,1)S(1)} %copy-done.15), channel_id=1, source_target_pairs={{0,1},{1,0},{2,3},{3,2},{4,5},{5,4},{6,7},{7,6},{8,9},{9,8},{10,11... | collective-permute-start | bytes 3145736 | tf_op jit(solution)/shard_map/ppermute | solution.py:396
  156.6 31.1 %collective-permute-start.24 = (bf16[16,64,256]{2,1,0:T(8,128)(2,1)S(1)}, bf16[16,64,256]{2,1,0:T(8,128)(2,1)S(1)}, u32[]{:S(2)}, u32[]{:S(2)}) collective-permute-start(bf16[16,64,256]{2,1,0:T(8,128)(2,1)S(1)} %get-tuple-element.110), channel_id=1, source_target_pairs={{0,4},{1,5},{2,6},{3,7},{4,0},{5,1},{6,2},{7,3},{8,12},{9,13},{10,... | collective-permute-start | bytes 1572872 | tf_op jit(solution)/shard_map/ppermute | solution.py:396
  175.1 47.1 %collective-permute-start.27 = (bf16[32,64,256]{2,1,0:T(8,128)(2,1)S(1)}, bf16[32,64,256]{2,1,0:T(8,128)(2,1)S(1)}, u32[]{:S(2)}, u32[]{:S(2)}) collective-permute-start(bf16[32,64,256]{2,1,0:T(8,128)(2,1)S(1)} %copy-done.13), channel_id=1, source_target_pairs={{0,1},{1,0},{2,3},{3,2},{4,5},{5,4},{6,7},{7,6},{8,9},{9,8},{10,11... | collective-permute-start | bytes 3145736 | tf_op jit(solution)/shard_map/ppermute | solution.py:396
  194.2 28.1 %collective-permute-start.29 = (bf16[32,64,256]{2,1,0:T(8,128)(2,1)S(1)}, bf16[32,64,256]{2,1,0:T(8,128)(2,1)S(1)}, u32[]{:S(2)}, u32[]{:S(2)}) collective-permute-start(bf16[32,64,256]{2,1,0:T(8,128)(2,1)S(1)} %add_convert_fusion), channel_id=1, source_target_pairs={{0,2},{1,3},{2,0},{3,1},{4,6},{5,7},{6,4},{7,5},{8,10},{9,11},{10,... | collective-permute-start | bytes 3145736 | tf_op jit(solution)/shard_map/ppermute | solution.py:396
  203.0 18.4 %collective-permute-start.26 = (bf16[4,64,256]{2,1,0:T(8,128)(2,1)S(1)}, bf16[4,64,256]{2,1,0:T(8,128)(2,1)S(1)}, u32[]{:S(2)}, u32[]{:S(2)}) collective-permute-start(bf16[4,64,256]{2,1,0:T(8,128)(2,1)S(1)} %slice.116), channel_id=1, source_target_pairs={{0,2},{1,3},{2,0},{3,1},{4,6},{5,7},{6,4},{7,5},{8,10},{9,11},{10,... | collective-permute-start | bytes 393224 | tf_op jit(solution)/shard_map/ppermute | solution.py:396
  (32 other events, 231.7 us)
